TPU v7x, 128 devices: a whole 4x4x4 slice. The times are simulated.
128 devices in a mesh: seq: 8 (over y_lo, x), res: 16 (over y_hi, z, core).
Axes of the slice: x: 4, y: 4 (y_hi: 2, y_lo: 2; y = y_hi * 2 + y_lo), z: 4, core: 2. Of those that a mesh axis runs over, the one named last changes fastest.
Arguments:
- alignment_input: bfloat16 [128, 512, 768], P('seq', 'res'), may hold values from -6 to 6
- row_query_key_value: bfloat16 [768, 2304], replicated, as said below
- row_output_weight: bfloat16 [768, 768], replicated, may hold values from -0.21875 to 0.21875
- column_query_key_value: bfloat16 [768, 2304], replicated, as said below
- column_output_weight: bfloat16 [768, 768], replicated, may hold values from -0.21875 to 0.21875
- feedforward_input_weight: bfloat16 [768, 3072], replicated, may hold values from -0.21875 to 0.21875
- feedforward_output_weight: bfloat16 [3072, 768], replicated, may hold values from -0.109375 to 0.109375
Outputs:
- layer_out: bfloat16 [128, 512, 768], P('seq', 'res')
Inputs may be any that keep to these rules, and one draw needn't show every extreme that they name: `row_query_key_value`: a projection matrix. `column_query_key_value`: a projection matrix.
All inputs are finite; a program needn't handle non-finite values.
Results may differ from a plain program's by a relative error of at most 0.015.
Values may be sent and summed in bfloat16 or wider, within the bound.
No kernel may reach another device: no remote copies, remote signals or barrier semaphores. Data moves between devices by JAX's collectives and lax.ppermute only.
A program may use at most 128 MiB of HBM per device.

v0:
```python
import math

import jax
import jax.numpy as jnp
from jax import lax
from jax.sharding import PartitionSpec as P

H = 12
DH = 64


def normalize_rows(values_in):
    wide = values_in.astype(jnp.float32)
    centre = jnp.mean(wide, axis=-1, keepdims=True)
    variance = jnp.mean((wide - centre) ** 2, axis=-1, keepdims=True)
    return ((wide - centre) * lax.rsqrt(variance + 1e-05)).astype(jnp.bfloat16)


def split_heads(projected):
    rows_n, res_n, triple = projected.shape
    width = triple // 3
    return [
        projected[:, :, index * width : (index + 1) * width].reshape(rows_n, res_n, H, DH)
        for index in range(3)
    ]


def col_attend(queries, keys, values):
    col_scores = jnp.einsum(
        "rjhc,sjhc->jhrs", queries, keys, preferred_element_type=jnp.float32
    ) * (1.0 / math.sqrt(DH))
    col_weights = jax.nn.softmax(col_scores, axis=-1).astype(jnp.bfloat16)
    return jnp.einsum(
        "jhrs,sjhc->rjhc", col_weights, values, preferred_element_type=jnp.float32
    ).astype(jnp.bfloat16)


def per_device(
    alignment_input,
    row_query_key_value,
    row_output_weight,
    column_query_key_value,
    column_output_weight,
    feedforward_input_weight,
    feedforward_output_weight,
):
    rows_per_shard, residues_per_shard, hidden_width = alignment_input.shape
    seq_count = lax.axis_size("seq")
    total_rows = rows_per_shard * seq_count
    row_factor = 1.0 / math.sqrt(DH * total_rows)
    normalized_first = normalize_rows(alignment_input)
    row_proj = jnp.dot(
        normalized_first, row_query_key_value, preferred_element_type=jnp.float32
    ).astype(jnp.bfloat16)
    queries, keys, values = split_heads(row_proj)
    partial_scores = jnp.einsum(
        "rihc,rjhc->ihj",
        queries,
        lax.all_gather(keys, "res", axis=1, tiled=True),
        preferred_element_type=jnp.float32,
    )
    row_scores = (
        lax.psum(partial_scores.astype(jnp.bfloat16), "seq").astype(jnp.float32) * row_factor
    )
    attn_weights = jax.nn.softmax(row_scores, axis=-1).astype(jnp.bfloat16)
    summed = jnp.einsum(
        "ihj,rjhc->rihc",
        attn_weights,
        lax.all_gather(values, "res", axis=1, tiled=True),
        preferred_element_type=jnp.float32,
    )
    row_attention_output = summed.astype(jnp.bfloat16).reshape(
        rows_per_shard, residues_per_shard, hidden_width
    )
    state_after_rows = (
        alignment_input.astype(jnp.float32)
        + jnp.dot(row_attention_output, row_output_weight, preferred_element_type=jnp.float32)
    ).astype(jnp.bfloat16)
    normed_b = normalize_rows(state_after_rows)
    col_proj = jnp.dot(normed_b, column_query_key_value, preferred_element_type=jnp.float32).astype(
        jnp.bfloat16
    )
    col_queries, col_keys, col_values = split_heads(col_proj)
    all_keys, all_values = (
        lax.all_gather(col_keys, "seq", axis=0, tiled=True),
        lax.all_gather(col_values, "seq", axis=0, tiled=True),
    )
    column_out = col_attend(col_queries, all_keys, all_values)
    column_out = column_out.reshape(rows_per_shard, residues_per_shard, hidden_width)
    after_cols = (
        state_after_rows.astype(jnp.float32)
        + jnp.dot(column_out, column_output_weight, preferred_element_type=jnp.float32)
    ).astype(jnp.bfloat16)
    hidden = jax.nn.gelu(
        jnp.dot(
            normalize_rows(after_cols), feedforward_input_weight, preferred_element_type=jnp.float32
        )
    ).astype(jnp.bfloat16)
    return (
        after_cols.astype(jnp.float32)
        + jnp.dot(hidden, feedforward_output_weight, preferred_element_type=jnp.float32)
    ).astype(jnp.bfloat16)


def solution(mesh):
    placed = (P("seq", "res", None), P(), P(), P(), P(), P(), P())
    return jax.shard_map(
        per_device, mesh=mesh, in_specs=placed, out_specs=P("seq", "res", None), check_vma=False
    )
```

profile of v0, /device:TPU:0, one launch (start us, length us, event | category | flops | bytes accessed | tf_op | source)
XLA Modules:
  0.0 765.3 jit_solution(7666002053737685798)
XLA Ops:
  6.5 0.0 copy-start
  6.5 0.0 all-gather.7.cloned.1.call-start
  6.5 1.5 convert_reduce_fusion.2
  8.0 1.5 fusion.31
  9.5 0.0 copy-done
  9.5 3.2 convolution_convert_fusion.1
  12.7 1.4 fusion.83
  14.2 2.7 reshape.65
  16.9 1.6 copy.15
  18.6 0.0 all-gather.7.cloned.1.call-update
  18.6 0.0 all-reduce.2.cloned.1.call-start
  18.6 2.7 reshape.66
  21.4 161.1 %all-gather.7.cloned.1.call-done = bf16[16,512,12,64]{3,1,0,2:T(8,128)(2,1)} async-done(((bf16[16,32,12,64]{3,1,0,2:T(8,128)(2,1)}), bf16[16,512,12,64]{3,1,0,2:T(8,128)(2,1)}) %all-gather.7.cloned.1.call-update) | async-done | bytes 12582928 | tf_op jit(solution)/shard_map/all_gather | solution.py:59
  182.5 12.8 %fusion.56 = bf16[32,12,512]{2,0,1:T(8,128)(2,1)} fusion(bf16[16,512,12,64]{3,1,0,2:T(8,128)(2,1)} %all-gather.7.cloned.1.call-done, bf16[16,32,12,64]{3,2,1,0:T(8,128)(2,1)S(1)} %reshape.66), kind=kOutput, calls=%fused_computation.61 | convolution fusion | flops 402849792 | bytes 13762560 | tf_op jit(solution)/shard_map/rihc,rjhc->ihj/dot_general | solution.py:56
  195.3 0.0 all-reduce.2.cloned.1.call-update
  195.3 0.0 all-gather.5.cloned.1.call-start
  195.4 1.3 reshape.64
  196.7 1.6 copy.14
  198.3 0.0 all-gather.5.cloned.1.call-update
  198.3 0.2 all-gather.11.cloned.1.call-start
  198.6 68.3 %all-reduce.2.cloned.1.call-done = bf16[32,12,512]{2,0,1:T(8,128)(2,1)} async-done(((bf16[32,12,512]{2,0,1:T(8,128)(2,1)}), bf16[32,12,512]{2,0,1:T(8,128)(2,1)}) %all-reduce.2.cloned.1.call-update) | async-done | bytes 393232 | tf_op jit(solution)/shard_map/psum | solution.py:63
  266.9 1.3 fusion.84
  268.1 162.2 %all-gather.5.cloned.1.call-done = bf16[16,512,12,64]{3,1,0,2:T(8,128)(2,1)} async-done(((bf16[16,32,12,64]{3,1,0,2:T(8,128)(2,1)}), bf16[16,512,12,64]{3,1,0,2:T(8,128)(2,1)}) %all-gather.5.cloned.1.call-update) | async-done | bytes 12582928 | tf_op jit(solution)/shard_map/all_gather | solution.py:69
  430.3 12.6 %fusion.42 = bf16[16,32,12,64]{3,1,0,2:T(8,128)(2,1)S(1)} fusion(bf16[16,512,12,64]{3,1,0,2:T(8,128)(2,1)} %all-gather.5.cloned.1.call-done, f32[32,12,512]{2,0,1:T(8,128)S(1)} %get-tuple-element.12, f32[32,12]{0,1:T(8,128)S(1)} %get-tuple-element.11), kind=kOutput, calls=%fused_computation.55 | convolution fusion | flops 403439616 | bytes 14157312 | tf_op jit(solution)/shard_map/ihj,rjhc->rihc/dot_general | solution.py:66
  443.0 1.1 copy.17
  444.1 0.0 copy-start.2
  444.1 2.0 reshape.67
  446.1 0.0 copy-done.2
  446.1 0.0 copy-start.6
  446.1 2.5 convert_reduce_fusion.1
  448.6 0.0 copy-start.3
  448.7 0.3 fusion.29
  449.0 0.0 copy-done.6
  449.0 2.1 convolution_convert_fusion
  451.1 0.0 copy-done.3
  451.1 1.5 fusion.82
  452.6 2.7 reshape.70
  455.4 3.1 copy.19
  458.4 0.0 all-gather.11.cloned.1.call-update
  458.5 0.3 all-gather.9.cloned.1.call-start
  458.7 2.7 reshape.68
  461.5 3.0 copy.18
  464.4 0.0 all-gather.9.cloned.1.call-update
  464.5 2.2 reshape.69
  466.7 126.2 %all-gather.11.cloned.1.call-done = bf16[128,32,12,64]{3,0,2,1:T(8,128)(2,1)} async-done(((bf16[16,32,12,64]{3,0,2,1:T(8,128)(2,1)}), bf16[128,32,12,64]{3,0,2,1:T(8,128)(2,1)}) %all-gather.11.cloned.1.call-update) | async-done | bytes 6291472 | tf_op jit(solution)/shard_map/all_gather | solution.py:85
  592.9 9.8 %fusion.36 = f32[32,12,16,128]{3,2,1,0:T(8,128)S(1)} fusion(bf16[128,32,12,64]{3,0,2,1:T(8,128)(2,1)} %all-gather.11.cloned.1.call-done, bf16[16,32,12,64]{3,2,1,0:T(8,128)(2,1)} %reshape.69), kind=kOutput, calls=%fused_computation.49 | convolution fusion | flops 100663296 | bytes 10223616 | tf_op jit(solution)/shard_map/rjhc,sjhc->jhrs/dot_general | solution.py:29
  602.7 2.6 fusion.85
  605.4 127.8 %all-gather.9.cloned.1.call-done = bf16[128,32,12,64]{3,0,2,1:T(8,128)(2,1)} async-done(((bf16[16,32,12,64]{3,0,2,1:T(8,128)(2,1)}), bf16[128,32,12,64]{3,0,2,1:T(8,128)(2,1)}) %all-gather.9.cloned.1.call-update) | async-done | bytes 6291472 | tf_op jit(solution)/shard_map/all_gather | solution.py:86
  733.1 9.0 %fusion.43 = bf16[16,32,12,64]{3,0,2,1:T(8,128)(2,1)S(1)} fusion(bf16[128,32,12,64]{3,0,2,1:T(8,128)(2,1)} %all-gather.9.cloned.1.call-done, f32[32,12,16,128]{3,2,1,0:T(8,128)} %get-tuple-element.16, f32[32,12,16]{2,1,0:T(8,128)S(1)} %get-tuple-element.15), kind=kOutput, calls=%fused_computation.56 | convolution fusion | flops 102629376 | bytes 10248192 | tf_op jit(solution)/shard_map/jhrs,sjhc->rjhc/dot_general | solution.py:33
  742.1 0.5 copy.21
  742.6 0.0 copy-start.4
  742.6 2.0 reshape.71
  744.7 0.0 copy-done.4
  744.7 2.4 convert_reduce_fusion
  747.0 0.0 copy-start.5
  747.1 0.9 copy-done.5
  747.9 0.3 fusion.27
  748.3 0.0 copy-start.1
  748.3 10.5 %fusion.35 = bf16[16,32,768]{2,1,0:T(8,128)(2,1)} fusion(bf16[16,32,768]{2,1,0:T(8,128)(2,1)} %copy-done.5, bf16[3072,768]{1,0:T(8,128)(2,1)} %param.13, bf16[768,3072]{1,0:T(8,128)(2,1)} %param.12, f32[16,32]{1,0:T(8,128)S(1)} %add_rsqrt_fusion, f32[16,32]{1,0:T(8,128)S(1)} %broadcast_multiply_fusion), kind=kOutput, calls=%fused_computation.48 | convolution fusion | flops 4848746496 | bytes 11014144 | tf_op jit(solution)/shard_map/dot_general | solution.py:101
  758.8 0.0 copy-done.1
  (6 shorter events, 0.0 us)
Async XLA Ops:
  6.5 3.0 copy-start
  6.5 176.0 %all-gather.7.cloned.1.call-start = ((), (), s32[]{:S(2)}) async-start(), calls=%async_computation.1 | async-start | bytes 26738688 | tf_op jit(solution)/shard_map/all_gather | solution.py:59
  18.6 248.3 %all-reduce.2.cloned.1.call-start = ((), (), s32[]{:S(2)}) async-start(), calls=%async_computation.2 | async-start | bytes 786432 | tf_op jit(solution)/shard_map/psum | solution.py:63
  195.3 235.0 %all-gather.5.cloned.1.call-start = ((), (), s32[]{:S(2)}) async-start(), calls=%async_computation | async-start | bytes 26738688 | tf_op jit(solution)/shard_map/all_gather | solution.py:69
  198.3 394.6 %all-gather.11.cloned.1.call-start = ((), (), s32[]{:S(2)}) async-start(), calls=%async_computation.4 | async-start | bytes 14155776 | tf_op jit(solution)/shard_map/all_gather | solution.py:85
  444.1 2.0 copy-start.2
  446.1 2.9 copy-start.6
  448.6 2.5 copy-start.3
  458.5 274.6 %all-gather.9.cloned.1.call-start = ((), (), s32[]{:S(2)}) async-start(), calls=%async_computation.3 | async-start | bytes 14155776 | tf_op jit(solution)/shard_map/all_gather | solution.py:86
  742.6 2.0 copy-start.4
  747.0 0.9 copy-start.5
  748.3 10.5 %copy-start.1 = (bf16[768,2304]{1,0:T(8,128)(2,1)S(1)}, bf16[768,2304]{1,0:T(8,128)(2,1)}, u32[]{:S(2)}) copy-start(bf16[768,2304]{1,0:T(8,128)(2,1)} %param.8) | copy-start | bytes 10616836
Sparse Core Ops, SparseCore 0:
  18.7 163.7 all-gather.6
  195.5 71.3 all-reduce.1
  269.4 160.8 all-gather.4
  458.6 134.3 all-gather.10
  594.4 138.6 all-gather.8
where the time goes:
time: 766 us; the launch traced here: 765 us
  waiting for transfers between devices  646 us (84%)
  matrix products  64.9 us (8%)
  local copies, waits for them, and re-layouts  33.3 us (4%)
  between operations  13.4 us (2%)
    all_gather x1, waiting for transfers between devices, per_device(): lax.all_gather(values, 'res', axis=1, tiled=True)  162 us
    all_gather x1, waiting for transfers between devices, per_device(): lax.all_gather(keys, 'res', axis=1, tiled=True)  161 us
    all_gather x1, waiting for transfers between devices, per_device(): lax.all_gather(col_values, 'seq', axis=0, tiled=True)  128 us
    all_gather x1, waiting for transfers between devices, per_device(): lax.all_gather(col_keys, 'seq', axis=0, tiled=True)  126 us
    psum x1, waiting for transfers between devices, per_device(): lax.psum(partial_scores.astype(jnp.bfloat16), 'seq').astype(jnp.float32)  68.3 us
    reshape x10, local copies, waits for them, and re-layouts, split_heads(): projected[:, :, index * width:(index + 1) * width]  23.8 us
  transfers between devices with their start and end apart: 5, of which 5 were waited for; matrix products, arithmetic and copies ran while one was open for 4% of the time, Pallas kernels for 0%

commit v1 on v0

v1 whole, which is shorter than its diff:
```python
import math

import jax
import jax.numpy as jnp
from jax import lax
from jax.sharding import Mesh, PartitionSpec as P

H = 12
DH = 64
D = H * DH
GROUPS = 4
HG = H // GROUPS
ROWS = 128
PLANE = ("y_lo", "x", "y_hi")
SEQ = ("y_lo", "x")


def normalize_rows(values_in):
    wide = values_in.astype(jnp.float32)
    centre = jnp.mean(wide, axis=-1, keepdims=True)
    variance = jnp.mean((wide - centre) ** 2, axis=-1, keepdims=True)
    return ((wide - centre) * lax.rsqrt(variance + 1e-05)).astype(jnp.bfloat16)


def dot32(a, b):
    return jnp.dot(a, b, preferred_element_type=jnp.float32)


def per_device(x, row_qkv, row_out, col_qkv, col_out, ff_in, ff_out):
    normed = normalize_rows(x).reshape(2, 256, D)
    by_group = row_qkv.reshape(D, 3, GROUPS, HG * DH).transpose(2, 0, 1, 3).reshape(GROUPS, D, 576)
    proj = jnp.einsum("ytd,zde->yzte", normed, by_group, preferred_element_type=jnp.float32)
    proj = proj.astype(jnp.bfloat16).reshape(8, 256, 576)
    x_cols = x.reshape(16, 8, 4, D).transpose(1, 2, 0, 3)
    x_cols = lax.all_to_all(x_cols, SEQ, 0, 0, tiled=True)
    got = lax.all_to_all(proj, ("y_hi", "z"), 0, 0, tiled=True)
    got = got.reshape(8, 8, 32, 3, HG, DH)
    q, k, v = got[:, :, :, 0], got[:, :, :, 1], got[:, :, :, 2]
    swap = [(0, 1), (1, 0)]
    k2 = lax.ppermute(k, "core", swap)
    v2 = lax.ppermute(v, "core", swap)
    k_all = jnp.stack([k, k2])
    v_all = jnp.stack([v, v2])
    scores = jnp.einsum("arihc,kbrjhc->haikbj", q, k_all, preferred_element_type=jnp.float32)
    scores = scores.reshape(HG, 16, 16, 512).transpose(1, 0, 2, 3).astype(jnp.bfloat16)
    parts = lax.all_to_all(scores, PLANE, 0, 0, tiled=True)
    total = jnp.sum(parts.astype(jnp.float32), axis=0) * (1.0 / math.sqrt(DH * ROWS))
    weights = jax.nn.softmax(total, axis=-1).astype(jnp.bfloat16)
    weights = lax.all_gather(weights, PLANE, axis=0, tiled=False)
    weights = weights.transpose(1, 0, 2, 3).reshape(HG, 8, 32, 2, 8, 32)
    att = jnp.einsum("haikbj,kbrjhc->airhc", weights, v_all, preferred_element_type=jnp.float32)
    att = att.astype(jnp.bfloat16).reshape(8, 8, 4, 8, HG * DH)
    att = att.transpose(1, 0, 2, 3, 4).reshape(64, 4, 8, HG * DH)
    att = lax.all_to_all(att, ("y_lo", "x", "y_hi", "z"), 0, 0, tiled=True)
    att = att.reshape(16, GROUPS, 4, 8, HG * DH).transpose(2, 0, 3, 1, 4).reshape(512, D)
    x_cols = x_cols.transpose(1, 0, 2, 3).reshape(512, D)
    after_rows = (x_cols.astype(jnp.float32) + dot32(att, row_out)).astype(jnp.bfloat16)
    col = dot32(normalize_rows(after_rows), col_qkv).astype(jnp.bfloat16)
    col = col.reshape(4, ROWS, 3, H, DH)
    cq, ck, cv = col[:, :, 0], col[:, :, 1], col[:, :, 2]
    cs = jnp.einsum("jrhc,jshc->jhrs", cq, ck, preferred_element_type=jnp.float32)
    cw = jax.nn.softmax(cs * (1.0 / math.sqrt(DH)), axis=-1).astype(jnp.bfloat16)
    co = jnp.einsum("jhrs,jshc->jrhc", cw, cv, preferred_element_type=jnp.float32)
    co = co.astype(jnp.bfloat16).reshape(512, D)
    after_cols = (after_rows.astype(jnp.float32) + dot32(co, col_out)).astype(jnp.bfloat16)
    hidden = jax.nn.gelu(dot32(normalize_rows(after_cols), ff_in)).astype(jnp.bfloat16)
    out = (after_cols.astype(jnp.float32) + dot32(hidden, ff_out)).astype(jnp.bfloat16)
    out = out.reshape(4, 8, 16, D).transpose(1, 0, 2, 3)
    out = lax.all_to_all(out, SEQ, 0, 0, tiled=True)
    return out.transpose(2, 0, 1, 3).reshape(16, 32, D)


def solution(mesh):
    fine = Mesh(mesh.devices.reshape(2, 4, 2, 4, 2), ("y_lo", "x", "y_hi", "z", "core"))
    tokens = P(SEQ, ("y_hi", "z", "core"), None)
    placed = (tokens, P(), P(), P(), P(), P(), P())
    return jax.shard_map(per_device, mesh=fine, in_specs=placed, out_specs=tokens, check_vma=False)
```

time: 766 us -> 265 us (0.35)
  waiting for transfers between devices: 646 us -> 24.2 us
  blocking collectives: 0 us -> 99.6 us
  local copies, waits for them, and re-layouts: 33.3 us -> 83 us
  matrix products: 64.9 us -> 29.6 us
  starting transfers between devices: 0.57 us -> 14.9 us
  between operations: 13.4 us -> 0.24 us
    all_gather x4 -> x0, waiting for transfers between devices: 577 us -> none  [the longest x1 162 us: per_device(): lax.all_gather(values, 'res', axis=1, tiled=True)]
    psum x1 -> x0, waiting for transfers between devices: 68.3 us -> none  [per_device(): lax.psum(partial_scores.astype(jnp.bfloat16), 'seq').astype(jnp.float32)]
    all_to_all x0 -> x2, blocking collectives: none -> 51.9 us  [the longest x1 39.1 us: per_device(): got = lax.all_to_all(proj, ('y_hi', 'z'), 0, 0, tiled=True)]
    all_gather x0 -> x1, blocking collectives: none -> 47.7 us  [per_device(): weights = lax.all_gather(weights, PLANE, axis=0, tiled=False)]
    dot_general x9, matrix products: 64.9 us -> 29.6 us  [the longest x4 17.3 us: dot32(): return jnp.dot(a, b, preferred_element_type=jnp.float32)]
    all_to_all x0 -> x3, waiting for transfers between devices: none -> 20.8 us  [the longest x1 11.1 us: per_device(): att = lax.all_to_all(att, ('y_lo', 'x', 'y_hi', 'z'), 0, 0, tiled=True)]
    convert_element_type x2 -> x7, local copies, waits for them, and re-layouts: 1.63 us -> 19.4 us  [the longest x3 10.5 us: per_device(): scores.reshape(HG, 16, 16, 512).transpose(1, 0, 2, 3).astype(jnp.bfloat16)]
    all_to_all x0 -> x3, starting transfers between devices: none -> 14.8 us  [the longest x1 5.74 us: per_device(): att = lax.all_to_all(att, ('y_lo', 'x', 'y_hi', 'z'), 0, 0, tiled=True)]
  transfers between devices with their start and end apart: 5 -> 5, of which waited for: 5 -> 3; matrix products, arithmetic and copies ran while one was open for 4% -> 11% of each run, Pallas kernels for 0% -> 0%
where the time goes in v1:
time: 265 us; the launch traced here: 264 us
  blocking collectives  99.6 us (38%)
  local copies, waits for them, and re-layouts  83 us (31%)
  matrix products  29.6 us (11%)
  waiting for transfers between devices  24.2 us (9%)
  starting transfers between devices  14.9 us (6%)
  other arithmetic  12.2 us (5%)
    all_gather x1, blocking collectives, per_device(): weights = lax.all_gather(weights, PLANE, axis=0, tiled=False)  47.7 us
    all_to_all x1, blocking collectives, per_device(): got = lax.all_to_all(proj, ('y_hi', 'z'), 0, 0, tiled=True)  39.1 us
    dot_general x4, matrix products, dot32(): return jnp.dot(a, b, preferred_element_type=jnp.float32)  17.3 us
    all_to_all x1, blocking collectives, per_device(): out = lax.all_to_all(out, SEQ, 0, 0, tiled=True)  12.8 us
    unnamed x16, local copies, waits for them, and re-layouts  12.5 us
    reshape x1, local copies, waits for them, and re-layouts, per_device(): got = got.reshape(8, 8, 32, 3, HG, DH)  12.2 us
    all_to_all x1, waiting for transfers between devices, per_device(): att = lax.all_to_all(att, ('y_lo', 'x', 'y_hi', 'z'), 0, 0, tiled=True)  11.1 us
    convert_element_type x3, local copies, waits for them, and re-layouts, per_device(): scores.reshape(HG, 16, 16, 512).transpose(1, 0, 2, 3).astype(jnp.bfloat16)  10.5 us
  transfers between devices with their start and end apart: 5, of which 3 were waited for; matrix products, arithmetic and copies ran while one was open for 11% of the time, Pallas kernels for 0%

profile of v1, /device:TPU:0, one launch (start us, length us, event | category | flops | bytes accessed | tf_op | source)
XLA Modules:
  0.0 263.7 jit_solution(1053063868192196215)
XLA Ops:
  0.0 0.0 copy-start
  0.0 1.5 convert_reduce_fusion.2
  1.5 1.5 fusion.33
  3.0 2.3 fusion.34
  5.2 5.7 %copy.60 = bf16[768,2304]{0,1:T(8,128)(2,1)} copy(bf16[768,2304]{1,0:T(8,128)(2,1)} %param.8) | data formatting | bytes 7077888 | tf_op args[1]
  11.0 2.3 copy.61
  13.3 0.0 copy-done.4
  13.3 2.1 convolution_convert_fusion.1
  15.4 39.1 %all_to_all.25 = bf16[8,256,576]{1,2,0:T(8,128)(2,1)} all-to-all(bf16[8,256,576]{1,2,0:T(8,128)(2,1)S(1)} %bitcast.142), channel_id=1, replica_groups=mesh['y_lo'=2,'x'=4,'y_hi'=2,'z'=4,'core'=2] {'y_hi','z'}, dimensions={0} | all-to-all | bytes 4718592 | tf_op jit(solution)/shard_map/all_to_all | solution.py:36
  54.6 4.4 %copy.62 = bf16[8,256,576]{2,1,0:T(8,128)(2,1)} copy(bf16[8,256,576]{1,2,0:T(8,128)(2,1)} %all_to_all.25) | data formatting | bytes 4718592 | tf_op jit(solution)/shard_map/all_to_all | solution.py:36
  59.0 12.2 %reshape.116 = bf16[8,8,32,3,3,64]{5,4,3,2,1,0:T(4,128)(2,1)} reshape(bf16[8,256,576]{2,1,0:T(8,128)(2,1)} %copy.62) | data formatting | bytes 4718592 | tf_op jit(solution)/shard_map/reshape | solution.py:37
  71.1 6.4 %fusion.73 = (bf16[8,8,32,1,3,64]{5,4,3,2,1,0:T(4,128)(2,1)}, bf16[8,8,32,1,3,64]{5,4,3,2,1,0:T(4,128)(2,1)S(1)}, bf16[8,8,32,1,3,64]{5,4,3,2,1,0:T(4,128)(2,1)S(1)}) fusion(bf16[8,8,32,3,3,64]{5,4,3,2,1,0:T(4,128)(2,1)} %reshape.116), kind=kLoop, calls=%fused_computation.96 | loop fusion | bytes 4718592 | tf_op jit(solution)/shard_map/slice | solution.py:38
  77.5 0.4 copy.125
  77.9 0.1 collective-permute-start.1
  78.0 3.4 %collective-permute-done.1 = bf16[8,8,32,3,64]{4,2,1,0,3:T(8,128)(2,1)S(1)} collective-permute-done((bf16[8,8,32,3,64]{4,2,1,0,3:T(8,128)(2,1)S(1)}, bf16[8,8,32,3,64]{4,2,1,0,3:T(8,128)(2,1)S(1)}, u32[]{:S(2)}, u32[]{:S(2)}) %collective-permute-start.1) | collective-permute-done | bytes 786464 | tf_op jit(solution)/shard_map/ppermute | solution.py:40
  81.4 3.7 %bitcast_convert_fusion = bf16[3,8,32,2,8,32]{5,2,4,3,1,0:T(8,128)(2,1)S(1)} fusion(bf16[1,8,8,32,3,64]{5,3,2,1,0,4:T(8,128)(2,1)S(1)} %bitcast.148, bf16[1,8,8,32,3,64]{5,3,2,1,0,4:T(8,128)(2,1)S(1)} %bitcast.144, bf16[8,8,32,1,3,64]{5,4,3,2,1,0:T(4,128)(2,1)S(1)} %get-tuple-element.7), kind=kOutput, calls=%fused_computation.10 | convolution fusion | flops 406192128 | bytes 3145728 | tf_op jit(solution)/shard_map/arihc,kbrjhc->haikbj/dot_general | solution.py:44
  85.1 3.1 %copy.68 = bf16[3,8,32,2,8,32]{5,4,3,2,1,0:T(8,128)(2,1)} copy(bf16[3,8,32,2,8,32]{5,2,4,3,1,0:T(8,128)(2,1)S(1)} %bitcast_convert_fusion) | data formatting | bytes 1572864 | tf_op jit(solution)/shard_map/convert_element_type | solution.py:45
  88.2 5.3 %convert_element_type.95 = bf16[3,16,16,512]{3,2,1,0:T(8,128)(2,1)} reshape(bf16[3,8,32,2,8,32]{5,4,3,2,1,0:T(8,128)(2,1)} %copy.68) | data formatting | bytes 1572864 | tf_op jit(solution)/shard_map/convert_element_type | solution.py:45
  93.5 2.1 copy.69
  95.6 4.9 %all-to-all-start.2 = ((bf16[16,3,16,512]{3,2,1,0:T(8,128)(2,1)}), bf16[16,3,16,512]{3,2,1,0:T(8,128)(2,1)}, u32[]{:S(2)}, u32[]{:S(2)}) async-start(bf16[16,3,16,512]{3,2,1,0:T(8,128)(2,1)} %copy.69), calls=%async_computation.2 | async-start | bytes 1572864 | tf_op jit(solution)/shard_map/all_to_all | solution.py:46
  100.5 2.5 copy.58
  102.9 3.1 %copy.126 = bf16[8,8,32,1,3,64]{5,2,0,1,4,3:T(8,128)(2,1)} copy(bf16[8,8,32,1,3,64]{5,4,3,2,1,0:T(4,128)(2,1)} %get-tuple-element.5) | data formatting | bytes 1572864
  106.0 0.0 collective-permute-start
  106.0 9.7 %all-to-all-done.2 = bf16[16,3,16,512]{3,2,1,0:T(8,128)(2,1)} async-done(((bf16[16,3,16,512]{3,2,1,0:T(8,128)(2,1)}), bf16[16,3,16,512]{3,2,1,0:T(8,128)(2,1)}, u32[]{:S(2)}, u32[]{:S(2)}) %all-to-all-start.2) | async-done | bytes 786464 | tf_op jit(solution)/shard_map/all_to_all | solution.py:46
  115.8 4.2 %all-to-all-start = ((bf16[8,4,16,768]{3,2,1,0:T(8,128)(2,1)}), bf16[8,4,16,768]{3,2,1,0:T(8,128)(2,1)}, u32[]{:S(2)}, u32[]{:S(2)}) async-start(bf16[8,4,16,768]{3,2,1,0:T(8,128)(2,1)} %bitcast.136), calls=%async_computation | async-start | bytes 1572864 | tf_op jit(solution)/shard_map/all_to_all | solution.py:35
  120.0 1.3 convert_reduce_fusion.3
  121.2 0.1 multiply_reduce_fusion.1
  121.3 0.2 exponential_reduce_fusion
  121.5 0.1 fusion.65
  121.6 47.7 %all_gather.4 = bf16[16,3,16,512]{3,2,0,1:T(8,128)(2,1)} all-gather(bf16[1,3,16,512]{3,2,0,1:T(8,128)(2,1)S(1)} %fusion.65), channel_id=1, replica_groups=mesh['y_lo'=2,'x'=4,'y_hi'=2,'z'=4,'core'=2] {'y_lo','x','y_hi'}, dimensions={0}, use_global_device_ids=true | all-gather | bytes 835584 | tf_op jit(solution)/shard_map/all_gather | solution.py:49
  169.3 4.6 %reshape.117 = bf16[3,8,32,2,8,32]{5,4,3,2,1,0:T(8,128)(2,1)} reshape(bf16[3,16,16,512]{3,2,1,0:T(8,128)(2,1)} %bitcast.141) | data formatting | bytes 1572864 | tf_op jit(solution)/shard_map/reshape | solution.py:50
  173.9 0.0 collective-permute-done
  173.9 5.3 %fusion.40 = bf16[8,32,8,3,64]{4,1,0,2,3:T(8,128)(2,1)S(1)} fusion(bf16[3,8,32,2,8,32,1]{5,4,3,2,1,0,6:T(8,128)(2,1)} %bitcast.139, bf16[1,8,8,32,3,64]{5,3,0,1,2,4:T(8,128)(2,1)} %bitcast.16, bf16[1,8,8,32,3,64]{5,3,0,1,2,4:T(8,128)(2,1)} %bitcast.128), kind=kOutput, calls=%fused_computation.57 | convolution fusion | flops 406192128 | bytes 3145728 | tf_op jit(solution)/shard_map/haikbj,kbrjhc->airhc/dot_general | solution.py:51
  179.2 2.7 %copy.71 = bf16[8,32,8,3,64]{4,3,2,1,0:T(4,128)(2,1)} copy(bf16[8,32,8,3,64]{4,1,0,2,3:T(8,128)(2,1)S(1)} %fusion.40) | data formatting | bytes 1572864 | tf_op jit(solution)/shard_map/convert_element_type | solution.py:52
  181.9 4.9 %reshape.118 = bf16[8,8,4,8,192]{4,3,2,1,0:T(8,128)(2,1)} reshape(bf16[8,32,8,3,64]{4,3,2,1,0:T(4,128)(2,1)} %copy.71) | data formatting | bytes 1572864 | tf_op jit(solution)/shard_map/reshape | solution.py:52
  186.8 2.3 copy.72
  189.1 0.0 all-to-all-done
  189.1 5.7 %all-to-all-start.3 = ((bf16[64,4,8,192]{3,2,1,0:T(8,128)(2,1)}), bf16[64,4,8,192]{3,2,1,0:T(8,128)(2,1)}, u32[]{:S(2)}, u32[]{:S(2)}) async-start(bf16[64,4,8,192]{3,2,1,0:T(8,128)(2,1)} %bitcast.134), calls=%async_computation.3 | async-start | bytes 2097152 | tf_op jit(solution)/shard_map/all_to_all | solution.py:54
  194.9 1.3 convert_bitcast_fusion
  196.2 1.3 copy.59
  197.5 11.1 %all-to-all-done.3 = bf16[64,4,8,192]{3,2,1,0:T(8,128)(2,1)} async-done(((bf16[64,4,8,192]{3,2,1,0:T(8,128)(2,1)}), bf16[64,4,8,192]{3,2,1,0:T(8,128)(2,1)}, u32[]{:S(2)}, u32[]{:S(2)}) %all-to-all-start.3) | async-done | bytes 786464 | tf_op jit(solution)/shard_map/all_to_all | solution.py:54
  208.5 3.6 %copy.127 = bf16[16,4,4,8,192]{4,1,3,0,2:T(4,128)(2,1)} copy(bf16[16,4,4,8,192]{4,3,2,1,0:T(8,128)(2,1)} %bitcast.39) | data formatting | bytes 1572864 | tf_op jit(solution)/shard_map/reshape | solution.py:55
  212.1 3.0 %reshape.121 = bf16[512,768]{1,0:T(8,128)(2,1)} reshape(bf16[4,16,8,4,192]{4,3,2,1,0:T(4,128)(2,1)} %bitcast.133) | data formatting | bytes 1572864 | tf_op jit(solution)/shard_map/reshape | solution.py:55
  215.1 2.9 %convert_reduce_fusion.1 = (f32[512]{0:T(512)S(1)}, bf16[512,768]{1,0:T(8,128)(2,1)S(1)}) fusion(bf16[512,768]{1,0:T(8,128)(2,1)} %reshape.121, bf16[768,768]{1,0:T(8,128)(2,1)} %param.9, f32[4,8,16,768]{3,2,1,0:T(8,128)} %copy.59), kind=kOutput, calls=%fused_computation.32 | convolution fusion | flops 605552128 | bytes 4327424 | tf_op jit(solution)/shard_map/dot_general | solution.py:26
  218.0 0.4 fusion.31
  218.3 0.5 copy-done.2
  218.8 0.0 copy-done
  218.8 3.5 %convolution_convert_fusion = bf16[512,2304]{1,0:T(8,128)(2,1)} fusion(bf16[768,2304]{1,0:T(8,128)(2,1)S(1)} %copy-done, bf16[512,768]{1,0:T(8,128)(2,1)S(1)} %get-tuple-element.16, f32[512]{0:T(512)S(1)} %add_rsqrt_fusion.2, f32[512]{0:T(512)S(1)} %broadcast_multiply_fusion.2), kind=kOutput, calls=%fused_computation.11 | convolution fusion | flops 1814691840 | bytes 6688768 | tf_op jit(solution)/shard_map/dot_general | solution.py:26
  222.3 4.3 %copy.74 = bf16[512,2304]{0,1:T(8,128)(2,1)} copy(bf16[512,2304]{1,0:T(8,128)(2,1)} %convolution_convert_fusion) | data formatting | bytes 4718592 | tf_op jit(solution)/shard_map/convert_element_type | solution.py:58
  226.6 4.2 %reshape.122 = bf16[4,128,3,12,64]{1,0,4,3,2:T(4,128)(2,1)S(1)} reshape(bf16[512,2304]{0,1:T(8,128)(2,1)} %copy.74) | data formatting | bytes 4718592 | tf_op jit(solution)/shard_map/reshape | solution.py:59
  230.8 0.9 fusion.74
  231.7 0.6 fusion.56
  232.3 3.3 %fusion.75 = (f32[4,12,128]{2,1,0:T(8,128)S(1)}, f32[4,12,128,128]{2,3,1,0:T(8,128)S(1)}) fusion(f32[4,12,128,128]{2,3,1,0:T(8,128)S(1)} %fusion.56), kind=kOutput, calls=%fused_computation.98 | output fusion | flops 3145855 | bytes 6316032 | tf_op jit(solution)/shard_map/sub | solution.py:62
  235.6 0.0 copy-start.3
  235.6 0.0 copy-start.5
  235.6 0.5 fusion.46
  236.2 0.6 copy.79
  236.8 0.3 copy-done.5
  237.1 0.9 convert_reduce_fusion
  238.1 0.4 fusion.29
  238.4 10.0 %fusion.36 = bf16[512,768]{1,0:T(8,128)(2,1)} fusion(bf16[512,768]{1,0:T(8,128)(2,1)S(1)} %get-tuple-element.20, bf16[3072,768]{1,0:T(8,128)(2,1)} %param.13, bf16[768,3072]{1,0:T(8,128)(2,1)} %param.12, f32[512]{0:T(512)S(1)} %add_rsqrt_fusion.1, f32[512]{0:T(512)S(1)} %broadcast_multiply_fusion.1), kind=kOutput, calls=%fused_computation.49 | convolution fusion | flops 4848746496 | bytes 11014144 | tf_op jit(solution)/shard_map/dot_general | solution.py:26
  248.4 1.3 copy.128
  249.8 12.8 %all_to_all.26 = bf16[8,4,16,768]{3,2,1,0:T(8,128)(2,1)S(1)} all-to-all(bf16[8,4,16,768]{3,2,1,0:T(8,128)(2,1)S(1)} %bitcast.137), channel_id=1, replica_groups=mesh['y_lo'=2,'x'=4,'y_hi'=2,'z'=4,'core'=2] {'y_lo','x'}, dimensions={0} | all-to-all | bytes 1572864 | tf_op jit(solution)/shard_map/all_to_all | solution.py:69
  262.6 1.1 copy.81
  (11 shorter events, 0.0 us)
Async XLA Ops:
  0.0 218.8 %copy-start = (bf16[768,2304]{1,0:T(8,128)(2,1)S(1)}, bf16[768,2304]{1,0:T(8,128)(2,1)}, u32[]{:S(2)}) copy-start(bf16[768,2304]{1,0:T(8,128)(2,1)} %param.10) | copy-start | bytes 10616836
  11.0 2.3 copy-start.4
  77.9 3.5 %collective-permute-start.1 = (bf16[8,8,32,3,64]{4,2,1,0,3:T(8,128)(2,1)S(1)}, bf16[8,8,32,3,64]{4,2,1,0,3:T(8,128)(2,1)S(1)}, u32[]{:S(2)}, u32[]{:S(2)}) collective-permute-start(bf16[8,8,32,3,64]{4,2,1,0,3:T(8,128)(2,1)S(1)} %bitcast.143), channel_id=1, source_target_pairs={{0,1},{1,0},{2,3},{3,2},{4,5},{5,4},{6,7},{7,6},{8,9},{9,8},{10,11... | collective-permute-start | bytes 2359304 | tf_op jit(solution)/shard_map/ppermute | solution.py:40
  95.6 20.2 %all-to-all-start.2 = ((bf16[16,3,16,512]{3,2,1,0:T(8,128)(2,1)}), bf16[16,3,16,512]{3,2,1,0:T(8,128)(2,1)}, u32[]{:S(2)}, u32[]{:S(2)}) async-start(bf16[16,3,16,512]{3,2,1,0:T(8,128)(2,1)} %copy.69), calls=%async_computation.2 | async-start | bytes 1572864 | tf_op jit(solution)/shard_map/all_to_all | solution.py:46
  106.0 67.8 %collective-permute-start = (bf16[8,8,32,3,64]{4,2,0,1,3:T(8,128)(2,1)}, bf16[8,8,32,3,64]{4,2,0,1,3:T(8,128)(2,1)}, u32[]{:S(2)}, u32[]{:S(2)}) collective-permute-start(bf16[8,8,32,3,64]{4,2,0,1,3:T(8,128)(2,1)} %bitcast.95.clone.2), channel_id=1, source_target_pairs={{0,1},{1,0},{2,3},{3,2},{4,5},{5,4},{6,7},{7,6},{8,9},{9,8},{10,11... | collective-permute-start | bytes 2359304 | tf_op jit(solution)/shard_map/ppermute | solution.py:41
  115.8 73.4 %all-to-all-start = ((bf16[8,4,16,768]{3,2,1,0:T(8,128)(2,1)}), bf16[8,4,16,768]{3,2,1,0:T(8,128)(2,1)}, u32[]{:S(2)}, u32[]{:S(2)}) async-start(bf16[8,4,16,768]{3,2,1,0:T(8,128)(2,1)} %bitcast.136), calls=%async_computation | async-start | bytes 1572864 | tf_op jit(solution)/shard_map/all_to_all | solution.py:35
  189.1 19.4 %all-to-all-start.3 = ((bf16[64,4,8,192]{3,2,1,0:T(8,128)(2,1)}), bf16[64,4,8,192]{3,2,1,0:T(8,128)(2,1)}, u32[]{:S(2)}, u32[]{:S(2)}) async-start(bf16[64,4,8,192]{3,2,1,0:T(8,128)(2,1)} %bitcast.134), calls=%async_computation.3 | async-start | bytes 2097152 | tf_op jit(solution)/shard_map/all_to_all | solution.py:54
  217.9 0.9 copy-start.2
  235.6 1.2 copy-start.3
  235.6 1.5 copy-start.5
  248.4 15.3 %copy-start.1 = (bf16[768,2304]{1,0:T(8,128)(2,1)S(1)}, bf16[768,2304]{1,0:T(8,128)(2,1)}, u32[]{:S(2)}) copy-start(bf16[768,2304]{1,0:T(8,128)(2,1)} %param.10) | copy-start | bytes 10616836

commit v2 on v1

v2 whole, which is shorter than its diff:
```python
import functools
import math

import jax
import jax.numpy as jnp
from jax import lax
from jax.experimental import pallas as pl
from jax.experimental.pallas import tpu as pltpu
from jax.sharding import Mesh, PartitionSpec as P

H = 12
DH = 64
D = H * DH
FF = 4 * D
ROWS = 128
SEQ = ("y_lo", "x")
PLANE = ("y_lo", "x", "y_hi")
CHIPS = ("y_lo", "x", "y_hi", "z")
BF = jnp.bfloat16
F32 = jnp.float32
MIB = 1 << 20

FULL = (0, 2, 3, 5)
HALF = (1, 1, 4, 4)


def dot32(a, b):
    return jnp.dot(a, b, preferred_element_type=F32)


def dot_t(a, b):
    return lax.dot_general(a, b, (((1,), (1,)), ((), ())), preferred_element_type=F32)


def swap_halves(v):
    return pltpu.roll(v, 64, 1)


def low_lanes(shape):
    return lax.broadcasted_iota(jnp.int32, shape, len(shape) - 1) % 128 < 64


def normalize(wide):
    centre = jnp.mean(wide, axis=-1, keepdims=True)
    off = wide - centre
    variance = jnp.mean(off * off, axis=-1, keepdims=True)
    return (off * lax.rsqrt(variance + 1e-05)).astype(BF)


def params(mib, **kw):
    return pltpu.CompilerParams(vmem_limit_bytes=mib * MIB, **kw)


def project_kernel(x_ref, w_ref, out_ref, normed):
    @pl.when(pl.program_id(0) == 0)
    def _():
        normed[...] = normalize(x_ref[...].astype(F32))

    val = dot32(normed[...], w_ref[...])
    low = low_lanes((128, 128))
    for z in range(4):
        for half in range(2):
            full = val[half * 256 : half * 256 + 256, FULL[z] * 128 : FULL[z] * 128 + 128]
            out_ref[half * 4 + z, 0:256, :] = full.astype(BF)
            cols = slice(HALF[z] * 128, HALF[z] * 128 + 128)
            first = val[half * 256 : half * 256 + 128, cols]
            second = val[half * 256 + 128 : half * 256 + 256, cols]
            if z % 2 == 0:
                pair = jnp.where(low, first, swap_halves(second))
            else:
                pair = jnp.where(low, swap_halves(first), second)
            out_ref[half * 4 + z, 256:384, :] = pair.astype(BF)


def project(x, w):
    return pl.pallas_call(
        project_kernel,
        grid=(3,),
        in_specs=[
            pl.BlockSpec((512, D), lambda t: (0, 0)),
            pl.BlockSpec((D, D), lambda t: (0, t)),
        ],
        out_specs=pl.BlockSpec((8, 384, 128), lambda t: (0, t, 0)),
        out_shape=jax.ShapeDtypeStruct((8, 1152, 128), BF),
        scratch_shapes=[pltpu.VMEM((512, D), BF)],
        compiler_params=params(24),
        cost_estimate=pl.CostEstimate(
            flops=2 * 512 * D * 3 * D, bytes_accessed=6 * MIB, transcendentals=0
        ),
        name="project",
    )(x, w)


def rows_of(ref, start):
    return ref[:, start : start + 32, :].reshape(256, 128)


def scores_kernel(q_ref, k1_ref, k2_ref, out_ref):
    low = low_lanes((256, 256))
    zero = jnp.zeros((256, 256), BF)
    total = [None, None, None]

    def add(h, part):
        total[h] = part if total[h] is None else total[h] + part

    def keys(start):
        return jnp.concatenate([rows_of(k1_ref, start), rows_of(k2_ref, start)], axis=0)

    for start in range(0, 384, 64):
        q = jnp.concatenate([rows_of(q_ref, start), rows_of(q_ref, start + 32)], axis=1)
        k = jnp.concatenate([keys(start), keys(start + 32)], axis=1)
        if start < 256:
            add(0, dot_t(jnp.where(low, q, zero), k))
            add(1, dot_t(jnp.where(low, zero, q), k))
        else:
            add(2, dot_t(q, k))
    for h in range(3):
        out_ref[:, h] = total[h].astype(BF).reshape(16, 16, 512)


def scores(got, k2):
    return pl.pallas_call(
        scores_kernel,
        grid=(1,),
        in_specs=[
            pl.BlockSpec((8, 384, 128), lambda t: (0, 0, 0)),
            pl.BlockSpec((8, 384, 128), lambda t: (0, 1, 0)),
            pl.BlockSpec((8, 384, 128), lambda t: (0, 0, 0)),
        ],
        out_specs=pl.BlockSpec((16, 3, 16, 512), lambda t: (0, 0, 0, 0)),
        out_shape=jax.ShapeDtypeStruct((16, 3, 16, 512), BF),
        compiler_params=params(24),
        cost_estimate=pl.CostEstimate(
            flops=2 * 5 * 256 * 512 * 512, bytes_accessed=3 * MIB, transcendentals=0
        ),
        name="scores",
    )(got, got, k2)


def softmax_kernel(parts_ref, out_ref):
    total = parts_ref[0].astype(F32)
    for s in range(1, 16):
        total += parts_ref[s].astype(F32)
    total *= 1.0 / math.sqrt(DH * ROWS)
    e = jnp.exp(total - jnp.max(total, axis=-1, keepdims=True))
    w = (e / jnp.sum(e, axis=-1, keepdims=True)).astype(BF)
    for s in range(16):
        out_ref[s] = w


def softmax(parts):
    return pl.pallas_call(
        softmax_kernel,
        out_shape=jax.ShapeDtypeStruct((16, 3, 16, 512), BF),
        compiler_params=params(16),
        cost_estimate=pl.CostEstimate(flops=MIB, bytes_accessed=2 * MIB, transcendentals=24576),
        name="softmax",
    )(parts)


def attend_kernel(w_ref, v1_ref, v2_ref, out_ref, full, part):
    low = low_lanes((256, 256))

    def values(start):
        return jnp.concatenate([rows_of(v1_ref, start), rows_of(v2_ref, start)], axis=0)

    weights = [w_ref[:, h].reshape(256, 512) for h in range(3)]
    for r in range(0, 8, 2):
        v = jnp.concatenate([values(r * 32), values(r * 32 + 32)], axis=1)
        got = jnp.where(low, dot32(weights[0], v), dot32(weights[1], v))
        full[pl.ds(r, 256, stride=8), :] = got[:, :128]
        full[pl.ds(r + 1, 256, stride=8), :] = got[:, 128:]
    for r in range(0, 4, 2):
        v = jnp.concatenate([values(256 + r * 32), values(288 + r * 32)], axis=1)
        got = dot32(weights[2], v)
        for s in range(2):
            tile = got[:, s * 128 : s * 128 + 128]
            part[pl.ds(r + s, 256, stride=8), :] = tile
            part[pl.ds(r + s + 4, 256, stride=8), :] = swap_halves(tile)
    low = low_lanes((16, 128))
    for a in range(8):
        for s in range(8):
            at = (a * 8 + s) * 32
            to = s * 8 + a
            out_ref[to, 0:32, :] = full[at : at + 32, :].astype(BF)
            pair = jnp.where(low, part[at : at + 16, :], swap_halves(part[at + 16 : at + 32, :]))
            out_ref[to, 32:48, :] = pair.astype(BF)


def attend(w, got, v2):
    return pl.pallas_call(
        attend_kernel,
        grid=(1,),
        in_specs=[
            pl.BlockSpec((16, 3, 16, 512), lambda t: (0, 0, 0, 0)),
            pl.BlockSpec((8, 384, 128), lambda t: (0, 2, 0)),
            pl.BlockSpec((8, 384, 128), lambda t: (0, 0, 0)),
        ],
        out_specs=pl.BlockSpec((64, 48, 128), lambda t: (0, 0, 0)),
        out_shape=jax.ShapeDtypeStruct((64, 48, 128), BF),
        scratch_shapes=[pltpu.VMEM((2048, 128), F32), pltpu.VMEM((2048, 128), F32)],
        compiler_params=params(24),
        cost_estimate=pl.CostEstimate(
            flops=2 * 5 * 256 * 512 * 512, bytes_accessed=3 * MIB, transcendentals=0
        ),
        name="attend",
    )(w, got, v2)


def columns_kernel(
    att_ref, x_ref, wo_hbm, wqkv_hbm, wco_hbm, w1_hbm, w2_hbm, out_ref,
    wo, wqkv, wco, w1, w2, att, state, col, sems,
):
    copies = []
    for at, (src, dst) in enumerate(
        ((wo_hbm, wo), (wqkv_hbm, wqkv), (wco_hbm, wco), (w1_hbm, w1), (w2_hbm, w2))
    ):
        copies.append(pltpu.make_async_copy(src, dst, sems.at[at]))
        copies[-1].start()
    low = low_lanes((128, 128))
    for z in range(4):
        whole = att_ref[:, z, 0:32, :].astype(F32).reshape(16, 4, 8, 128)
        for i in range(4):
            tile = whole[:, i].reshape(128, 128).astype(BF)
            att[i * 128 : i * 128 + 128, FULL[z] * 128 : FULL[z] * 128 + 128] = tile
    for p in range(2):
        even = att_ref[:, 2 * p, 32:48, :].astype(F32).reshape(16, 2, 8, 128)
        odd = att_ref[:, 2 * p + 1, 32:48, :].astype(F32).reshape(16, 2, 8, 128)
        for i in range(4):
            first = even[:, i % 2].reshape(128, 128)
            second = odd[:, i % 2].reshape(128, 128)
            if i < 2:
                second = swap_halves(second)
            else:
                first = swap_halves(first)
            tile = jnp.where(low, first, second).astype(BF)
            at = HALF[2 * p] * 128
            att[i * 128 : i * 128 + 128, at : at + 128] = tile
    x = jnp.concatenate([x_ref[:, i].reshape(128, D) for i in range(4)], axis=0)
    copies[0].wait()
    after_rows = (x.astype(F32) + dot32(att[...], wo[...])).astype(BF)
    state[...] = after_rows
    normed = normalize(after_rows.astype(F32))
    copies[1].wait()
    for t in range(3):
        col[:, t * D : t * D + D] = dot32(normed, wqkv[:, t * D : t * D + D]).astype(BF)
    zero = jnp.zeros((128, 128), BF)
    for i in range(4):
        rows = slice(i * 128, i * 128 + 128)
        for t in range(6):
            q = col[rows, t * 128 : t * 128 + 128]
            k = col[rows, D + t * 128 : D + t * 128 + 128]
            v = col[rows, 2 * D + t * 128 : 2 * D + t * 128 + 128]
            pair = jnp.concatenate([jnp.where(low, q, zero), jnp.where(low, zero, q)], axis=0)
            s = dot_t(pair, k) * (1.0 / math.sqrt(DH))
            e = jnp.exp(s - jnp.max(s, axis=-1, keepdims=True))
            w = (e / jnp.sum(e, axis=-1, keepdims=True)).astype(BF)
            o = dot32(w, v)
            att[rows, t * 128 : t * 128 + 128] = jnp.where(low, o[:128], o[128:]).astype(BF)
    copies[2].wait()
    after_cols = (state[...].astype(F32) + dot32(att[...], wco[...])).astype(BF)
    state[...] = after_cols
    normed = normalize(after_cols.astype(F32))
    copies[3].wait()
    copies[4].wait()
    total = after_cols.astype(F32)
    for t in range(4):
        hidden = jax.nn.gelu(dot32(normed, w1[:, t * D : t * D + D])).astype(BF)
        total += dot32(hidden, w2[t * D : t * D + D, :])
    out = total.astype(BF)
    for i in range(4):
        out_ref[:, i] = out[i * 128 : i * 128 + 128].reshape(8, 16, D)


def columns(att, x, wo, wqkv, wco, w1, w2):
    vmem = pl.BlockSpec(memory_space=pltpu.VMEM)
    anywhere = pl.BlockSpec(memory_space=pl.ANY)
    return pl.pallas_call(
        columns_kernel,
        in_specs=[vmem, vmem] + [anywhere] * 5,
        out_specs=vmem,
        out_shape=jax.ShapeDtypeStruct((8, 4, 16, D), BF),
        scratch_shapes=[
            pltpu.VMEM((D, D), BF),
            pltpu.VMEM((D, 3 * D), BF),
            pltpu.VMEM((D, D), BF),
            pltpu.VMEM((D, FF), BF),
            pltpu.VMEM((FF, D), BF),
            pltpu.VMEM((512, D), BF),
            pltpu.VMEM((512, D), BF),
            pltpu.VMEM((512, 3 * D), BF),
            pltpu.SemaphoreType.DMA((5,)),
        ],
        compiler_params=params(48),
        cost_estimate=pl.CostEstimate(
            flops=8 * 10**9, bytes_accessed=18 * MIB, transcendentals=3 * MIB
        ),
        name="columns",
    )(att, x, wo, wqkv, wco, w1, w2)


def per_device(x, row_qkv, row_out, col_qkv, col_out, ff_in, ff_out):
    swap = [(0, 1), (1, 0)]
    got = lax.all_to_all(project(x.reshape(512, D), row_qkv), ("y_hi", "z"), 0, 0, tiled=True)
    k2 = lax.ppermute(got[:, 384:768], "core", swap)
    v2 = lax.ppermute(got[:, 768:], "core", swap)
    x_cols = x.reshape(16, 8, 4, D).transpose(1, 2, 0, 3)
    x_cols = lax.all_to_all(x_cols, SEQ, 0, 0, tiled=True)
    parts = lax.all_to_all(scores(got, k2), PLANE, 0, 0, tiled=True)
    weights = lax.all_to_all(softmax(parts), PLANE, 0, 0, tiled=True)
    att = lax.all_to_all(attend(weights, got, v2), CHIPS, 0, 0, tiled=True)
    out = columns(att.reshape(16, 4, 48, 128), x_cols, row_out, col_qkv, col_out, ff_in, ff_out)
    out = lax.all_to_all(out, SEQ, 0, 0, tiled=True)
    return out.transpose(2, 0, 1, 3).reshape(16, 32, D)


def solution(mesh):
    fine = Mesh(mesh.devices.reshape(2, 4, 2, 4, 2), ("y_lo", "x", "y_hi", "z", "core"))
    tokens = P(SEQ, ("y_hi", "z", "core"), None)
    placed = (tokens, P(), P(), P(), P(), P(), P())
    return jax.shard_map(per_device, mesh=fine, in_specs=placed, out_specs=tokens, check_vma=False)
```

time: 265 us -> 155 us (0.58)
  local copies, waits for them, and re-layouts: 83 us -> 12 us
  matrix products: 29.6 us -> 0 us
  Pallas kernels: 0 us -> 20.6 us
  other arithmetic: 12.2 us -> 0 us
  starting transfers between devices: 14.9 us -> 7.92 us
  blocking collectives: 99.6 us -> 92.7 us
  waiting for transfers between devices: 24.2 us -> 21 us
    all_gather x1 -> x0, blocking collectives: 47.7 us -> none  [per_device(): weights = lax.all_gather(weights, PLANE, axis=0, tiled=False)]
    all_to_all x1 -> x3, blocking collectives: 39.1 us -> 79 us  [the longest x1 39 us: per_device(): lax.all_to_all(project(x.reshape(512, D), row_qkv), ('y_hi', 'z'), 0, 0,...]
    reshape x7 -> x0, local copies, waits for them, and re-layouts: 33.7 us -> none  [the longest x1 12.2 us: per_device(): got = got.reshape(8, 8, 32, 3, HG, DH)]
    dot_general x9 -> x0, matrix products: 29.6 us -> none  [the longest x4 17.3 us: dot32(): return jnp.dot(a, b, preferred_element_type=jnp.float32)]
    pallas_call x0 -> x5, Pallas kernels: none -> 20.6 us  [the longest x1 13.7 us: columns(): pl.pallas_call(columns_kernel, in_specs=[vmem, vmem] + [anywhere] * 5, ou...]
    convert_element_type x7 -> x0, local copies, waits for them, and re-layouts: 19.4 us -> none  [the longest x3 10.5 us: per_device(): scores.reshape(HG, 16, 16, 512).transpose(1, 0, 2, 3).astype(jnp.bfloat16)]
    all_to_all x2 -> x1, waiting for transfers between devices: 20.8 us -> 11 us  [per_device(): weights = lax.all_to_all(softmax(parts), PLANE, 0, 0, tiled=True)]
    all_to_all x1, waiting for transfers between devices: 0.01 us -> 7.74 us  [per_device(): x_cols = lax.all_to_all(x_cols, SEQ, 0, 0, tiled=True)]
  transfers between devices with their start and end apart: 5 -> 4, of which waited for: 3 -> 3; matrix products, arithmetic and copies ran while one was open for 11% -> 2% of each run, Pallas kernels for 0% -> 1%
where the time goes in v2:
time: 155 us; the launch traced here: 154 us
  blocking collectives  92.7 us (60%)
  waiting for transfers between devices  21 us (14%)
  Pallas kernels  20.6 us (13%)
  local copies, waits for them, and re-layouts  12 us (8%)
  starting transfers between devices  7.92 us (5%)
    all_to_all x1, blocking collectives, per_device(): lax.all_to_all(project(x.reshape(512, D), row_qkv), ('y_hi', 'z'), 0, 0,...  39 us
    all_to_all x1, blocking collectives, per_device(): att = lax.all_to_all(attend(weights, got, v2), CHIPS, 0, 0, tiled=True)  20.6 us
    all_to_all x1, blocking collectives, per_device(): parts = lax.all_to_all(scores(got, k2), PLANE, 0, 0, tiled=True)  19.3 us
    all_to_all x1, blocking collectives, per_device(): out = lax.all_to_all(out, SEQ, 0, 0, tiled=True)  13.7 us
    pallas_call x1, Pallas kernels, columns(): pl.pallas_call(columns_kernel, in_specs=[vmem, vmem] + [anywhere] * 5, ou...  13.7 us
    all_to_all x1, waiting for transfers between devices, per_device(): weights = lax.all_to_all(softmax(parts), PLANE, 0, 0, tiled=True)  11 us
    unnamed x13, local copies, waits for them, and re-layouts  9.89 us
    all_to_all x1, waiting for transfers between devices, per_device(): x_cols = lax.all_to_all(x_cols, SEQ, 0, 0, tiled=True)  7.74 us
  transfers between devices with their start and end apart: 4, of which 3 were waited for; matrix products, arithmetic and copies ran while one was open for 2% of the time, Pallas kernels for 1%

profile of v2, /device:TPU:0, one launch (start us, length us, event | category | flops | bytes accessed | tf_op | source)
XLA Modules:
  0.0 154.4 jit_solution(1655334220061024068)
XLA Ops:
  0.0 0.0 copy-start.2
  0.0 1.1 copy-done.2
  1.1 0.0 copy-start.3
  1.1 2.0 %copy-done.3 = bf16[768,2304]{1,0:T(8,128)(2,1)S(1)} copy-done((bf16[768,2304]{1,0:T(8,128)(2,1)S(1)}, bf16[768,2304]{1,0:T(8,128)(2,1)}, u32[]{:S(2)}) %copy-start.3) | copy-done | bytes 3538968
  3.1 3.4 %project.1 = bf16[8,1152,128]{2,1,0:T(8,128)(2,1)S(1)} custom-call(bf16[512,768]{1,0:T(8,128)(2,1)S(1)} %bitcast.8, bf16[768,2304]{1,0:T(8,128)(2,1)S(1)} %copy-done.3), custom_call_target="tpu_custom_call" | custom-call | flops 1811939328 | bytes 6291456 | tf_op jit(solution)/shard_map/project/pallas_call | solution.py:76
  6.5 39.0 %all_to_all.30.q_ref.k1_ref.v1_ref = bf16[8,1152,128]{2,1,0:T(8,128)(2,1)S(1)} all-to-all(bf16[8,1152,128]{2,1,0:T(8,128)(2,1)S(1)} %project.1), channel_id=1, replica_groups=mesh['y_lo'=2,'x'=4,'y_hi'=2,'z'=4,'core'=2] {'y_hi','z'}, dimensions={0} | all-to-all | bytes 4718592 | tf_op jit(solution)/shard_map/all_to_all | solution.py:304
  45.5 1.0 fusion
  46.6 0.0 collective-permute-start
  46.6 2.3 %collective-permute-done.k2_ref = bf16[8,384,128]{2,1,0:T(8,128)(2,1)S(1)} collective-permute-done((bf16[8,384,128]{2,1,0:T(8,128)(2,1)S(1)}, bf16[8,384,128]{2,1,0:T(8,128)(2,1)S(1)}, u32[]{:S(2)}, u32[]{:S(2)}) %collective-permute-start) | collective-permute-done | bytes 786464 | tf_op jit(solution)/shard_map/ppermute | solution.py:305
  48.8 0.9 scores.1
  49.7 19.3 %all_to_all.31.parts_ref = bf16[16,3,16,512]{3,2,1,0:T(8,128)(2,1)S(1)} all-to-all(bf16[16,3,16,512]{3,2,1,0:T(8,128)(2,1)S(1)} %scores.1), channel_id=1, replica_groups=mesh['y_lo'=2,'x'=4,'y_hi'=2,'z'=4,'core'=2] {'y_lo','x','y_hi'}, dimensions={0} | all-to-all | bytes 1572864 | tf_op jit(solution)/shard_map/all_to_all | solution.py:309
  69.1 0.3 softmax.1
  69.4 0.0 copy-start.1
  69.4 0.9 copy-done.1
  70.3 3.6 %all-to-all-start.2 = ((bf16[16,3,16,512]{3,2,1,0:T(8,128)(2,1)}), bf16[16,3,16,512]{3,2,1,0:T(8,128)(2,1)S(1)}, u32[]{:S(2)}, u32[]{:S(2)}) async-start(bf16[16,3,16,512]{3,2,1,0:T(8,128)(2,1)} %copy-done.1), calls=%async_computation.2 | async-start | bytes 1572864 | tf_op jit(solution)/shard_map/all_to_all | solution.py:310
  73.9 0.1 collective-permute-start.1
  74.0 2.5 %copy.8 = bf16[16,32,768]{2,0,1:T(8,128)(2,1)} copy(bf16[16,32,768]{2,1,0:T(8,128)(2,1)} %param.7) | data formatting | bytes 1572864 | tf_op args[0]
  76.4 11.0 %all-to-all-done.2.w_ref = bf16[16,3,16,512]{3,2,1,0:T(8,128)(2,1)S(1)} async-done(((bf16[16,3,16,512]{3,2,1,0:T(8,128)(2,1)}), bf16[16,3,16,512]{3,2,1,0:T(8,128)(2,1)S(1)}, u32[]{:S(2)}, u32[]{:S(2)}) %all-to-all-start.2) | async-done | bytes 786464 | tf_op jit(solution)/shard_map/all_to_all | solution.py:310
  87.4 4.2 %all-to-all-start.4 = ((bf16[8,4,16,768]{3,2,1,0:T(8,128)(2,1)}), bf16[8,4,16,768]{3,2,1,0:T(8,128)(2,1)}, u32[]{:S(2)}, u32[]{:S(2)}) async-start(bf16[8,4,16,768]{3,2,1,0:T(8,128)(2,1)} %bitcast.10), calls=%async_computation.4 | async-start | bytes 1572864 | tf_op jit(solution)/shard_map/all_to_all | solution.py:308
  91.6 0.0 collective-permute-done.1.v2_ref
  91.7 2.3 %attend.1 = bf16[64,48,128]{2,1,0:T(8,128)(2,1)S(1)} custom-call(bf16[16,3,16,512]{3,2,1,0:T(8,128)(2,1)S(1)} %all-to-all-done.2.w_ref, bf16[8,1152,128]{2,1,0:T(8,128)(2,1)S(1)} %all_to_all.30.q_ref.k1_ref.v1_ref, bf16[8,384,128]{2,1,0:T(8,128)(2,1)} %collective-permute-done.1.v2_ref), custom_call_target="tpu_custom_call" | custom-call | flops 671088640 | bytes 3145728 | tf_op jit(solution)/shard_map/attend/pallas_call | solution.py:191
  94.0 0.0 copy-start
  94.0 0.9 copy-done
  94.9 7.7 %all-to-all-done.4.x_ref = bf16[8,4,16,768]{3,2,1,0:T(8,128)(2,1)} async-done(((bf16[8,4,16,768]{3,2,1,0:T(8,128)(2,1)}), bf16[8,4,16,768]{3,2,1,0:T(8,128)(2,1)}, u32[]{:S(2)}, u32[]{:S(2)}) %all-to-all-start.4) | async-done | bytes 786464 | tf_op jit(solution)/shard_map/all_to_all | solution.py:308
  102.6 20.6 %all_to_all.32 = bf16[64,48,128]{2,1,0:T(8,128)(2,1)S(1)} all-to-all(bf16[64,48,128]{2,1,0:T(8,128)(2,1)} %copy-done), channel_id=1, replica_groups=mesh['y_lo'=2,'x'=4,'y_hi'=2,'z'=4,'core'=2] {'y_lo','x','y_hi','z'}, dimensions={0} | all-to-all | bytes 1572864 | tf_op jit(solution)/shard_map/all_to_all | solution.py:311
  123.2 0.0 copy-start.4
  123.2 1.3 copy-done.4
  124.5 0.0 copy-start.5
  124.5 1.3 copy-done.5
  125.8 13.7 %columns.1 = bf16[8,4,16,768]{3,2,1,0:T(8,128)(2,1)S(1)} custom-call(bf16[16,4,48,128]{3,2,1,0:T(8,128)(2,1)S(1)} %bitcast.9, bf16[8,4,16,768]{3,2,1,0:T(8,128)(2,1)} %all-to-all-done.4.x_ref, bf16[768,768]{1,0:T(8,128)(2,1)S(1)} %copy-done.4, bf16[768,2304]{1,0:T(8,128)(2,1)} %wqkv_hbm.1, bf16[768,768]{1,0:T(8,128)(2,1)S(1)} %copy-done.5, ...), custom_call_target="tpu_custom_call" | custom-call | flops 8000000000 | bytes 18874368 | tf_op jit(solution)/shard_map/columns/pallas_call | solution.py:278
  139.5 13.7 %all_to_all.33 = bf16[8,4,16,768]{3,2,1,0:T(8,128)(2,1)S(1)} all-to-all(bf16[8,4,16,768]{3,2,1,0:T(8,128)(2,1)S(1)} %columns.1), channel_id=1, replica_groups=mesh['y_lo'=2,'x'=4,'y_hi'=2,'z'=4,'core'=2] {'y_lo','x'}, dimensions={0} | all-to-all | bytes 1572864 | tf_op jit(solution)/shard_map/all_to_all | solution.py:313
  153.2 1.1 copy.9
Async XLA Ops:
  0.0 1.1 copy-start.2
  1.1 2.0 %copy-start.3 = (bf16[768,2304]{1,0:T(8,128)(2,1)S(1)}, bf16[768,2304]{1,0:T(8,128)(2,1)}, u32[]{:S(2)}) copy-start(bf16[768,2304]{1,0:T(8,128)(2,1)} %w_ref.1) | copy-start | bytes 10616836
  46.6 2.3 %collective-permute-start = (bf16[8,384,128]{2,1,0:T(8,128)(2,1)S(1)}, bf16[8,384,128]{2,1,0:T(8,128)(2,1)S(1)}, u32[]{:S(2)}, u32[]{:S(2)}) collective-permute-start(bf16[8,384,128]{2,1,0:T(8,128)(2,1)S(1)} %get-tuple-element.6), channel_id=1, source_target_pairs={{0,1},{1,0},{2,3},{3,2},{4,5},{5,4},{6,7},{7,6},{8,9},{9,8},{10,11... | collective-permute-start | bytes 2359304 | tf_op jit(solution)/shard_map/ppermute | solution.py:305
  69.4 0.9 copy-start.1
  70.3 17.2 %all-to-all-start.2 = ((bf16[16,3,16,512]{3,2,1,0:T(8,128)(2,1)}), bf16[16,3,16,512]{3,2,1,0:T(8,128)(2,1)S(1)}, u32[]{:S(2)}, u32[]{:S(2)}) async-start(bf16[16,3,16,512]{3,2,1,0:T(8,128)(2,1)} %copy-done.1), calls=%async_computation.2 | async-start | bytes 1572864 | tf_op jit(solution)/shard_map/all_to_all | solution.py:310
  73.9 17.8 %collective-permute-start.1 = (bf16[8,384,128]{2,1,0:T(8,128)(2,1)}, bf16[8,384,128]{2,1,0:T(8,128)(2,1)}, u32[]{:S(2)}, u32[]{:S(2)}) collective-permute-start(bf16[8,384,128]{2,1,0:T(8,128)(2,1)} %get-tuple-element.5), channel_id=1, source_target_pairs={{0,1},{1,0},{2,3},{3,2},{4,5},{5,4},{6,7},{7,6},{8,9},{9,8},{10,11... | collective-permute-start | bytes 2359304 | tf_op jit(solution)/shard_map/ppermute | solution.py:306
  87.4 15.2 %all-to-all-start.4 = ((bf16[8,4,16,768]{3,2,1,0:T(8,128)(2,1)}), bf16[8,4,16,768]{3,2,1,0:T(8,128)(2,1)}, u32[]{:S(2)}, u32[]{:S(2)}) async-start(bf16[8,4,16,768]{3,2,1,0:T(8,128)(2,1)} %bitcast.10), calls=%async_computation.4 | async-start | bytes 1572864 | tf_op jit(solution)/shard_map/all_to_all | solution.py:308
  94.0 0.9 copy-start
  123.2 1.3 copy-start.4
  124.5 1.3 copy-start.5

commit v3 on v2

--- a/solution.py
+++ b/solution.py
@@ -51,39 +51,59 @@
     return pltpu.CompilerParams(vmem_limit_bytes=mib * MIB, **kw)
 
 
-def project_kernel(x_ref, w_ref, out_ref, normed):
-    @pl.when(pl.program_id(0) == 0)
-    def _():
-        normed[...] = normalize(x_ref[...].astype(F32))
-
-    val = dot32(normed[...], w_ref[...])
+def project_kernel(x_hbm, w_hbm, out_hbm, x_ref, w_ref, out_ref, sems):
+    get_x = pltpu.make_async_copy(x_hbm, x_ref, sems.at[3])
+    get_x.start()
+    get_w = []
+    for t in range(3):
+        cols = slice(t * D, t * D + D)
+        get_w.append(pltpu.make_async_copy(w_hbm.at[:, cols], w_ref.at[:, cols], sems.at[t]))
+    get_w[0].start()
+    get_x.wait()
+    get_w[1].start()
+    get_w[2].start()
+    normed = normalize(x_ref[...].astype(F32))
     low = low_lanes((128, 128))
-    for z in range(4):
-        for half in range(2):
-            full = val[half * 256 : half * 256 + 256, FULL[z] * 128 : FULL[z] * 128 + 128]
-            out_ref[half * 4 + z, 0:256, :] = full.astype(BF)
-            cols = slice(HALF[z] * 128, HALF[z] * 128 + 128)
-            first = val[half * 256 : half * 256 + 128, cols]
-            second = val[half * 256 + 128 : half * 256 + 256, cols]
-            if z % 2 == 0:
-                pair = jnp.where(low, first, swap_halves(second))
-            else:
-                pair = jnp.where(low, swap_halves(first), second)
-            out_ref[half * 4 + z, 256:384, :] = pair.astype(BF)
+    put = []
+    for t in range(3):
+        get_w[t].wait()
+        val = dot32(normed, w_ref[:, t * D : t * D + D])
+        at = t * 384
+        for z in range(4):
+            for half in range(2):
+                full = val[half * 256 : half * 256 + 256, FULL[z] * 128 : FULL[z] * 128 + 128]
+                out_ref[half * 4 + z, at : at + 256, :] = full.astype(BF)
+                cols = slice(HALF[z] * 128, HALF[z] * 128 + 128)
+                first = val[half * 256 : half * 256 + 128, cols]
+                second = val[half * 256 + 128 : half * 256 + 256, cols]
+                if z % 2 == 0:
+                    pair = jnp.where(low, first, swap_halves(second))
+                else:
+                    pair = jnp.where(low, swap_halves(first), second)
+                out_ref[half * 4 + z, at + 256 : at + 384, :] = pair.astype(BF)
+        part = pl.ds(at, 384)
+        put.append(
+            pltpu.make_async_copy(out_ref.at[:, part], out_hbm.at[:, part], sems.at[4 + t])
+        )
+        put[t].start()
+    for t in range(3):
+        put[t].wait()
 
 
 def project(x, w):
+    hbm = pl.BlockSpec(memory_space=pltpu.HBM)
     return pl.pallas_call(
         project_kernel,
-        grid=(3,),
-        in_specs=[
-            pl.BlockSpec((512, D), lambda t: (0, 0)),
-            pl.BlockSpec((D, D), lambda t: (0, t)),
+        in_specs=[hbm, hbm],
+        out_specs=hbm,
+        out_shape=jax.ShapeDtypeStruct((8, 1152, 128), BF),
+        scratch_shapes=[
+            pltpu.VMEM((512, D), BF),
+            pltpu.VMEM((D, 3 * D), BF),
+            pltpu.VMEM((8, 1152, 128), BF),
+            pltpu.SemaphoreType.DMA((7,)),
         ],
-        out_specs=pl.BlockSpec((8, 384, 128), lambda t: (0, t, 0)),
-        out_shape=jax.ShapeDtypeStruct((8, 1152, 128), BF),
-        scratch_shapes=[pltpu.VMEM((512, D), BF)],
-        compiler_params=params(24),
+        compiler_params=params(58),
         cost_estimate=pl.CostEstimate(
             flops=2 * 512 * D * 3 * D, bytes_accessed=6 * MIB, transcendentals=0
         ),
@@ -129,7 +149,7 @@
         ],
         out_specs=pl.BlockSpec((16, 3, 16, 512), lambda t: (0, 0, 0, 0)),
         out_shape=jax.ShapeDtypeStruct((16, 3, 16, 512), BF),
-        compiler_params=params(24),
+        compiler_params=params(12),
         cost_estimate=pl.CostEstimate(
             flops=2 * 5 * 256 * 512 * 512, bytes_accessed=3 * MIB, transcendentals=0
         ),
@@ -152,7 +172,7 @@
     return pl.pallas_call(
         softmax_kernel,
         out_shape=jax.ShapeDtypeStruct((16, 3, 16, 512), BF),
-        compiler_params=params(16),
+        compiler_params=params(6),
         cost_estimate=pl.CostEstimate(flops=MIB, bytes_accessed=2 * MIB, transcendentals=24576),
         name="softmax",
     )(parts)
@@ -199,7 +219,7 @@
         out_specs=pl.BlockSpec((64, 48, 128), lambda t: (0, 0, 0)),
         out_shape=jax.ShapeDtypeStruct((64, 48, 128), BF),
         scratch_shapes=[pltpu.VMEM((2048, 128), F32), pltpu.VMEM((2048, 128), F32)],
-        compiler_params=params(24),
+        compiler_params=params(12),
         cost_estimate=pl.CostEstimate(
             flops=2 * 5 * 256 * 512 * 512, bytes_accessed=3 * MIB, transcendentals=0
         ),
@@ -208,15 +228,29 @@
 
 
 def columns_kernel(
-    att_ref, x_ref, wo_hbm, wqkv_hbm, wco_hbm, w1_hbm, w2_hbm, out_ref,
-    wo, wqkv, wco, w1, w2, att, state, col, sems,
+    me_ref, att_hbm, x0, x1, x2, x3, wo_hbm, wqkv_hbm, wco_hbm, w1_hbm, w2_hbm, out_ref,
+    att_ref, wo, wqkv, wco, w1, w2, att, x_in, state, col, sems,
 ):
-    copies = []
-    for at, (src, dst) in enumerate(
-        ((wo_hbm, wo), (wqkv_hbm, wqkv), (wco_hbm, wco), (w1_hbm, w1), (w2_hbm, w2))
-    ):
-        copies.append(pltpu.make_async_copy(src, dst, sems.at[at]))
-        copies[-1].start()
+    def copy(src, dst, sem):
+        return pltpu.make_async_copy(src, dst, sems.at[sem])
+
+    get_att = copy(att_hbm, att_ref, 0)
+    get_att.start()
+    get_wo = copy(wo_hbm, wo, 1)
+    get_wo.start()
+    get_x = []
+    for k, block in enumerate((x0, x1, x2, x3)):
+        for side in range(2):
+            y = me_ref[0] if side == 0 else 1 - me_ref[0]
+            at = pl.multiple_of((y * 4 + (me_ref[1] ^ k)) * 16, 16)
+            get_x.append(copy(block.at[side], x_in.at[:, pl.ds(at, 16), :], 2 + 2 * k + side))
+            get_x[-1].start()
+    get_wqkv = copy(wqkv_hbm, wqkv, 10)
+    get_wqkv.start()
+    get_wco = copy(wco_hbm, wco, 11)
+    get_w1 = copy(w1_hbm, w1, 12)
+    get_w2 = copy(w2_hbm, w2, 13)
+    get_att.wait()
     low = low_lanes((128, 128))
     for z in range(4):
         whole = att_ref[:, z, 0:32, :].astype(F32).reshape(16, 4, 8, 128)
@@ -236,12 +270,16 @@
             tile = jnp.where(low, first, second).astype(BF)
             at = HALF[2 * p] * 128
             att[i * 128 : i * 128 + 128, at : at + 128] = tile
-    x = jnp.concatenate([x_ref[:, i].reshape(128, D) for i in range(4)], axis=0)
-    copies[0].wait()
-    after_rows = (x.astype(F32) + dot32(att[...], wo[...])).astype(BF)
+    get_wo.wait()
+    for block in get_x:
+        block.wait()
+    after_rows = (x_in[...].reshape(512, D).astype(F32) + dot32(att[...], wo[...])).astype(BF)
     state[...] = after_rows
     normed = normalize(after_rows.astype(F32))
-    copies[1].wait()
+    get_wqkv.wait()
+    get_wco.start()
+    get_w1.start()
+    get_w2.start()
     for t in range(3):
         col[:, t * D : t * D + D] = dot32(normed, wqkv[:, t * D : t * D + D]).astype(BF)
     zero = jnp.zeros((128, 128), BF)
@@ -257,12 +295,12 @@
             w = (e / jnp.sum(e, axis=-1, keepdims=True)).astype(BF)
             o = dot32(w, v)
             att[rows, t * 128 : t * 128 + 128] = jnp.where(low, o[:128], o[128:]).astype(BF)
-    copies[2].wait()
+    get_wco.wait()
     after_cols = (state[...].astype(F32) + dot32(att[...], wco[...])).astype(BF)
     state[...] = after_cols
     normed = normalize(after_cols.astype(F32))
-    copies[3].wait()
-    copies[4].wait()
+    get_w1.wait()
+    get_w2.wait()
     total = after_cols.astype(F32)
     for t in range(4):
         hidden = jax.nn.gelu(dot32(normed, w1[:, t * D : t * D + D])).astype(BF)
@@ -272,44 +310,60 @@
         out_ref[:, i] = out[i * 128 : i * 128 + 128].reshape(8, 16, D)
 
 
-def columns(att, x, wo, wqkv, wco, w1, w2):
+def columns(me, att, x, wo, wqkv, wco, w1, w2):
     vmem = pl.BlockSpec(memory_space=pltpu.VMEM)
     anywhere = pl.BlockSpec(memory_space=pl.ANY)
     return pl.pallas_call(
         columns_kernel,
-        in_specs=[vmem, vmem] + [anywhere] * 5,
+        in_specs=[pl.BlockSpec(memory_space=pltpu.SMEM)] + [anywhere] * 10,
         out_specs=vmem,
         out_shape=jax.ShapeDtypeStruct((8, 4, 16, D), BF),
         scratch_shapes=[
+            pltpu.VMEM((16, 4, 48, 128), BF),
             pltpu.VMEM((D, D), BF),
             pltpu.VMEM((D, 3 * D), BF),
             pltpu.VMEM((D, D), BF),
             pltpu.VMEM((D, FF), BF),
             pltpu.VMEM((FF, D), BF),
             pltpu.VMEM((512, D), BF),
+            pltpu.VMEM((4, 128, D), BF),
             pltpu.VMEM((512, D), BF),
             pltpu.VMEM((512, 3 * D), BF),
-            pltpu.SemaphoreType.DMA((5,)),
+            pltpu.SemaphoreType.DMA((14,)),
         ],
-        compiler_params=params(48),
+        compiler_params=params(60),
         cost_estimate=pl.CostEstimate(
             flops=8 * 10**9, bytes_accessed=18 * MIB, transcendentals=3 * MIB
         ),
         name="columns",
-    )(att, x, wo, wqkv, wco, w1, w2)
+    )(me, att, *x, wo, wqkv, wco, w1, w2)
 
 
 def per_device(x, row_qkv, row_out, col_qkv, col_out, ff_in, ff_out):
+    barrier = lax.optimization_barrier
     swap = [(0, 1), (1, 0)]
-    got = lax.all_to_all(project(x.reshape(512, D), row_qkv), ("y_hi", "z"), 0, 0, tiled=True)
+    y_me, x_me = lax.axis_index("y_lo"), lax.axis_index("x")
+    halves = x.reshape(16, 2, 16, D)
+    far = lax.ppermute(lax.dynamic_index_in_dim(halves, 1 - y_me, 1, False), "y_lo", swap)
+    proj, x, far = barrier((project(x.reshape(512, D), row_qkv), x, far))
+    got = lax.all_to_all(proj, ("y_hi", "z"), 0, 0, tiled=True)
+    mine = lax.dynamic_index_in_dim(x.reshape(16, 2, 16, D), y_me, 1, False)
+    x_cols = jnp.stack([mine, far]).reshape(2, 16, 4, 4, D).transpose(2, 0, 3, 1, 4)
+    near = []
+    for k in range(4):
+        block = lax.dynamic_index_in_dim(x_cols, x_me ^ k, 0, False)
+        near.append(lax.ppermute(block, "x", [(i, i ^ k) for i in range(4)]) if k else block)
+    got, near = barrier((got, near))
     k2 = lax.ppermute(got[:, 384:768], "core", swap)
+    parts, got = barrier((scores(got, k2), got))
+    parts = lax.all_to_all(parts, PLANE, 0, 0, tiled=True)
     v2 = lax.ppermute(got[:, 768:], "core", swap)
-    x_cols = x.reshape(16, 8, 4, D).transpose(1, 2, 0, 3)
-    x_cols = lax.all_to_all(x_cols, SEQ, 0, 0, tiled=True)
-    parts = lax.all_to_all(scores(got, k2), PLANE, 0, 0, tiled=True)
-    weights = lax.all_to_all(softmax(parts), PLANE, 0, 0, tiled=True)
-    att = lax.all_to_all(attend(weights, got, v2), CHIPS, 0, 0, tiled=True)
-    out = columns(att.reshape(16, 4, 48, 128), x_cols, row_out, col_qkv, col_out, ff_in, ff_out)
+    parts, v2 = barrier((parts, v2))
+    shares = lax.all_to_all(softmax(parts), PLANE, 0, 0, tiled=True)
+    att = lax.all_to_all(attend(shares, got, v2), CHIPS, 0, 0, tiled=True)
+    att = att.reshape(16, 4, 48, 128)
+    me = jnp.stack([y_me, x_me]).astype(jnp.int32)
+    out = columns(me, att, near, row_out, col_qkv, col_out, ff_in, ff_out)
     out = lax.all_to_all(out, SEQ, 0, 0, tiled=True)
     return out.transpose(2, 0, 1, 3).reshape(16, 32, D)
 

time: 155 us -> 143 us (0.923)
  blocking collectives: 92.7 us -> 52 us
  waiting for transfers between devices: 21 us -> 42.1 us
  starting transfers between devices: 7.92 us -> 20.3 us
  local copies, waits for them, and re-layouts: 12 us -> 3.41 us
  Pallas kernels: 20.6 us -> 23.6 us
    all_to_all x3 -> x2, blocking collectives: 79 us -> 38.2 us  [the longest x1 21.2 us: per_device(): parts = lax.all_to_all(parts, PLANE, 0, 0, tiled=True)]
    ppermute x0 -> x4, waiting for transfers between devices: none -> 10.9 us  [the longest x3 7.39 us: per_device(): lax.ppermute(block, 'x', [(i, i ^ k) for i in range(4)])]
    all_to_all x2, waiting for transfers between devices: 18.7 us -> 28.9 us  [the longest x1 15.3 us: per_device(): got = lax.all_to_all(proj, ('y_hi', 'z'), 0, 0, tiled=True)]
    unnamed x13 -> x11, local copies, waits for them, and re-layouts: 9.89 us -> 1.02 us
    ppermute x0 -> x4, starting transfers between devices: none -> 6.44 us  [the longest x3 4.7 us: per_device(): lax.ppermute(block, 'x', [(i, i ^ k) for i in range(4)])]
    all_to_all x2, starting transfers between devices: 7.83 us -> 13.5 us  [the longest x1 8.11 us: per_device(): got = lax.all_to_all(proj, ('y_hi', 'z'), 0, 0, tiled=True)]
    pallas_call x2, Pallas kernels: 17.1 us -> 20.4 us  [the longest x1 14.9 us: columns(): pl.pallas_call(columns_kernel, in_specs=[pl.BlockSpec(memory_space=pltpu....]
  transfers between devices with their start and end apart: 4 -> 8, of which waited for: 3 -> 7; matrix products, arithmetic and copies ran while one was open for 2% -> 1% of each run, Pallas kernels for 1% -> 4%
where the time goes in v3:
time: 143 us
  blocking collectives  52 us (36%)
  waiting for transfers between devices  42.1 us (29%)
  Pallas kernels  23.6 us (17%)
  starting transfers between devices  20.3 us (14%)
  local copies, waits for them, and re-layouts  3.41 us (2%)
    all_to_all x1, blocking collectives, per_device(): parts = lax.all_to_all(parts, PLANE, 0, 0, tiled=True)  21.2 us
    all_to_all x1, blocking collectives, per_device(): shares = lax.all_to_all(softmax(parts), PLANE, 0, 0, tiled=True)  17.1 us
    all_to_all x1, waiting for transfers between devices, per_device(): got = lax.all_to_all(proj, ('y_hi', 'z'), 0, 0, tiled=True)  15.3 us
    pallas_call x1, Pallas kernels, columns(): pl.pallas_call(columns_kernel, in_specs=[pl.BlockSpec(memory_space=pltpu....  14.9 us
    all_to_all x1, blocking collectives, per_device(): out = lax.all_to_all(out, SEQ, 0, 0, tiled=True)  13.7 us
    all_to_all x1, waiting for transfers between devices, per_device(): att = lax.all_to_all(attend(shares, got, v2), CHIPS, 0, 0, tiled=True)  13.6 us
    all_to_all x1, starting transfers between devices, per_device(): got = lax.all_to_all(proj, ('y_hi', 'z'), 0, 0, tiled=True)  8.11 us
    ppermute x3, waiting for transfers between devices, per_device(): lax.ppermute(block, 'x', [(i, i ^ k) for i in range(4)])  7.39 us
  transfers between devices with their start and end apart: 8, of which 7 were waited for; matrix products, arithmetic and copies ran while one was open for 1% of the time, Pallas kernels for 4%

profile of v3, /device:TPU:0, one launch (start us, length us, event | category | flops | bytes accessed | tf_op | source)
XLA Modules:
  0.0 142.9 jit_solution(9986235502655387039)
XLA Ops:
  0.0 1.0 constant_dynamic-slice_fusion.1
  1.0 0.1 copy.13
  1.2 1.7 %collective-permute-start = (bf16[16,16,768]{2,0,1:T(8,128)(2,1)S(1)}, bf16[16,16,768]{2,0,1:T(8,128)(2,1)S(1)}, u32[]{:S(2)}, u32[]{:S(2)}) collective-permute-start(bf16[16,16,768]{2,0,1:T(8,128)(2,1)S(1)} %bitcast.36), channel_id=1, source_target_pairs={{0,64},{64,0},{1,65},{65,1},{2,66},{66,2},{3,67},{67,3},{4,68},{68... | collective-permute-start | bytes 1179656 | tf_op jit(solution)/shard_map/ppermute | solution.py:347
  2.9 5.6 %project.1 = bf16[8,1152,128]{2,1,0:T(8,128)(2,1)} custom-call(bf16[512,768]{1,0:T(8,128)(2,1)} %bitcast.34, bf16[768,2304]{1,0:T(8,128)(2,1)} %w_hbm.1), custom_call_target="tpu_custom_call" | custom-call | flops 1811939328 | bytes 6291456 | tf_op jit(solution)/shard_map/project/pallas_call | solution.py:95
  8.5 0.0 copy-start.1
  8.5 3.5 %collective-permute-done = bf16[16,16,768]{2,0,1:T(8,128)(2,1)S(1)} collective-permute-done((bf16[16,16,768]{2,0,1:T(8,128)(2,1)S(1)}, bf16[16,16,768]{2,0,1:T(8,128)(2,1)S(1)}, u32[]{:S(2)}, u32[]{:S(2)}) %collective-permute-start) | collective-permute-done | bytes 393248 | tf_op jit(solution)/shard_map/ppermute | solution.py:347
  12.0 8.1 %all-to-all-start = ((bf16[8,1152,128]{2,1,0:T(8,128)(2,1)}), bf16[8,1152,128]{2,1,0:T(8,128)(2,1)S(1)}, u32[]{:S(2)}, u32[]{:S(2)}) async-start(bf16[8,1152,128]{2,1,0:T(8,128)(2,1)} %project.1), calls=%async_computation | async-start | bytes 4718592 | tf_op jit(solution)/shard_map/all_to_all | solution.py:349
  20.1 0.0 copy-done.1
  20.2 0.1 copy.11
  20.3 0.8 fusion.1
  21.0 2.8 %collective-permute-start.3 = (bf16[2,4,16,768]{3,2,1,0:T(8,128)(2,1)S(1)}, bf16[2,4,16,768]{3,2,1,0:T(8,128)(2,1)S(1)}, u32[]{:S(2)}, u32[]{:S(2)}) collective-permute-start(bf16[2,4,16,768]{3,2,1,0:T(8,128)(2,1)S(1)} %get-tuple-element.29), channel_id=1, source_target_pairs={{0,48},{16,32},{32,16},{48,0},{1,49},{17,33},{33,17},{49,1},{2,50}... | collective-permute-start | bytes 589832 | tf_op jit(solution)/shard_map/ppermute | solution.py:355
  23.8 0.2 collective-permute-start.1
  24.0 1.7 %collective-permute-start.2 = (bf16[2,4,16,768]{3,2,1,0:T(8,128)(2,1)S(1)}, bf16[2,4,16,768]{3,2,1,0:T(8,128)(2,1)S(1)}, u32[]{:S(2)}, u32[]{:S(2)}) collective-permute-start(bf16[2,4,16,768]{3,2,1,0:T(8,128)(2,1)S(1)} %get-tuple-element.32), channel_id=1, source_target_pairs={{0,32},{16,48},{32,0},{48,16},{1,33},{17,49},{33,1},{49,17},{2,34}... | collective-permute-start | bytes 589832 | tf_op jit(solution)/shard_map/ppermute | solution.py:355
  25.7 3.8 %collective-permute-done.3.x3 = bf16[2,4,16,768]{3,2,1,0:T(8,128)(2,1)S(1)} collective-permute-done((bf16[2,4,16,768]{3,2,1,0:T(8,128)(2,1)S(1)}, bf16[2,4,16,768]{3,2,1,0:T(8,128)(2,1)S(1)}, u32[]{:S(2)}, u32[]{:S(2)}) %collective-permute-start.3) | collective-permute-done | bytes 196640 | tf_op jit(solution)/shard_map/ppermute | solution.py:355
  29.5 0.0 copy-start.2
  29.6 1.6 %collective-permute-done.1.x1 = bf16[2,4,16,768]{3,2,1,0:T(8,128)(2,1)S(1)} collective-permute-done((bf16[2,4,16,768]{3,2,1,0:T(8,128)(2,1)S(1)}, bf16[2,4,16,768]{3,2,1,0:T(8,128)(2,1)S(1)}, u32[]{:S(2)}, u32[]{:S(2)}) %collective-permute-start.1) | collective-permute-done | bytes 196640 | tf_op jit(solution)/shard_map/ppermute | solution.py:355
  31.1 0.0 copy-start.3
  31.1 2.0 %collective-permute-done.2.x2 = bf16[2,4,16,768]{3,2,1,0:T(8,128)(2,1)S(1)} collective-permute-done((bf16[2,4,16,768]{3,2,1,0:T(8,128)(2,1)S(1)}, bf16[2,4,16,768]{3,2,1,0:T(8,128)(2,1)S(1)}, u32[]{:S(2)}, u32[]{:S(2)}) %collective-permute-start.2) | collective-permute-done | bytes 196640 | tf_op jit(solution)/shard_map/ppermute | solution.py:355
  33.1 0.0 copy-start.4
  33.1 15.3 %all-to-all-done.q_ref.k1_ref.v1_ref = bf16[8,1152,128]{2,1,0:T(8,128)(2,1)S(1)} async-done(((bf16[8,1152,128]{2,1,0:T(8,128)(2,1)}), bf16[8,1152,128]{2,1,0:T(8,128)(2,1)S(1)}, u32[]{:S(2)}, u32[]{:S(2)}) %all-to-all-start) | async-done | bytes 2359328 | tf_op jit(solution)/shard_map/all_to_all | solution.py:349
  48.5 0.1 slice.6
  48.5 0.1 collective-permute-start.4
  48.6 2.3 %collective-permute-done.4.k2_ref = bf16[8,384,128]{2,1,0:T(8,128)(2,1)S(1)} collective-permute-done((bf16[8,384,128]{2,1,0:T(8,128)(2,1)S(1)}, bf16[8,384,128]{2,1,0:T(8,128)(2,1)S(1)}, u32[]{:S(2)}, u32[]{:S(2)}) %collective-permute-start.4) | collective-permute-done | bytes 786464 | tf_op jit(solution)/shard_map/ppermute | solution.py:357
  50.9 0.9 scores.1
  51.8 0.0 copy-done.2
  51.8 0.0 copy-done.3
  51.8 0.0 copy-done.4
  51.8 0.1 slice.7
  51.9 0.2 collective-permute-start.5
  52.1 21.2 %all_to_all.25.parts_ref = bf16[16,3,16,512]{3,2,1,0:T(8,128)(2,1)S(1)} all-to-all(bf16[16,3,16,512]{3,2,1,0:T(8,128)(2,1)S(1)} %scores.1), channel_id=1, replica_groups=mesh['y_lo'=2,'x'=4,'y_hi'=2,'z'=4,'core'=2] {'y_lo','x','y_hi'}, dimensions={0} | all-to-all | bytes 1572864 | tf_op jit(solution)/shard_map/all_to_all | solution.py:359
  73.3 0.0 collective-permute-done.5.v2_ref
  73.3 0.3 softmax.1
  73.6 17.1 %all_to_all.26.w_ref = bf16[16,3,16,512]{3,2,1,0:T(8,128)(2,1)S(1)} all-to-all(bf16[16,3,16,512]{3,2,1,0:T(8,128)(2,1)S(1)} %softmax.1), channel_id=1, replica_groups=mesh['y_lo'=2,'x'=4,'y_hi'=2,'z'=4,'core'=2] {'y_lo','x','y_hi'}, dimensions={0} | all-to-all | bytes 1572864 | tf_op jit(solution)/shard_map/all_to_all | solution.py:362
  90.6 2.0 %attend.1 = bf16[64,48,128]{2,1,0:T(8,128)(2,1)} custom-call(bf16[16,3,16,512]{3,2,1,0:T(8,128)(2,1)S(1)} %all_to_all.26.w_ref, bf16[8,1152,128]{2,1,0:T(8,128)(2,1)S(1)} %all-to-all-done.q_ref.k1_ref.v1_ref, bf16[8,384,128]{2,1,0:T(8,128)(2,1)S(1)} %collective-permute-done.5.v2_ref), custom_call_target="tpu_custom_call" | custom-call | flops 671088640 | bytes 3145728 | tf_op jit(solution)/shard_map/attend/pallas_call | solution.py:211
  92.6 5.4 %all-to-all-start.3 = ((bf16[64,48,128]{2,1,0:T(8,128)(2,1)}), bf16[64,48,128]{2,1,0:T(8,128)(2,1)S(1)}, u32[]{:S(2)}, u32[]{:S(2)}) async-start(bf16[64,48,128]{2,1,0:T(8,128)(2,1)} %attend.1), calls=%async_computation.3 | async-start | bytes 1572864 | tf_op jit(solution)/shard_map/all_to_all | solution.py:363
  98.1 0.7 pad_add_fusion.me_ref
  98.7 13.6 %all-to-all-done.3 = bf16[64,48,128]{2,1,0:T(8,128)(2,1)S(1)} async-done(((bf16[64,48,128]{2,1,0:T(8,128)(2,1)}), bf16[64,48,128]{2,1,0:T(8,128)(2,1)S(1)}, u32[]{:S(2)}, u32[]{:S(2)}) %all-to-all-start.3) | async-done | bytes 786464 | tf_op jit(solution)/shard_map/all_to_all | solution.py:363
  112.3 0.0 copy-start
  112.3 0.9 copy-done
  113.2 14.9 %columns.1 = bf16[8,4,16,768]{3,2,1,0:T(8,128)(2,1)} custom-call(s32[2]{0:T(128)} %pad_add_fusion.me_ref, bf16[16,4,48,128]{3,2,1,0:T(8,128)(2,1)} %bitcast.32, bf16[2,4,16,768]{3,2,1,0:T(8,128)(2,1)} %get-tuple-element.25.x0, bf16[2,4,16,768]{3,2,1,0:T(8,128)(2,1)} %copy-done.3, bf16[2,4,16,768]{3,2,1,0:T(8,128)(2,1)} %copy-done.4, ...), custom_call_target="tpu_custom_call" | custom-call | flops 8000000000 | bytes 18874368 | tf_op jit(solution)/shard_map/columns/pallas_call | solution.py:316
  128.1 13.7 %all_to_all.27 = bf16[8,4,16,768]{3,2,1,0:T(8,128)(2,1)S(1)} all-to-all(bf16[8,4,16,768]{3,2,1,0:T(8,128)(2,1)} %columns.1), channel_id=1, replica_groups=mesh['y_lo'=2,'x'=4,'y_hi'=2,'z'=4,'core'=2] {'y_lo','x'}, dimensions={0} | all-to-all | bytes 1572864 | tf_op jit(solution)/shard_map/all_to_all | solution.py:367
  141.8 1.1 copy.10
  (1 shorter events, 0.0 us)
Async XLA Ops:
  1.2 10.9 %collective-permute-start = (bf16[16,16,768]{2,0,1:T(8,128)(2,1)S(1)}, bf16[16,16,768]{2,0,1:T(8,128)(2,1)S(1)}, u32[]{:S(2)}, u32[]{:S(2)}) collective-permute-start(bf16[16,16,768]{2,0,1:T(8,128)(2,1)S(1)} %bitcast.36), channel_id=1, source_target_pairs={{0,64},{64,0},{1,65},{65,1},{2,66},{66,2},{3,67},{67,3},{4,68},{68... | collective-permute-start | bytes 1179656 | tf_op jit(solution)/shard_map/ppermute | solution.py:347
  8.5 11.7 %copy-start.1 = (bf16[16,32,768]{2,1,0:T(8,128)(2,1)S(1)}, bf16[16,32,768]{2,1,0:T(8,128)(2,1)}, u32[]{:S(2)}) copy-start(bf16[16,32,768]{2,1,0:T(8,128)(2,1)} %param.7) | copy-start | bytes 2359300
  12.0 36.5 %all-to-all-start = ((bf16[8,1152,128]{2,1,0:T(8,128)(2,1)}), bf16[8,1152,128]{2,1,0:T(8,128)(2,1)S(1)}, u32[]{:S(2)}, u32[]{:S(2)}) async-start(bf16[8,1152,128]{2,1,0:T(8,128)(2,1)} %project.1), calls=%async_computation | async-start | bytes 4718592 | tf_op jit(solution)/shard_map/all_to_all | solution.py:349
  21.0 8.5 %collective-permute-start.3 = (bf16[2,4,16,768]{3,2,1,0:T(8,128)(2,1)S(1)}, bf16[2,4,16,768]{3,2,1,0:T(8,128)(2,1)S(1)}, u32[]{:S(2)}, u32[]{:S(2)}) collective-permute-start(bf16[2,4,16,768]{3,2,1,0:T(8,128)(2,1)S(1)} %get-tuple-element.29), channel_id=1, source_target_pairs={{0,48},{16,32},{32,16},{48,0},{1,49},{17,33},{33,17},{49,1},{2,50}... | collective-permute-start | bytes 589832 | tf_op jit(solution)/shard_map/ppermute | solution.py:355
  23.8 7.3 %collective-permute-start.1 = (bf16[2,4,16,768]{3,2,1,0:T(8,128)(2,1)S(1)}, bf16[2,4,16,768]{3,2,1,0:T(8,128)(2,1)S(1)}, u32[]{:S(2)}, u32[]{:S(2)}) collective-permute-start(bf16[2,4,16,768]{3,2,1,0:T(8,128)(2,1)S(1)} %get-tuple-element.31), channel_id=1, source_target_pairs={{0,16},{16,0},{32,48},{48,32},{1,17},{17,1},{33,49},{49,33},{2,18}... | collective-permute-start | bytes 589832 | tf_op jit(solution)/shard_map/ppermute | solution.py:355
  24.0 9.1 %collective-permute-start.2 = (bf16[2,4,16,768]{3,2,1,0:T(8,128)(2,1)S(1)}, bf16[2,4,16,768]{3,2,1,0:T(8,128)(2,1)S(1)}, u32[]{:S(2)}, u32[]{:S(2)}) collective-permute-start(bf16[2,4,16,768]{3,2,1,0:T(8,128)(2,1)S(1)} %get-tuple-element.32), channel_id=1, source_target_pairs={{0,32},{16,48},{32,0},{48,16},{1,33},{17,49},{33,1},{49,17},{2,34}... | collective-permute-start | bytes 589832 | tf_op jit(solution)/shard_map/ppermute | solution.py:355
  29.5 22.2 %copy-start.2 = (bf16[2,4,16,768]{3,2,1,0:T(8,128)(2,1)}, bf16[2,4,16,768]{3,2,1,0:T(8,128)(2,1)S(1)}, u32[]{:S(2)}) copy-start(bf16[2,4,16,768]{3,2,1,0:T(8,128)(2,1)S(1)} %collective-permute-done.3.x3) | copy-start | bytes 589828
  31.1 20.7 %copy-start.3 = (bf16[2,4,16,768]{3,2,1,0:T(8,128)(2,1)}, bf16[2,4,16,768]{3,2,1,0:T(8,128)(2,1)S(1)}, u32[]{:S(2)}) copy-start(bf16[2,4,16,768]{3,2,1,0:T(8,128)(2,1)S(1)} %collective-permute-done.1.x1) | copy-start | bytes 589828
  33.1 18.7 %copy-start.4 = (bf16[2,4,16,768]{3,2,1,0:T(8,128)(2,1)}, bf16[2,4,16,768]{3,2,1,0:T(8,128)(2,1)S(1)}, u32[]{:S(2)}) copy-start(bf16[2,4,16,768]{3,2,1,0:T(8,128)(2,1)S(1)} %collective-permute-done.2.x2) | copy-start | bytes 589828
  48.5 2.4 %collective-permute-start.4 = (bf16[8,384,128]{2,1,0:T(8,128)(2,1)S(1)}, bf16[8,384,128]{2,1,0:T(8,128)(2,1)S(1)}, u32[]{:S(2)}, u32[]{:S(2)}) collective-permute-start(bf16[8,384,128]{2,1,0:T(8,128)(2,1)S(1)} %slice.6), channel_id=1, source_target_pairs={{0,1},{1,0},{2,3},{3,2},{4,5},{5,4},{6,7},{7,6},{8,9},{9,8},{10,11... | collective-permute-start | bytes 2359304 | tf_op jit(solution)/shard_map/ppermute | solution.py:357
  51.9 21.4 %collective-permute-start.5 = (bf16[8,384,128]{2,1,0:T(8,128)(2,1)S(1)}, bf16[8,384,128]{2,1,0:T(8,128)(2,1)S(1)}, u32[]{:S(2)}, u32[]{:S(2)}) collective-permute-start(bf16[8,384,128]{2,1,0:T(8,128)(2,1)S(1)} %slice.7), channel_id=1, source_target_pairs={{0,1},{1,0},{2,3},{3,2},{4,5},{5,4},{6,7},{7,6},{8,9},{9,8},{10,11... | collective-permute-start | bytes 2359304 | tf_op jit(solution)/shard_map/ppermute | solution.py:360
  92.6 19.6 %all-to-all-start.3 = ((bf16[64,48,128]{2,1,0:T(8,128)(2,1)}), bf16[64,48,128]{2,1,0:T(8,128)(2,1)S(1)}, u32[]{:S(2)}, u32[]{:S(2)}) async-start(bf16[64,48,128]{2,1,0:T(8,128)(2,1)} %attend.1), calls=%async_computation.3 | async-start | bytes 1572864 | tf_op jit(solution)/shard_map/all_to_all | solution.py:363
  112.3 0.9 copy-start

commit v4 on v3

--- a/solution.py
+++ b/solution.py
@@ -228,16 +228,12 @@
 
 
 def columns_kernel(
-    me_ref, att_hbm, x0, x1, x2, x3, wo_hbm, wqkv_hbm, wco_hbm, w1_hbm, w2_hbm, out_ref,
-    att_ref, wo, wqkv, wco, w1, w2, att, x_in, state, col, sems,
+    me_ref, att_ref, x0, x1, x2, x3, wo, wqkv, wco, w1, w2, out_ref,
+    att, x_in, state, col, sems,
 ):
     def copy(src, dst, sem):
         return pltpu.make_async_copy(src, dst, sems.at[sem])
 
-    get_att = copy(att_hbm, att_ref, 0)
-    get_att.start()
-    get_wo = copy(wo_hbm, wo, 1)
-    get_wo.start()
     get_x = []
     for k, block in enumerate((x0, x1, x2, x3)):
         for side in range(2):
@@ -245,12 +241,6 @@
             at = pl.multiple_of((y * 4 + (me_ref[1] ^ k)) * 16, 16)
             get_x.append(copy(block.at[side], x_in.at[:, pl.ds(at, 16), :], 2 + 2 * k + side))
             get_x[-1].start()
-    get_wqkv = copy(wqkv_hbm, wqkv, 10)
-    get_wqkv.start()
-    get_wco = copy(wco_hbm, wco, 11)
-    get_w1 = copy(w1_hbm, w1, 12)
-    get_w2 = copy(w2_hbm, w2, 13)
-    get_att.wait()
     low = low_lanes((128, 128))
     for z in range(4):
         whole = att_ref[:, z, 0:32, :].astype(F32).reshape(16, 4, 8, 128)
@@ -270,16 +260,11 @@
             tile = jnp.where(low, first, second).astype(BF)
             at = HALF[2 * p] * 128
             att[i * 128 : i * 128 + 128, at : at + 128] = tile
-    get_wo.wait()
     for block in get_x:
         block.wait()
     after_rows = (x_in[...].reshape(512, D).astype(F32) + dot32(att[...], wo[...])).astype(BF)
     state[...] = after_rows
     normed = normalize(after_rows.astype(F32))
-    get_wqkv.wait()
-    get_wco.start()
-    get_w1.start()
-    get_w2.start()
     for t in range(3):
         col[:, t * D : t * D + D] = dot32(normed, wqkv[:, t * D : t * D + D]).astype(BF)
     zero = jnp.zeros((128, 128), BF)
@@ -295,12 +280,9 @@
             w = (e / jnp.sum(e, axis=-1, keepdims=True)).astype(BF)
             o = dot32(w, v)
             att[rows, t * 128 : t * 128 + 128] = jnp.where(low, o[:128], o[128:]).astype(BF)
-    get_wco.wait()
     after_cols = (state[...].astype(F32) + dot32(att[...], wco[...])).astype(BF)
     state[...] = after_cols
     normed = normalize(after_cols.astype(F32))
-    get_w1.wait()
-    get_w2.wait()
     total = after_cols.astype(F32)
     for t in range(4):
         hidden = jax.nn.gelu(dot32(normed, w1[:, t * D : t * D + D])).astype(BF)
@@ -315,23 +297,19 @@
     anywhere = pl.BlockSpec(memory_space=pl.ANY)
     return pl.pallas_call(
         columns_kernel,
-        in_specs=[pl.BlockSpec(memory_space=pltpu.SMEM)] + [anywhere] * 10,
+        in_specs=[pl.BlockSpec(memory_space=pltpu.SMEM), vmem]
+        + [anywhere] * 4
+        + [vmem] * 5,
         out_specs=vmem,
         out_shape=jax.ShapeDtypeStruct((8, 4, 16, D), BF),
         scratch_shapes=[
-            pltpu.VMEM((16, 4, 48, 128), BF),
-            pltpu.VMEM((D, D), BF),
-            pltpu.VMEM((D, 3 * D), BF),
-            pltpu.VMEM((D, D), BF),
-            pltpu.VMEM((D, FF), BF),
-            pltpu.VMEM((FF, D), BF),
             pltpu.VMEM((512, D), BF),
             pltpu.VMEM((4, 128, D), BF),
             pltpu.VMEM((512, D), BF),
             pltpu.VMEM((512, 3 * D), BF),
-            pltpu.SemaphoreType.DMA((14,)),
+            pltpu.SemaphoreType.DMA((11,)),
         ],
-        compiler_params=params(60),
+        compiler_params=params(24),
         cost_estimate=pl.CostEstimate(
             flops=8 * 10**9, bytes_accessed=18 * MIB, transcendentals=3 * MIB
         ),
@@ -345,7 +323,8 @@
     y_me, x_me = lax.axis_index("y_lo"), lax.axis_index("x")
     halves = x.reshape(16, 2, 16, D)
     far = lax.ppermute(lax.dynamic_index_in_dim(halves, 1 - y_me, 1, False), "y_lo", swap)
-    proj, x, far = barrier((project(x.reshape(512, D), row_qkv), x, far))
+    me = jnp.stack([y_me, x_me]).astype(jnp.int32)
+    proj, x, far, me = barrier((project(x.reshape(512, D), row_qkv), x, far, me))
     got = lax.all_to_all(proj, ("y_hi", "z"), 0, 0, tiled=True)
     mine = lax.dynamic_index_in_dim(x.reshape(16, 2, 16, D), y_me, 1, False)
     x_cols = jnp.stack([mine, far]).reshape(2, 16, 4, 4, D).transpose(2, 0, 3, 1, 4)
@@ -362,7 +341,6 @@
     shares = lax.all_to_all(softmax(parts), PLANE, 0, 0, tiled=True)
     att = lax.all_to_all(attend(shares, got, v2), CHIPS, 0, 0, tiled=True)
     att = att.reshape(16, 4, 48, 128)
-    me = jnp.stack([y_me, x_me]).astype(jnp.int32)
     out = columns(me, att, near, row_out, col_qkv, col_out, ff_in, ff_out)
     out = lax.all_to_all(out, SEQ, 0, 0, tiled=True)
     return out.transpose(2, 0, 1, 3).reshape(16, 32, D)

time: 143 us -> 138 us (0.965)
  blocking collectives: 52 us -> 71.1 us
  waiting for transfers between devices: 42.1 us -> 29 us
  starting transfers between devices: 20.3 us -> 14.9 us
  Pallas kernels: 23.6 us -> 20.2 us
    all_to_all x0 -> x1, blocking collectives: none -> 19.6 us  [per_device(): att = lax.all_to_all(attend(shares, got, v2), CHIPS, 0, 0, tiled=True)]
    all_to_all x1 -> x0, waiting for transfers between devices: 13.6 us -> none  [per_device(): att = lax.all_to_all(attend(shares, got, v2), CHIPS, 0, 0, tiled=True)]
    all_to_all x1 -> x0, starting transfers between devices: 5.41 us -> none  [per_device(): att = lax.all_to_all(attend(shares, got, v2), CHIPS, 0, 0, tiled=True)]
    pallas_call x1, Pallas kernels: 14.9 us -> 12.3 us  [columns(): pl.pallas_call(columns_kernel, in_specs=[pl.BlockSpec(memory_space=pltpu....]
  transfers between devices with their start and end apart: 8 -> 7, of which waited for: 7 -> 6; matrix products, arithmetic and copies ran while one was open for 1% -> 0% of each run, Pallas kernels for 4% -> 4%
where the time goes in v4:
time: 138 us
  blocking collectives  71.1 us (52%)
  waiting for transfers between devices  29 us (21%)
  Pallas kernels  20.2 us (15%)
  starting transfers between devices  14.9 us (11%)
  local copies, waits for them, and re-layouts  2.55 us (2%)
    all_to_all x1, blocking collectives, per_device(): parts = lax.all_to_all(parts, PLANE, 0, 0, tiled=True)  21.4 us
    all_to_all x1, blocking collectives, per_device(): att = lax.all_to_all(attend(shares, got, v2), CHIPS, 0, 0, tiled=True)  19.6 us
    all_to_all x1, blocking collectives, per_device(): shares = lax.all_to_all(softmax(parts), PLANE, 0, 0, tiled=True)  17.2 us
    all_to_all x1, waiting for transfers between devices, per_device(): got = lax.all_to_all(proj, ('y_hi', 'z'), 0, 0, tiled=True)  15.9 us
    all_to_all x1, blocking collectives, per_device(): out = lax.all_to_all(out, SEQ, 0, 0, tiled=True)  12.9 us
    pallas_call x1, Pallas kernels, columns(): pl.pallas_call(columns_kernel, in_specs=[pl.BlockSpec(memory_space=pltpu....  12.3 us
    all_to_all x1, starting transfers between devices, per_device(): got = lax.all_to_all(proj, ('y_hi', 'z'), 0, 0, tiled=True)  8.11 us
    ppermute x3, waiting for transfers between devices, per_device(): lax.ppermute(block, 'x', [(i, i ^ k) for i in range(4)])  7.4 us
  transfers between devices with their start and end apart: 7, of which 6 were waited for; matrix products, arithmetic and copies ran while one was open for 0% of the time, Pallas kernels for 4%

profile of v4, /device:TPU:0, one launch (start us, length us, event | category | flops | bytes accessed | tf_op | source)
XLA Modules:
  0.0 138.1 jit_solution(11063423670757870888)
XLA Ops:
  0.0 1.0 constant_dynamic-slice_fusion.1
  1.0 0.1 copy.13
  1.2 1.7 %collective-permute-start = (bf16[16,16,768]{2,0,1:T(8,128)(2,1)S(1)}, bf16[16,16,768]{2,0,1:T(8,128)(2,1)S(1)}, u32[]{:S(2)}, u32[]{:S(2)}) collective-permute-start(bf16[16,16,768]{2,0,1:T(8,128)(2,1)S(1)} %bitcast.40), channel_id=1, source_target_pairs={{0,64},{64,0},{1,65},{65,1},{2,66},{66,2},{3,67},{67,3},{4,68},{68... | collective-permute-start | bytes 1179656 | tf_op jit(solution)/shard_map/ppermute | solution.py:325
  2.9 0.1 pad_add_fusion.me_ref
  3.0 5.6 %project.1 = bf16[8,1152,128]{2,1,0:T(8,128)(2,1)} custom-call(bf16[512,768]{1,0:T(8,128)(2,1)} %bitcast.38, bf16[768,2304]{1,0:T(8,128)(2,1)} %w_hbm.1), custom_call_target="tpu_custom_call" | custom-call | flops 1811939328 | bytes 6291456 | tf_op jit(solution)/shard_map/project/pallas_call | solution.py:95
  8.5 0.0 copy-start.3
  8.6 3.5 %collective-permute-done = bf16[16,16,768]{2,0,1:T(8,128)(2,1)S(1)} collective-permute-done((bf16[16,16,768]{2,0,1:T(8,128)(2,1)S(1)}, bf16[16,16,768]{2,0,1:T(8,128)(2,1)S(1)}, u32[]{:S(2)}, u32[]{:S(2)}) %collective-permute-start) | collective-permute-done | bytes 393248 | tf_op jit(solution)/shard_map/ppermute | solution.py:325
  12.0 8.1 %all-to-all-start = ((bf16[8,1152,128]{2,1,0:T(8,128)(2,1)}), bf16[8,1152,128]{2,1,0:T(8,128)(2,1)S(1)}, u32[]{:S(2)}, u32[]{:S(2)}) async-start(bf16[8,1152,128]{2,1,0:T(8,128)(2,1)} %project.1), calls=%async_computation | async-start | bytes 4718592 | tf_op jit(solution)/shard_map/all_to_all | solution.py:328
  20.1 0.0 copy-done.3
  20.2 0.1 copy.11
  20.3 0.1 fusion.1
  20.4 2.8 %collective-permute-start.3 = (bf16[2,4,16,768]{3,2,1,0:T(8,128)(2,1)S(1)}, bf16[2,4,16,768]{3,2,1,0:T(8,128)(2,1)S(1)}, u32[]{:S(2)}, u32[]{:S(2)}) collective-permute-start(bf16[2,4,16,768]{3,2,1,0:T(8,128)(2,1)S(1)} %get-tuple-element.31), channel_id=1, source_target_pairs={{0,48},{16,32},{32,16},{48,0},{1,49},{17,33},{33,17},{49,1},{2,50}... | collective-permute-start | bytes 589832 | tf_op jit(solution)/shard_map/ppermute | solution.py:334
  23.2 0.2 collective-permute-start.1
  23.4 1.7 %collective-permute-start.2 = (bf16[2,4,16,768]{3,2,1,0:T(8,128)(2,1)S(1)}, bf16[2,4,16,768]{3,2,1,0:T(8,128)(2,1)S(1)}, u32[]{:S(2)}, u32[]{:S(2)}) collective-permute-start(bf16[2,4,16,768]{3,2,1,0:T(8,128)(2,1)S(1)} %get-tuple-element.34), channel_id=1, source_target_pairs={{0,32},{16,48},{32,0},{48,16},{1,33},{17,49},{33,1},{49,17},{2,34}... | collective-permute-start | bytes 589832 | tf_op jit(solution)/shard_map/ppermute | solution.py:334
  25.2 3.8 %collective-permute-done.3.x3 = bf16[2,4,16,768]{3,2,1,0:T(8,128)(2,1)S(1)} collective-permute-done((bf16[2,4,16,768]{3,2,1,0:T(8,128)(2,1)S(1)}, bf16[2,4,16,768]{3,2,1,0:T(8,128)(2,1)S(1)}, u32[]{:S(2)}, u32[]{:S(2)}) %collective-permute-start.3) | collective-permute-done | bytes 196640 | tf_op jit(solution)/shard_map/ppermute | solution.py:334
  29.0 1.6 %collective-permute-done.1.x1 = bf16[2,4,16,768]{3,2,1,0:T(8,128)(2,1)S(1)} collective-permute-done((bf16[2,4,16,768]{3,2,1,0:T(8,128)(2,1)S(1)}, bf16[2,4,16,768]{3,2,1,0:T(8,128)(2,1)S(1)}, u32[]{:S(2)}, u32[]{:S(2)}) %collective-permute-start.1) | collective-permute-done | bytes 196640 | tf_op jit(solution)/shard_map/ppermute | solution.py:334
  30.5 2.0 %collective-permute-done.2.x2 = bf16[2,4,16,768]{3,2,1,0:T(8,128)(2,1)S(1)} collective-permute-done((bf16[2,4,16,768]{3,2,1,0:T(8,128)(2,1)S(1)}, bf16[2,4,16,768]{3,2,1,0:T(8,128)(2,1)S(1)}, u32[]{:S(2)}, u32[]{:S(2)}) %collective-permute-start.2) | collective-permute-done | bytes 196640 | tf_op jit(solution)/shard_map/ppermute | solution.py:334
  32.6 15.9 %all-to-all-done.q_ref.k1_ref.v1_ref = bf16[8,1152,128]{2,1,0:T(8,128)(2,1)S(1)} async-done(((bf16[8,1152,128]{2,1,0:T(8,128)(2,1)}), bf16[8,1152,128]{2,1,0:T(8,128)(2,1)S(1)}, u32[]{:S(2)}, u32[]{:S(2)}) %all-to-all-start) | async-done | bytes 2359328 | tf_op jit(solution)/shard_map/all_to_all | solution.py:328
  48.5 0.1 slice.6
  48.5 0.1 collective-permute-start.4
  48.6 2.3 %collective-permute-done.4.k2_ref = bf16[8,384,128]{2,1,0:T(8,128)(2,1)S(1)} collective-permute-done((bf16[8,384,128]{2,1,0:T(8,128)(2,1)S(1)}, bf16[8,384,128]{2,1,0:T(8,128)(2,1)S(1)}, u32[]{:S(2)}, u32[]{:S(2)}) %collective-permute-start.4) | collective-permute-done | bytes 786464 | tf_op jit(solution)/shard_map/ppermute | solution.py:336
  50.9 0.0 slice-start
  50.9 0.0 slice-start.2
  50.9 0.9 scores.1
  51.8 0.1 slice.7
  51.9 0.2 collective-permute-start.5
  52.1 21.4 %all_to_all.25.parts_ref = bf16[16,3,16,512]{3,2,1,0:T(8,128)(2,1)S(1)} all-to-all(bf16[16,3,16,512]{3,2,1,0:T(8,128)(2,1)S(1)} %scores.1), channel_id=1, replica_groups=mesh['y_lo'=2,'x'=4,'y_hi'=2,'z'=4,'core'=2] {'y_lo','x','y_hi'}, dimensions={0} | all-to-all | bytes 1572864 | tf_op jit(solution)/shard_map/all_to_all | solution.py:338
  73.5 0.0 slice-start.1
  73.5 0.0 slice-start.3
  73.5 0.0 collective-permute-done.5.v2_ref
  73.5 0.3 softmax.1
  73.8 17.2 %all_to_all.26.w_ref = bf16[16,3,16,512]{3,2,1,0:T(8,128)(2,1)S(1)} all-to-all(bf16[16,3,16,512]{3,2,1,0:T(8,128)(2,1)S(1)} %softmax.1), channel_id=1, replica_groups=mesh['y_lo'=2,'x'=4,'y_hi'=2,'z'=4,'core'=2] {'y_lo','x','y_hi'}, dimensions={0} | all-to-all | bytes 1572864 | tf_op jit(solution)/shard_map/all_to_all | solution.py:341
  91.0 0.0 copy-start
  91.0 0.0 copy-start.1
  91.0 0.0 copy-start.2
  91.0 1.2 attend.1
  92.2 19.6 %all_to_all.27 = bf16[64,48,128]{2,1,0:T(8,128)(2,1)S(1)} all-to-all(bf16[64,48,128]{2,1,0:T(8,128)(2,1)S(1)} %attend.1), channel_id=1, replica_groups=mesh['y_lo'=2,'x'=4,'y_hi'=2,'z'=4,'core'=2] {'y_lo','x','y_hi','z'}, dimensions={0} | all-to-all | bytes 1572864 | tf_op jit(solution)/shard_map/all_to_all | solution.py:342
  111.8 0.0 slice-done
  111.8 0.0 slice-done.2
  111.8 0.0 slice-done.1
  111.8 0.0 slice-done.3
  111.8 0.0 copy-done
  111.8 0.0 copy-done.1
  111.8 0.0 copy-done.2
  111.8 12.3 %columns.1 = bf16[8,4,16,768]{3,2,1,0:T(8,128)(2,1)S(1)} custom-call(s32[2]{0:T(128)S(1)} %pad_add_fusion.me_ref, bf16[16,4,48,128]{3,2,1,0:T(8,128)(2,1)S(1)} %bitcast.30, bf16[2,4,16,768]{3,2,1,0:T(8,128)(2,1)S(1)} %get-tuple-element.27.x0, bf16[2,4,16,768]{3,2,1,0:T(8,128)(2,1)S(1)} %collective-permute-done.1.x1, ...), custom_call_target="tpu_custom_call" | custom-call | flops 8000000000 | bytes 18874368 | tf_op jit(solution)/shard_map/columns/pallas_call | solution.py:298
  124.1 12.9 %all_to_all.28 = bf16[8,4,16,768]{3,2,1,0:T(8,128)(2,1)S(1)} all-to-all(bf16[8,4,16,768]{3,2,1,0:T(8,128)(2,1)S(1)} %columns.1), channel_id=1, replica_groups=mesh['y_lo'=2,'x'=4,'y_hi'=2,'z'=4,'core'=2] {'y_lo','x'}, dimensions={0} | all-to-all | bytes 1572864 | tf_op jit(solution)/shard_map/all_to_all | solution.py:345
  137.0 1.1 copy.10
  (3 shorter events, 0.0 us)
Async XLA Ops:
  1.2 10.9 %collective-permute-start = (bf16[16,16,768]{2,0,1:T(8,128)(2,1)S(1)}, bf16[16,16,768]{2,0,1:T(8,128)(2,1)S(1)}, u32[]{:S(2)}, u32[]{:S(2)}) collective-permute-start(bf16[16,16,768]{2,0,1:T(8,128)(2,1)S(1)} %bitcast.40), channel_id=1, source_target_pairs={{0,64},{64,0},{1,65},{65,1},{2,66},{66,2},{3,67},{67,3},{4,68},{68... | collective-permute-start | bytes 1179656 | tf_op jit(solution)/shard_map/ppermute | solution.py:325
  8.5 11.6 %copy-start.3 = (bf16[16,32,768]{2,1,0:T(8,128)(2,1)S(1)}, bf16[16,32,768]{2,1,0:T(8,128)(2,1)}, u32[]{:S(2)}) copy-start(bf16[16,32,768]{2,1,0:T(8,128)(2,1)} %param.7) | copy-start | bytes 2359300
  12.0 36.5 %all-to-all-start = ((bf16[8,1152,128]{2,1,0:T(8,128)(2,1)}), bf16[8,1152,128]{2,1,0:T(8,128)(2,1)S(1)}, u32[]{:S(2)}, u32[]{:S(2)}) async-start(bf16[8,1152,128]{2,1,0:T(8,128)(2,1)} %project.1), calls=%async_computation | async-start | bytes 4718592 | tf_op jit(solution)/shard_map/all_to_all | solution.py:328
  20.4 8.6 %collective-permute-start.3 = (bf16[2,4,16,768]{3,2,1,0:T(8,128)(2,1)S(1)}, bf16[2,4,16,768]{3,2,1,0:T(8,128)(2,1)S(1)}, u32[]{:S(2)}, u32[]{:S(2)}) collective-permute-start(bf16[2,4,16,768]{3,2,1,0:T(8,128)(2,1)S(1)} %get-tuple-element.31), channel_id=1, source_target_pairs={{0,48},{16,32},{32,16},{48,0},{1,49},{17,33},{33,17},{49,1},{2,50}... | collective-permute-start | bytes 589832 | tf_op jit(solution)/shard_map/ppermute | solution.py:334
  23.2 7.3 %collective-permute-start.1 = (bf16[2,4,16,768]{3,2,1,0:T(8,128)(2,1)S(1)}, bf16[2,4,16,768]{3,2,1,0:T(8,128)(2,1)S(1)}, u32[]{:S(2)}, u32[]{:S(2)}) collective-permute-start(bf16[2,4,16,768]{3,2,1,0:T(8,128)(2,1)S(1)} %get-tuple-element.33), channel_id=1, source_target_pairs={{0,16},{16,0},{32,48},{48,32},{1,17},{17,1},{33,49},{49,33},{2,18}... | collective-permute-start | bytes 589832 | tf_op jit(solution)/shard_map/ppermute | solution.py:334
  23.4 9.1 %collective-permute-start.2 = (bf16[2,4,16,768]{3,2,1,0:T(8,128)(2,1)S(1)}, bf16[2,4,16,768]{3,2,1,0:T(8,128)(2,1)S(1)}, u32[]{:S(2)}, u32[]{:S(2)}) collective-permute-start(bf16[2,4,16,768]{3,2,1,0:T(8,128)(2,1)S(1)} %get-tuple-element.34), channel_id=1, source_target_pairs={{0,32},{16,48},{32,0},{48,16},{1,33},{17,49},{33,1},{49,17},{2,34}... | collective-permute-start | bytes 589832 | tf_op jit(solution)/shard_map/ppermute | solution.py:334
  48.5 2.4 %collective-permute-start.4 = (bf16[8,384,128]{2,1,0:T(8,128)(2,1)S(1)}, bf16[8,384,128]{2,1,0:T(8,128)(2,1)S(1)}, u32[]{:S(2)}, u32[]{:S(2)}) collective-permute-start(bf16[8,384,128]{2,1,0:T(8,128)(2,1)S(1)} %slice.6), channel_id=1, source_target_pairs={{0,1},{1,0},{2,3},{3,2},{4,5},{5,4},{6,7},{7,6},{8,9},{9,8},{10,11... | collective-permute-start | bytes 2359304 | tf_op jit(solution)/shard_map/ppermute | solution.py:336
  50.9 60.9 %slice-start = ((s8[4718592]{0:T(1024)(128)(4,1)}), s8[4194304]{0:T(1024)(128)(4,1)S(1)}, s32[]{:S(2)}) async-start(s8[4718592]{0:T(1024)(128)(4,1)} %bitcast.31), calls=%async_computation.5 | async-start | bytes 8388608
  50.9 60.9 %slice-start.2 = ((s8[4718592]{0:T(1024)(128)(4,1)}), s8[4194304]{0:T(1024)(128)(4,1)S(1)}, s32[]{:S(2)}) async-start(s8[4718592]{0:T(1024)(128)(4,1)} %bitcast.33), calls=%async_computation.7 | async-start | bytes 8388608
  51.9 21.6 %collective-permute-start.5 = (bf16[8,384,128]{2,1,0:T(8,128)(2,1)S(1)}, bf16[8,384,128]{2,1,0:T(8,128)(2,1)S(1)}, u32[]{:S(2)}, u32[]{:S(2)}) collective-permute-start(bf16[8,384,128]{2,1,0:T(8,128)(2,1)S(1)} %slice.7), channel_id=1, source_target_pairs={{0,1},{1,0},{2,3},{3,2},{4,5},{5,4},{6,7},{7,6},{8,9},{9,8},{10,11... | collective-permute-start | bytes 2359304 | tf_op jit(solution)/shard_map/ppermute | solution.py:339
  73.5 38.2 %slice-start.1 = ((s8[4718592]{0:T(1024)(128)(4,1)}), s8[524288]{0:T(1024)(128)(4,1)S(1)}, s32[]{:S(2)}) async-start(s8[4718592]{0:T(1024)(128)(4,1)} %bitcast.31), calls=%async_computation.6 | async-start | bytes 1048576
  73.5 38.2 %slice-start.3 = ((s8[4718592]{0:T(1024)(128)(4,1)}), s8[524288]{0:T(1024)(128)(4,1)S(1)}, s32[]{:S(2)}) async-start(s8[4718592]{0:T(1024)(128)(4,1)} %bitcast.33), calls=%async_computation.8 | async-start | bytes 1048576
  91.0 20.8 %copy-start = (bf16[768,2304]{1,0:T(8,128)(2,1)S(1)}, bf16[768,2304]{1,0:T(8,128)(2,1)}, u32[]{:S(2)}) copy-start(bf16[768,2304]{1,0:T(8,128)(2,1)} %wqkv.1) | copy-start | bytes 10616836
  91.0 20.8 %copy-start.1 = (bf16[768,768]{1,0:T(8,128)(2,1)S(1)}, bf16[768,768]{1,0:T(8,128)(2,1)}, u32[]{:S(2)}) copy-start(bf16[768,768]{1,0:T(8,128)(2,1)} %wo.1) | copy-start | bytes 3538948
  91.0 20.8 %copy-start.2 = (bf16[768,768]{1,0:T(8,128)(2,1)S(1)}, bf16[768,768]{1,0:T(8,128)(2,1)}, u32[]{:S(2)}) copy-start(bf16[768,768]{1,0:T(8,128)(2,1)} %wco.1) | copy-start | bytes 3538948

commit v5 on v4

v5 whole, which is shorter than its diff:
```python
import functools
import math

import jax
import jax.numpy as jnp
from jax import lax
from jax.experimental import pallas as pl
from jax.experimental.pallas import tpu as pltpu
from jax.sharding import Mesh, PartitionSpec as P

H = 12
DH = 64
D = H * DH
FF = 4 * D
ROWS = 128
SEQ = ("y_lo", "x")
CHIPS = ("y_lo", "x", "y_hi", "z")
BF = jnp.bfloat16
F32 = jnp.float32
MIB = 1 << 20

FULL = (0, 2, 3, 5)
HALF = (1, 1, 4, 4)

KEY, VALUE, QUERY = 0, 512, 1024


def dot32(a, b):
    return jnp.dot(a, b, preferred_element_type=F32)


def dot_t(a, b):
    return lax.dot_general(a, b, (((1,), (1,)), ((), ())), preferred_element_type=F32)


def swap_halves(v):
    return pltpu.roll(v, 64, 1)


def low_lanes(shape):
    return lax.broadcasted_iota(jnp.int32, shape, len(shape) - 1) % 128 < 64


def normalize(wide):
    centre = jnp.mean(wide, axis=-1, keepdims=True)
    off = wide - centre
    variance = jnp.mean(off * off, axis=-1, keepdims=True)
    return (off * lax.rsqrt(variance + 1e-05)).astype(BF)


def params(mib, **kw):
    return pltpu.CompilerParams(vmem_limit_bytes=mib * MIB, **kw)


def project_kernel(x_hbm, w_hbm, out_hbm, x_ref, w_ref, out_ref, sems):
    get_x = pltpu.make_async_copy(x_hbm, x_ref, sems.at[3])
    get_x.start()
    get_w = []
    for t in range(3):
        cols = slice(t * D, t * D + D)
        get_w.append(pltpu.make_async_copy(w_hbm.at[:, cols], w_ref.at[:, cols], sems.at[t]))
    get_w[0].start()
    get_x.wait()
    get_w[1].start()
    get_w[2].start()
    normed = normalize(x_ref[...].astype(F32))
    low = low_lanes((256, 128))
    put = []
    for t in range(3):
        get_w[t].wait()
        val = dot32(normed, w_ref[:, t * D : t * D + D])
        at = (QUERY, KEY, VALUE)[t]
        for tile in range(6):
            first = val[:256, tile * 128 : tile * 128 + 128]
            second = val[256:, tile * 128 : tile * 128 + 128]
            heads = (
                jnp.where(low, first, swap_halves(second)).astype(BF),
                jnp.where(low, swap_halves(first), second).astype(BF),
            )
            if tile in FULL:
                for y in range(2):
                    out_ref[y * 4 + FULL.index(tile), at : at + 256, :] = heads[y]
            else:
                for y in range(2):
                    for side in range(2):
                        z = HALF.index(tile) + side
                        if t > 0:
                            out_ref[y * 4 + z, at + 256 : at + 512, :] = heads[side]
                        else:
                            part = heads[side].reshape(8, 2, 16, 128)[:, y].reshape(128, 128)
                            out_ref[y * 4 + z, at + 256 : at + 384, :] = part
        part = pl.ds(at, 384 if t == 0 else 512)
        put.append(
            pltpu.make_async_copy(out_ref.at[:, part], out_hbm.at[:, part], sems.at[4 + t])
        )
        put[t].start()
    for t in range(3):
        put[t].wait()


def project(x, w):
    hbm = pl.BlockSpec(memory_space=pltpu.HBM)
    return pl.pallas_call(
        project_kernel,
        in_specs=[hbm, hbm],
        out_specs=hbm,
        out_shape=jax.ShapeDtypeStruct((8, 1408, 128), BF),
        scratch_shapes=[
            pltpu.VMEM((512, D), BF),
            pltpu.VMEM((D, 3 * D), BF),
            pltpu.VMEM((8, 1408, 128), BF),
            pltpu.SemaphoreType.DMA((7,)),
        ],
        compiler_params=params(58),
        cost_estimate=pl.CostEstimate(
            flops=2 * 512 * D * 3 * D, bytes_accessed=6 * MIB, transcendentals=0
        ),
        name="project",
    )(x, w)


def rows_of(ref, start, size=32):
    return ref[:, start : start + size, :].reshape(8 * size, 128)


def pair_of(refs, start):
    sides = [
        jnp.concatenate([rows_of(ref, at + start + 32 * n) for ref, at in refs], axis=0)
        for n in range(2)
    ]
    return jnp.concatenate(sides, axis=1)


def scores_kernel(got_ref, k2_ref, out_ref):
    for head, size in ((0, 32), (1, 16)):
        total = None
        keys = ((got_ref, KEY + head * 256), (k2_ref, head * 256))
        for r in range(0, 8, 2):
            at = QUERY + head * 256 + r * size
            q = jnp.concatenate(
                [rows_of(got_ref, at, size), rows_of(got_ref, at + size, size)], axis=1
            )
            part = dot_t(q, pair_of(keys, r * 32))
            total = part if total is None else total + part
        at = head * 32
        out_ref[:, at : at + size, :] = total.astype(BF).reshape(8, size, 512)


def scores(got, k2):
    vmem = pl.BlockSpec(memory_space=pltpu.VMEM)
    return pl.pallas_call(
        scores_kernel,
        in_specs=[vmem, vmem],
        out_specs=vmem,
        out_shape=jax.ShapeDtypeStruct((8, 48, 512), BF),
        compiler_params=params(12),
        cost_estimate=pl.CostEstimate(
            flops=2 * 384 * 512 * 1024, bytes_accessed=3 * MIB, transcendentals=0
        ),
        name="scores",
    )(got, k2)


def softmax_kernel(parts_ref, out_ref):
    total = parts_ref[0].astype(F32)
    for s in range(1, 8):
        total += parts_ref[s].astype(F32)
    total *= 1.0 / math.sqrt(DH * ROWS)
    e = jnp.exp(total - jnp.max(total, axis=-1, keepdims=True))
    w = (e / jnp.sum(e, axis=-1, keepdims=True)).astype(BF)
    for s in range(8):
        out_ref[s] = w


def softmax(parts):
    return pl.pallas_call(
        softmax_kernel,
        out_shape=jax.ShapeDtypeStruct((8, 48, 512), BF),
        compiler_params=params(6),
        cost_estimate=pl.CostEstimate(flops=MIB, bytes_accessed=MIB, transcendentals=24576),
        name="softmax",
    )(parts)


def attend_kernel(w_ref, got_ref, v2_ref, out_ref, whole, part):
    for head, size, dest in ((0, 32, whole), (1, 16, part)):
        at = head * 32
        w = w_ref[:, at : at + size, :].reshape(8 * size, 512)
        values = ((got_ref, VALUE + head * 256), (v2_ref, head * 256))
        for r in range(0, 8, 2):
            got = dot32(w, pair_of(values, r * 32))
            dest[pl.ds(r, 8 * size, stride=8), :] = got[:, :128]
            dest[pl.ds(r + 1, 8 * size, stride=8), :] = got[:, 128:]
    for a in range(8):
        for s in range(8):
            to = s * 8 + a
            at = (a * 32 + s * 2) * 8
            out_ref[to, 0:16, :] = whole[at : at + 16, :].astype(BF)
            out_ref[to, 16:32, :] = whole[at + 128 : at + 144, :].astype(BF)
            at = (a * 16 + s * 2) * 8
            out_ref[to, 32:48, :] = part[at : at + 16, :].astype(BF)


def attend(w, got, v2):
    vmem = pl.BlockSpec(memory_space=pltpu.VMEM)
    return pl.pallas_call(
        attend_kernel,
        in_specs=[vmem, vmem, vmem],
        out_specs=vmem,
        out_shape=jax.ShapeDtypeStruct((64, 48, 128), BF),
        scratch_shapes=[pltpu.VMEM((2048, 128), F32), pltpu.VMEM((1024, 128), F32)],
        compiler_params=params(12),
        cost_estimate=pl.CostEstimate(
            flops=2 * 384 * 512 * 1024, bytes_accessed=3 * MIB, transcendentals=0
        ),
        name="attend",
    )(w, got, v2)


def columns_kernel(
    me_ref, att_ref, x0, x1, x2, x3, wo, wqkv, wco, w1, w2, out_ref,
    att, x_in, state, col, sems,
):
    def copy(src, dst, sem):
        return pltpu.make_async_copy(src, dst, sems.at[sem])

    get_x = []
    for k, block in enumerate((x0, x1, x2, x3)):
        for side in range(2):
            y = me_ref[0] if side == 0 else 1 - me_ref[0]
            at = pl.multiple_of((y * 4 + (me_ref[1] ^ k)) * 16, 16)
            get_x.append(copy(block.at[side], x_in.at[:, pl.ds(at, 16), :], 2 + 2 * k + side))
            get_x[-1].start()
    low = low_lanes((8, 8, 128))

    def place(i, tile, first, second):
        top = jnp.where(low, first, pltpu.roll(second, 64, 2))
        bottom = jnp.where(low, pltpu.roll(first, 64, 2), second)
        both = jnp.concatenate([top, bottom], axis=1).reshape(128, 128).astype(BF)
        att[i * 128 : i * 128 + 128, tile * 128 : tile * 128 + 128] = both

    for z in range(4):
        for pair in range(2):
            first = att_ref[:, 0, z, pair * 16 : pair * 16 + 16, :].astype(F32)
            second = att_ref[:, 1, z, pair * 16 : pair * 16 + 16, :].astype(F32)
            for n in range(2):
                rows = slice(n * 8, n * 8 + 8)
                place(pair * 2 + n, FULL[z], first[:, rows], second[:, rows])
    for z in (0, 2):
        for y in range(2):
            first = att_ref[:, y, z, 32:48, :].astype(F32)
            second = att_ref[:, y, z + 1, 32:48, :].astype(F32)
            for n in range(2):
                rows = slice(n * 8, n * 8 + 8)
                place(y * 2 + n, HALF[z], first[:, rows], second[:, rows])
    low = low_lanes((128, 128))
    for block in get_x:
        block.wait()
    after_rows = (x_in[...].reshape(512, D).astype(F32) + dot32(att[...], wo[...])).astype(BF)
    state[...] = after_rows
    normed = normalize(after_rows.astype(F32))
    for t in range(3):
        col[:, t * D : t * D + D] = dot32(normed, wqkv[:, t * D : t * D + D]).astype(BF)
    zero = jnp.zeros((128, 128), BF)
    for i in range(4):
        rows = slice(i * 128, i * 128 + 128)
        for t in range(6):
            q = col[rows, t * 128 : t * 128 + 128]
            k = col[rows, D + t * 128 : D + t * 128 + 128]
            v = col[rows, 2 * D + t * 128 : 2 * D + t * 128 + 128]
            pair = jnp.concatenate([jnp.where(low, q, zero), jnp.where(low, zero, q)], axis=0)
            s = dot_t(pair, k) * (1.0 / math.sqrt(DH))
            e = jnp.exp(s - jnp.max(s, axis=-1, keepdims=True))
            w = (e / jnp.sum(e, axis=-1, keepdims=True)).astype(BF)
            o = dot32(w, v)
            att[rows, t * 128 : t * 128 + 128] = jnp.where(low, o[:128], o[128:]).astype(BF)
    after_cols = (state[...].astype(F32) + dot32(att[...], wco[...])).astype(BF)
    state[...] = after_cols
    normed = normalize(after_cols.astype(F32))
    total = after_cols.astype(F32)
    for t in range(4):
        hidden = jax.nn.gelu(dot32(normed, w1[:, t * D : t * D + D])).astype(BF)
        total += dot32(hidden, w2[t * D : t * D + D, :])
    out = total.astype(BF)
    for i in range(4):
        out_ref[:, i] = out[i * 128 : i * 128 + 128].reshape(8, 16, D)


def columns(me, att, x, wo, wqkv, wco, w1, w2):
    vmem = pl.BlockSpec(memory_space=pltpu.VMEM)
    anywhere = pl.BlockSpec(memory_space=pl.ANY)
    return pl.pallas_call(
        columns_kernel,
        in_specs=[pl.BlockSpec(memory_space=pltpu.SMEM), vmem]
        + [anywhere] * 4
        + [vmem] * 5,
        out_specs=vmem,
        out_shape=jax.ShapeDtypeStruct((8, 4, 16, D), BF),
        scratch_shapes=[
            pltpu.VMEM((512, D), BF),
            pltpu.VMEM((4, 128, D), BF),
            pltpu.VMEM((512, D), BF),
            pltpu.VMEM((512, 3 * D), BF),
            pltpu.SemaphoreType.DMA((11,)),
        ],
        compiler_params=params(24),
        cost_estimate=pl.CostEstimate(
            flops=8 * 10**9, bytes_accessed=18 * MIB, transcendentals=3 * MIB
        ),
        name="columns",
    )(me, att, *x, wo, wqkv, wco, w1, w2)


def per_device(x, row_qkv, row_out, col_qkv, col_out, ff_in, ff_out):
    barrier = lax.optimization_barrier
    swap = [(0, 1), (1, 0)]
    y_me, x_me = lax.axis_index("y_lo"), lax.axis_index("x")
    halves = x.reshape(16, 2, 2, 8, D)
    far = lax.ppermute(lax.dynamic_index_in_dim(halves, 1 - y_me, 2, False), "y_lo", swap)
    me = jnp.stack([y_me, x_me]).astype(jnp.int32)
    proj, x, far, me = barrier((project(x.reshape(512, D), row_qkv), x, far, me))
    got = lax.all_to_all(proj, ("y_hi", "z"), 0, 0, tiled=True)
    mine = lax.dynamic_index_in_dim(x.reshape(16, 2, 2, 8, D), y_me, 2, False)
    x_cols = jnp.stack([mine, far]).reshape(2, 16, 2, 4, 2, D)
    x_cols = x_cols.transpose(3, 0, 2, 4, 1, 5).reshape(4, 2, 4, 16, D)
    near = []
    for k in range(4):
        block = lax.dynamic_index_in_dim(x_cols, x_me ^ k, 0, False)
        near.append(lax.ppermute(block, "x", [(i, i ^ k) for i in range(4)]) if k else block)
    got, near = barrier((got, near))
    k2 = lax.ppermute(got[:, KEY : KEY + 512], "core", swap)
    parts, got = barrier((scores(got, k2), got))
    parts = lax.all_to_all(parts, SEQ, 0, 0, tiled=True)
    v2 = lax.ppermute(got[:, VALUE : VALUE + 512], "core", swap)
    parts, v2 = barrier((parts, v2))
    shares = lax.all_to_all(softmax(parts), SEQ, 0, 0, tiled=True)
    att = lax.all_to_all(attend(shares, got, v2), CHIPS, 0, 0, tiled=True)
    att = att.reshape(8, 2, 4, 48, 128)
    out = columns(me, att, near, row_out, col_qkv, col_out, ff_in, ff_out)
    out = lax.all_to_all(out, SEQ, 0, 0, tiled=True)
    return out.reshape(8, 2, 2, 16, D).transpose(3, 1, 0, 2, 4).reshape(16, 32, D)


def solution(mesh):
    fine = Mesh(mesh.devices.reshape(2, 4, 2, 4, 2), ("y_lo", "x", "y_hi", "z", "core"))
    tokens = P(SEQ, ("y_hi", "z", "core"), None)
    placed = (tokens, P(), P(), P(), P(), P(), P())
    return jax.shard_map(per_device, mesh=fine, in_specs=placed, out_specs=tokens, check_vma=False)
```

time: 138 us -> 132 us (0.957)
  blocking collectives: 71.1 us -> 58.3 us
  waiting for transfers between devices: 29 us -> 33.1 us
  local copies, waits for them, and re-layouts: 2.55 us -> 5.18 us
    all_to_all x2, blocking collectives: 38.6 us -> 24.7 us  [the longest x1 13.7 us: per_device(): parts = lax.all_to_all(parts, SEQ, 0, 0, tiled=True)]
    ppermute x3, waiting for transfers between devices: 7.4 us -> 9.47 us  [per_device(): lax.ppermute(block, 'x', [(i, i ^ k) for i in range(4)])]
    all_to_all x1, waiting for transfers between devices: 15.9 us -> 17.7 us  [per_device(): got = lax.all_to_all(proj, ('y_hi', 'z'), 0, 0, tiled=True)]
    all_to_all x1, blocking collectives: 19.6 us -> 21 us  [per_device(): att = lax.all_to_all(attend(shares, got, v2), CHIPS, 0, 0, tiled=True)]
  transfers between devices with their start and end apart: 7 -> 7, of which waited for: 6 -> 6; matrix products, arithmetic and copies ran while one was open for 0% -> 1% of each run, Pallas kernels for 4% -> 4%
where the time goes in v5:
time: 132 us
  blocking collectives  58.3 us (44%)
  waiting for transfers between devices  33.1 us (25%)
  Pallas kernels  19.7 us (15%)
  starting transfers between devices  14.9 us (11%)
  local copies, waits for them, and re-layouts  5.18 us (4%)
    all_to_all x1, blocking collectives, per_device(): att = lax.all_to_all(attend(shares, got, v2), CHIPS, 0, 0, tiled=True)  21 us
    all_to_all x1, waiting for transfers between devices, per_device(): got = lax.all_to_all(proj, ('y_hi', 'z'), 0, 0, tiled=True)  17.7 us
    all_to_all x1, blocking collectives, per_device(): parts = lax.all_to_all(parts, SEQ, 0, 0, tiled=True)  13.7 us
    all_to_all x1, blocking collectives, per_device(): out = lax.all_to_all(out, SEQ, 0, 0, tiled=True)  12.6 us
    pallas_call x1, Pallas kernels, columns(): pl.pallas_call(columns_kernel, in_specs=[pl.BlockSpec(memory_space=pltpu....  12.4 us
    all_to_all x1, blocking collectives, per_device(): shares = lax.all_to_all(softmax(parts), SEQ, 0, 0, tiled=True)  11 us
    ppermute x3, waiting for transfers between devices, per_device(): lax.ppermute(block, 'x', [(i, i ^ k) for i in range(4)])  9.47 us
    all_to_all x1, starting transfers between devices, per_device(): got = lax.all_to_all(proj, ('y_hi', 'z'), 0, 0, tiled=True)  8.11 us
  transfers between devices with their start and end apart: 7, of which 6 were waited for; matrix products, arithmetic and copies ran while one was open for 1% of the time, Pallas kernels for 4%

profile of v5, /device:TPU:0, one launch (start us, length us, event | category | flops | bytes accessed | tf_op | source)
XLA Modules:
  0.0 131.7 jit_solution(5269240804712534654)
XLA Ops:
  0.0 1.0 constant_dynamic-slice_fusion.1
  1.0 0.1 copy.17
  1.2 1.7 %collective-permute-start = (bf16[16,2,8,768]{3,0,2,1:T(8,128)(2,1)S(1)}, bf16[16,2,8,768]{3,0,2,1:T(8,128)(2,1)S(1)}, u32[]{:S(2)}, u32[]{:S(2)}) collective-permute-start(bf16[16,2,8,768]{3,0,2,1:T(8,128)(2,1)S(1)} %bitcast.36), channel_id=1, source_target_pairs={{0,64},{64,0},{1,65},{65,1},{2,66},{66,2},{3,67},{67,3},{4,68},{68... | collective-permute-start | bytes 1179656 | tf_op jit(solution)/shard_map/ppermute | solution.py:319
  2.9 0.1 pad_add_fusion.me_ref
  3.0 5.7 %project.1 = bf16[8,1408,128]{2,1,0:T(8,128)(2,1)} custom-call(bf16[512,768]{1,0:T(8,128)(2,1)} %bitcast.31, bf16[768,2304]{1,0:T(8,128)(2,1)} %w_hbm.1), custom_call_target="tpu_custom_call" | custom-call | flops 1811939328 | bytes 6291456 | tf_op jit(solution)/shard_map/project/pallas_call | solution.py:103
  8.6 3.4 %collective-permute-done = bf16[16,2,8,768]{3,0,2,1:T(8,128)(2,1)S(1)} collective-permute-done((bf16[16,2,8,768]{3,0,2,1:T(8,128)(2,1)S(1)}, bf16[16,2,8,768]{3,0,2,1:T(8,128)(2,1)S(1)}, u32[]{:S(2)}, u32[]{:S(2)}) %collective-permute-start) | collective-permute-done | bytes 393248 | tf_op jit(solution)/shard_map/ppermute | solution.py:319
  12.0 8.1 %all-to-all-start = ((bf16[8,1408,128]{2,1,0:T(8,128)(2,1)}), bf16[8,1408,128]{2,1,0:T(8,128)(2,1)S(1)}, u32[]{:S(2)}, u32[]{:S(2)}) async-start(bf16[8,1408,128]{2,1,0:T(8,128)(2,1)} %project.1), calls=%async_computation | async-start | bytes 5767168 | tf_op jit(solution)/shard_map/all_to_all | solution.py:322
  20.1 1.0 constant_dynamic-slice_fusion
  21.1 0.1 copy.12
  21.3 0.1 maximum_bitcast_fusion
  21.3 0.1 copy.13
  21.4 0.1 dynamic-slice_bitcast_fusion
  21.5 1.6 %collective-permute-start.1 = (bf16[2,4,16,768]{3,2,1,0:T(8,128)(2,1)S(1)}, bf16[2,4,16,768]{3,2,1,0:T(8,128)(2,1)S(1)}, u32[]{:S(2)}, u32[]{:S(2)}) collective-permute-start(bf16[2,4,16,768]{3,2,1,0:T(8,128)(2,1)S(1)} %get-tuple-element.33), channel_id=1, source_target_pairs={{0,16},{16,0},{32,48},{48,32},{1,17},{17,1},{33,49},{49,33},{2,18}... | collective-permute-start | bytes 589832 | tf_op jit(solution)/shard_map/ppermute | solution.py:329
  23.1 2.7 %collective-permute-start.2 = (bf16[2,4,16,768]{3,2,1,0:T(8,128)(2,1)S(1)}, bf16[2,4,16,768]{3,2,1,0:T(8,128)(2,1)S(1)}, u32[]{:S(2)}, u32[]{:S(2)}) collective-permute-start(bf16[2,4,16,768]{3,2,1,0:T(8,128)(2,1)S(1)} %get-tuple-element.32), channel_id=1, source_target_pairs={{0,32},{16,48},{32,0},{48,16},{1,33},{17,49},{33,1},{49,17},{2,34}... | collective-permute-start | bytes 589832 | tf_op jit(solution)/shard_map/ppermute | solution.py:329
  25.8 0.5 collective-permute-start.3
  26.3 2.9 %collective-permute-done.1.x1 = bf16[2,4,16,768]{3,2,1,0:T(8,128)(2,1)S(1)} collective-permute-done((bf16[2,4,16,768]{3,2,1,0:T(8,128)(2,1)S(1)}, bf16[2,4,16,768]{3,2,1,0:T(8,128)(2,1)S(1)}, u32[]{:S(2)}, u32[]{:S(2)}) %collective-permute-start.1) | collective-permute-done | bytes 196640 | tf_op jit(solution)/shard_map/ppermute | solution.py:329
  29.2 4.4 %collective-permute-done.2.x2 = bf16[2,4,16,768]{3,2,1,0:T(8,128)(2,1)S(1)} collective-permute-done((bf16[2,4,16,768]{3,2,1,0:T(8,128)(2,1)S(1)}, bf16[2,4,16,768]{3,2,1,0:T(8,128)(2,1)S(1)}, u32[]{:S(2)}, u32[]{:S(2)}) %collective-permute-start.2) | collective-permute-done | bytes 196640 | tf_op jit(solution)/shard_map/ppermute | solution.py:329
  33.6 2.2 %collective-permute-done.3.x3 = bf16[2,4,16,768]{3,2,1,0:T(8,128)(2,1)S(1)} collective-permute-done((bf16[2,4,16,768]{3,2,1,0:T(8,128)(2,1)S(1)}, bf16[2,4,16,768]{3,2,1,0:T(8,128)(2,1)S(1)}, u32[]{:S(2)}, u32[]{:S(2)}) %collective-permute-start.3) | collective-permute-done | bytes 196640 | tf_op jit(solution)/shard_map/ppermute | solution.py:329
  35.7 0.0 copy-start.3
  35.7 0.7 copy-done.3
  36.4 17.7 %all-to-all-done.got_ref = bf16[8,1408,128]{2,1,0:T(8,128)(2,1)S(1)} async-done(((bf16[8,1408,128]{2,1,0:T(8,128)(2,1)}), bf16[8,1408,128]{2,1,0:T(8,128)(2,1)S(1)}, u32[]{:S(2)}, u32[]{:S(2)}) %all-to-all-start) | async-done | bytes 2883616 | tf_op jit(solution)/shard_map/all_to_all | solution.py:322
  54.1 0.0 copy-start.4
  54.1 0.1 slice.6
  54.2 0.1 collective-permute-start.4
  54.3 2.6 %collective-permute-done.4.k2_ref = bf16[8,512,128]{2,1,0:T(8,128)(2,1)S(1)} collective-permute-done((bf16[8,512,128]{2,1,0:T(8,128)(2,1)S(1)}, bf16[8,512,128]{2,1,0:T(8,128)(2,1)S(1)}, u32[]{:S(2)}, u32[]{:S(2)}) %collective-permute-start.4) | collective-permute-done | bytes 1048608 | tf_op jit(solution)/shard_map/ppermute | solution.py:331
  56.9 0.0 slice-start
  56.9 0.0 slice-start.2
  56.9 0.7 scores.1
  57.7 0.1 slice.7
  57.7 0.2 collective-permute-start.5
  57.9 13.7 %all_to_all.25.parts_ref = bf16[8,48,512]{2,1,0:T(8,128)(2,1)S(1)} all-to-all(bf16[8,48,512]{2,1,0:T(8,128)(2,1)S(1)} %scores.1), channel_id=1, replica_groups=mesh['y_lo'=2,'x'=4,'y_hi'=2,'z'=4,'core'=2] {'y_lo','x'}, dimensions={0} | all-to-all | bytes 786432 | tf_op jit(solution)/shard_map/all_to_all | solution.py:333
  71.6 0.0 slice-start.1
  71.6 0.0 slice-start.3
  71.6 0.0 collective-permute-done.5.v2_ref
  71.6 0.2 softmax.1
  71.9 11.0 %all_to_all.26.w_ref = bf16[8,48,512]{2,1,0:T(8,128)(2,1)S(1)} all-to-all(bf16[8,48,512]{2,1,0:T(8,128)(2,1)S(1)} %softmax.1), channel_id=1, replica_groups=mesh['y_lo'=2,'x'=4,'y_hi'=2,'z'=4,'core'=2] {'y_lo','x'}, dimensions={0} | all-to-all | bytes 786432 | tf_op jit(solution)/shard_map/all_to_all | solution.py:336
  82.9 0.0 copy-start
  82.9 0.0 copy-start.1
  82.9 0.0 copy-start.2
  82.9 0.7 attend.1
  83.6 21.0 %all_to_all.27 = bf16[64,48,128]{2,1,0:T(8,128)(2,1)S(1)} all-to-all(bf16[64,48,128]{2,1,0:T(8,128)(2,1)S(1)} %attend.1), channel_id=1, replica_groups=mesh['y_lo'=2,'x'=4,'y_hi'=2,'z'=4,'core'=2] {'y_lo','x','y_hi','z'}, dimensions={0} | all-to-all | bytes 1572864 | tf_op jit(solution)/shard_map/all_to_all | solution.py:337
  104.7 0.0 copy-done.4
  104.7 0.0 slice-done
  104.7 0.0 slice-done.2
  104.7 0.0 slice-done.1
  104.7 0.0 slice-done.3
  104.7 0.0 copy-done
  104.7 0.0 copy-done.1
  104.7 0.0 copy-done.2
  104.7 12.4 %columns.1 = bf16[8,4,16,768]{3,2,1,0:T(8,128)(2,1)S(1)} custom-call(s32[2]{0:T(128)S(1)} %pad_add_fusion.me_ref, bf16[8,2,4,48,128]{4,3,2,1,0:T(8,128)(2,1)S(1)} %bitcast.25, bf16[2,4,16,768]{3,2,1,0:T(8,128)(2,1)S(1)} %get-tuple-element.27.x0, bf16[2,4,16,768]{3,2,1,0:T(8,128)(2,1)S(1)} %collective-permute-done.1.x1, ...), custom_call_target="tpu_custom_call" | custom-call | flops 8000000000 | bytes 18874368 | tf_op jit(solution)/shard_map/columns/pallas_call | solution.py:292
  117.1 12.6 %all_to_all.28 = bf16[8,4,16,768]{3,2,1,0:T(8,128)(2,1)S(1)} all-to-all(bf16[8,4,16,768]{3,2,1,0:T(8,128)(2,1)S(1)} %columns.1), channel_id=1, replica_groups=mesh['y_lo'=2,'x'=4,'y_hi'=2,'z'=4,'core'=2] {'y_lo','x'}, dimensions={0} | all-to-all | bytes 1572864 | tf_op jit(solution)/shard_map/all_to_all | solution.py:340
  129.7 0.8 copy.14
  130.5 1.2 reshape.33
  (2 shorter events, 0.0 us)
Async XLA Ops:
  1.2 10.9 %collective-permute-start = (bf16[16,2,8,768]{3,0,2,1:T(8,128)(2,1)S(1)}, bf16[16,2,8,768]{3,0,2,1:T(8,128)(2,1)S(1)}, u32[]{:S(2)}, u32[]{:S(2)}) collective-permute-start(bf16[16,2,8,768]{3,0,2,1:T(8,128)(2,1)S(1)} %bitcast.36), channel_id=1, source_target_pairs={{0,64},{64,0},{1,65},{65,1},{2,66},{66,2},{3,67},{67,3},{4,68},{68... | collective-permute-start | bytes 1179656 | tf_op jit(solution)/shard_map/ppermute | solution.py:319
  12.0 42.1 %all-to-all-start = ((bf16[8,1408,128]{2,1,0:T(8,128)(2,1)}), bf16[8,1408,128]{2,1,0:T(8,128)(2,1)S(1)}, u32[]{:S(2)}, u32[]{:S(2)}) async-start(bf16[8,1408,128]{2,1,0:T(8,128)(2,1)} %project.1), calls=%async_computation | async-start | bytes 5767168 | tf_op jit(solution)/shard_map/all_to_all | solution.py:322
  21.5 7.7 %collective-permute-start.1 = (bf16[2,4,16,768]{3,2,1,0:T(8,128)(2,1)S(1)}, bf16[2,4,16,768]{3,2,1,0:T(8,128)(2,1)S(1)}, u32[]{:S(2)}, u32[]{:S(2)}) collective-permute-start(bf16[2,4,16,768]{3,2,1,0:T(8,128)(2,1)S(1)} %get-tuple-element.33), channel_id=1, source_target_pairs={{0,16},{16,0},{32,48},{48,32},{1,17},{17,1},{33,49},{49,33},{2,18}... | collective-permute-start | bytes 589832 | tf_op jit(solution)/shard_map/ppermute | solution.py:329
  23.1 10.5 %collective-permute-start.2 = (bf16[2,4,16,768]{3,2,1,0:T(8,128)(2,1)S(1)}, bf16[2,4,16,768]{3,2,1,0:T(8,128)(2,1)S(1)}, u32[]{:S(2)}, u32[]{:S(2)}) collective-permute-start(bf16[2,4,16,768]{3,2,1,0:T(8,128)(2,1)S(1)} %get-tuple-element.32), channel_id=1, source_target_pairs={{0,32},{16,48},{32,0},{48,16},{1,33},{17,49},{33,1},{49,17},{2,34}... | collective-permute-start | bytes 589832 | tf_op jit(solution)/shard_map/ppermute | solution.py:329
  25.8 9.9 %collective-permute-start.3 = (bf16[2,4,16,768]{3,2,1,0:T(8,128)(2,1)S(1)}, bf16[2,4,16,768]{3,2,1,0:T(8,128)(2,1)S(1)}, u32[]{:S(2)}, u32[]{:S(2)}) collective-permute-start(bf16[2,4,16,768]{3,2,1,0:T(8,128)(2,1)S(1)} %get-tuple-element.31), channel_id=1, source_target_pairs={{0,48},{16,32},{32,16},{48,0},{1,49},{17,33},{33,17},{49,1},{2,50}... | collective-permute-start | bytes 589832 | tf_op jit(solution)/shard_map/ppermute | solution.py:329
  35.7 0.7 copy-start.3
  54.1 50.6 %copy-start.4 = (bf16[2,4,16,768]{3,2,1,0:T(8,128)(2,1)S(1)}, bf16[2,4,16,768]{3,2,1,0:T(8,128)(2,1)}, u32[]{:S(2)}) copy-start(bf16[2,4,16,768]{3,2,1,0:T(8,128)(2,1)} %copy-done.3) | copy-start | bytes 589828
  54.2 2.7 %collective-permute-start.4 = (bf16[8,512,128]{2,1,0:T(8,128)(2,1)S(1)}, bf16[8,512,128]{2,1,0:T(8,128)(2,1)S(1)}, u32[]{:S(2)}, u32[]{:S(2)}) collective-permute-start(bf16[8,512,128]{2,1,0:T(8,128)(2,1)S(1)} %slice.6), channel_id=1, source_target_pairs={{0,1},{1,0},{2,3},{3,2},{4,5},{5,4},{6,7},{7,6},{8,9},{9,8},{10,11... | collective-permute-start | bytes 3145736 | tf_op jit(solution)/shard_map/ppermute | solution.py:331
  56.9 47.8 %slice-start = ((s8[4718592]{0:T(1024)(128)(4,1)}), s8[4194304]{0:T(1024)(128)(4,1)S(1)}, s32[]{:S(2)}) async-start(s8[4718592]{0:T(1024)(128)(4,1)} %bitcast.26), calls=%async_computation.5 | async-start | bytes 8388608
  56.9 47.8 %slice-start.2 = ((s8[4718592]{0:T(1024)(128)(4,1)}), s8[4194304]{0:T(1024)(128)(4,1)S(1)}, s32[]{:S(2)}) async-start(s8[4718592]{0:T(1024)(128)(4,1)} %bitcast.28), calls=%async_computation.7 | async-start | bytes 8388608
  57.7 13.9 %collective-permute-start.5 = (bf16[8,512,128]{2,1,0:T(8,128)(2,1)S(1)}, bf16[8,512,128]{2,1,0:T(8,128)(2,1)S(1)}, u32[]{:S(2)}, u32[]{:S(2)}) collective-permute-start(bf16[8,512,128]{2,1,0:T(8,128)(2,1)S(1)} %slice.7), channel_id=1, source_target_pairs={{0,1},{1,0},{2,3},{3,2},{4,5},{5,4},{6,7},{7,6},{8,9},{9,8},{10,11... | collective-permute-start | bytes 3145736 | tf_op jit(solution)/shard_map/ppermute | solution.py:334
  71.6 33.0 %slice-start.1 = ((s8[4718592]{0:T(1024)(128)(4,1)}), s8[524288]{0:T(1024)(128)(4,1)S(1)}, s32[]{:S(2)}) async-start(s8[4718592]{0:T(1024)(128)(4,1)} %bitcast.26), calls=%async_computation.6 | async-start | bytes 1048576
  71.6 33.0 %slice-start.3 = ((s8[4718592]{0:T(1024)(128)(4,1)}), s8[524288]{0:T(1024)(128)(4,1)S(1)}, s32[]{:S(2)}) async-start(s8[4718592]{0:T(1024)(128)(4,1)} %bitcast.28), calls=%async_computation.8 | async-start | bytes 1048576
  82.9 21.8 %copy-start = (bf16[768,2304]{1,0:T(8,128)(2,1)S(1)}, bf16[768,2304]{1,0:T(8,128)(2,1)}, u32[]{:S(2)}) copy-start(bf16[768,2304]{1,0:T(8,128)(2,1)} %wqkv.1) | copy-start | bytes 10616836
  82.9 21.8 %copy-start.1 = (bf16[768,768]{1,0:T(8,128)(2,1)S(1)}, bf16[768,768]{1,0:T(8,128)(2,1)}, u32[]{:S(2)}) copy-start(bf16[768,768]{1,0:T(8,128)(2,1)} %wo.1) | copy-start | bytes 3538948
  82.9 21.8 %copy-start.2 = (bf16[768,768]{1,0:T(8,128)(2,1)S(1)}, bf16[768,768]{1,0:T(8,128)(2,1)}, u32[]{:S(2)}) copy-start(bf16[768,768]{1,0:T(8,128)(2,1)} %wco.1) | copy-start | bytes 3538948

commit v6 on v5

--- a/solution.py
+++ b/solution.py
@@ -33,6 +33,10 @@
     return lax.dot_general(a, b, (((1,), (1,)), ((), ())), preferred_element_type=F32)
 
 
+def dot_tn(a, b):
+    return lax.dot_general(a, b, (((0,), (0,)), ((), ())), preferred_element_type=F32)
+
+
 def swap_halves(v):
     return pltpu.roll(v, 64, 1)
 
@@ -52,7 +56,7 @@
     return pltpu.CompilerParams(vmem_limit_bytes=mib * MIB, **kw)
 
 
-def project_kernel(x_hbm, w_hbm, out_hbm, x_ref, w_ref, out_ref, sems):
+def project_kernel(x_hbm, w_hbm, out_hbm, x_ref, w_ref, out_ref, third, sems):
     get_x = pltpu.make_async_copy(x_hbm, x_ref, sems.at[3])
     get_x.start()
     get_w = []
@@ -74,20 +78,26 @@
             first = val[:256, tile * 128 : tile * 128 + 128]
             second = val[256:, tile * 128 : tile * 128 + 128]
             heads = (
-                jnp.where(low, first, swap_halves(second)).astype(BF),
-                jnp.where(low, swap_halves(first), second).astype(BF),
+                jnp.where(low, first, swap_halves(second)),
+                jnp.where(low, swap_halves(first), second),
             )
             if tile in FULL:
                 for y in range(2):
-                    out_ref[y * 4 + FULL.index(tile), at : at + 256, :] = heads[y]
+                    out_ref[y * 4 + FULL.index(tile), at : at + 256, :] = heads[y].astype(BF)
             else:
-                for y in range(2):
-                    for side in range(2):
-                        z = HALF.index(tile) + side
+                for side in range(2):
+                    z = HALF.index(tile) + side
+                    if t == 0:
+                        third[z * 256 : z * 256 + 256, :] = heads[side]
+                    for y in range(2):
                         if t > 0:
-                            out_ref[y * 4 + z, at + 256 : at + 512, :] = heads[side]
+                            out_ref[y * 4 + z, at + 256 : at + 512, :] = heads[side].astype(BF)
                         else:
-                            part = heads[side].reshape(8, 2, 16, 128)[:, y].reshape(128, 128)
+                            picked = [
+                                third[pl.ds(z * 256 + y * 2 + n, 64, stride=4), :].reshape(8, 8, 128)
+                                for n in range(2)
+                            ]
+                            part = jnp.concatenate(picked, axis=1).reshape(128, 128).astype(BF)
                             out_ref[y * 4 + z, at + 256 : at + 384, :] = part
         part = pl.ds(at, 384 if t == 0 else 512)
         put.append(
@@ -109,6 +119,7 @@
             pltpu.VMEM((512, D), BF),
             pltpu.VMEM((D, 3 * D), BF),
             pltpu.VMEM((8, 1408, 128), BF),
+            pltpu.VMEM((1024, 128), F32),
             pltpu.SemaphoreType.DMA((7,)),
         ],
         compiler_params=params(58),
@@ -167,7 +178,7 @@
         total += parts_ref[s].astype(F32)
     total *= 1.0 / math.sqrt(DH * ROWS)
     e = jnp.exp(total - jnp.max(total, axis=-1, keepdims=True))
-    w = (e / jnp.sum(e, axis=-1, keepdims=True)).astype(BF)
+    w = (e * (1.0 / jnp.sum(e, axis=-1, keepdims=True))).astype(BF)
     for s in range(8):
         out_ref[s] = w
 
@@ -194,11 +205,11 @@
     for a in range(8):
         for s in range(8):
             to = s * 8 + a
-            at = (a * 32 + s * 2) * 8
-            out_ref[to, 0:16, :] = whole[at : at + 16, :].astype(BF)
-            out_ref[to, 16:32, :] = whole[at + 128 : at + 144, :].astype(BF)
-            at = (a * 16 + s * 2) * 8
-            out_ref[to, 32:48, :] = part[at : at + 16, :].astype(BF)
+            at = (a * 32 + s * 4) * 8
+            out_ref[to, 0:32, :] = whole[at : at + 32, :].astype(BF)
+            at = (a * 16 + s) * 8
+            pair = jnp.concatenate([part[at : at + 8, :], part[at + 64 : at + 72, :]], axis=0)
+            out_ref[to, 32:48, :] = pair.astype(BF)
 
 
 def attend(w, got, v2):
@@ -219,18 +230,8 @@
 
 def columns_kernel(
     me_ref, att_ref, x0, x1, x2, x3, wo, wqkv, wco, w1, w2, out_ref,
-    att, x_in, state, col, sems,
+    att, x_in, state, col,
 ):
-    def copy(src, dst, sem):
-        return pltpu.make_async_copy(src, dst, sems.at[sem])
-
-    get_x = []
-    for k, block in enumerate((x0, x1, x2, x3)):
-        for side in range(2):
-            y = me_ref[0] if side == 0 else 1 - me_ref[0]
-            at = pl.multiple_of((y * 4 + (me_ref[1] ^ k)) * 16, 16)
-            get_x.append(copy(block.at[side], x_in.at[:, pl.ds(at, 16), :], 2 + 2 * k + side))
-            get_x[-1].start()
     low = low_lanes((8, 8, 128))
 
     def place(i, tile, first, second):
@@ -254,8 +255,12 @@
                 rows = slice(n * 8, n * 8 + 8)
                 place(y * 2 + n, HALF[z], first[:, rows], second[:, rows])
     low = low_lanes((128, 128))
-    for block in get_x:
-        block.wait()
+    for k, block in enumerate((x0, x1, x2, x3)):
+        for side in range(2):
+            y = me_ref[0] if side == 0 else 1 - me_ref[0]
+            at = pl.multiple_of((y * 4 + (me_ref[1] ^ k)) * 16, 16)
+            for i in range(4):
+                x_in[i, pl.ds(at, 16), :] = block[side, i]
     after_rows = (x_in[...].reshape(512, D).astype(F32) + dot32(att[...], wo[...])).astype(BF)
     state[...] = after_rows
     normed = normalize(after_rows.astype(F32))
@@ -269,10 +274,10 @@
             k = col[rows, D + t * 128 : D + t * 128 + 128]
             v = col[rows, 2 * D + t * 128 : 2 * D + t * 128 + 128]
             pair = jnp.concatenate([jnp.where(low, q, zero), jnp.where(low, zero, q)], axis=0)
-            s = dot_t(pair, k) * (1.0 / math.sqrt(DH))
-            e = jnp.exp(s - jnp.max(s, axis=-1, keepdims=True))
-            w = (e / jnp.sum(e, axis=-1, keepdims=True)).astype(BF)
-            o = dot32(w, v)
+            s = dot_t(k, pair) * (1.0 / math.sqrt(DH))
+            e = jnp.exp(s - jnp.max(s, axis=0, keepdims=True))
+            w = (e * (1.0 / jnp.sum(e, axis=0, keepdims=True))).astype(BF)
+            o = dot_tn(w, v)
             att[rows, t * 128 : t * 128 + 128] = jnp.where(low, o[:128], o[128:]).astype(BF)
     after_cols = (state[...].astype(F32) + dot32(att[...], wco[...])).astype(BF)
     state[...] = after_cols
@@ -288,12 +293,9 @@
 
 def columns(me, att, x, wo, wqkv, wco, w1, w2):
     vmem = pl.BlockSpec(memory_space=pltpu.VMEM)
-    anywhere = pl.BlockSpec(memory_space=pl.ANY)
     return pl.pallas_call(
         columns_kernel,
-        in_specs=[pl.BlockSpec(memory_space=pltpu.SMEM), vmem]
-        + [anywhere] * 4
-        + [vmem] * 5,
+        in_specs=[pl.BlockSpec(memory_space=pltpu.SMEM)] + [vmem] * 10,
         out_specs=vmem,
         out_shape=jax.ShapeDtypeStruct((8, 4, 16, D), BF),
         scratch_shapes=[
@@ -301,7 +303,6 @@
             pltpu.VMEM((4, 128, D), BF),
             pltpu.VMEM((512, D), BF),
             pltpu.VMEM((512, 3 * D), BF),
-            pltpu.SemaphoreType.DMA((11,)),
         ],
         compiler_params=params(24),
         cost_estimate=pl.CostEstimate(
@@ -315,14 +316,13 @@
     barrier = lax.optimization_barrier
     swap = [(0, 1), (1, 0)]
     y_me, x_me = lax.axis_index("y_lo"), lax.axis_index("x")
-    halves = x.reshape(16, 2, 2, 8, D)
-    far = lax.ppermute(lax.dynamic_index_in_dim(halves, 1 - y_me, 2, False), "y_lo", swap)
+    halves = x.reshape(16, 2, 16, D)
+    far = lax.ppermute(lax.dynamic_index_in_dim(halves, 1 - y_me, 1, False), "y_lo", swap)
     me = jnp.stack([y_me, x_me]).astype(jnp.int32)
     proj, x, far, me = barrier((project(x.reshape(512, D), row_qkv), x, far, me))
     got = lax.all_to_all(proj, ("y_hi", "z"), 0, 0, tiled=True)
-    mine = lax.dynamic_index_in_dim(x.reshape(16, 2, 2, 8, D), y_me, 2, False)
-    x_cols = jnp.stack([mine, far]).reshape(2, 16, 2, 4, 2, D)
-    x_cols = x_cols.transpose(3, 0, 2, 4, 1, 5).reshape(4, 2, 4, 16, D)
+    mine = lax.dynamic_index_in_dim(x.reshape(16, 2, 16, D), y_me, 1, False)
+    x_cols = jnp.stack([mine, far]).reshape(2, 16, 4, 4, D).transpose(2, 0, 3, 1, 4)
     near = []
     for k in range(4):
         block = lax.dynamic_index_in_dim(x_cols, x_me ^ k, 0, False)
@@ -338,7 +338,7 @@
     att = att.reshape(8, 2, 4, 48, 128)
     out = columns(me, att, near, row_out, col_qkv, col_out, ff_in, ff_out)
     out = lax.all_to_all(out, SEQ, 0, 0, tiled=True)
-    return out.reshape(8, 2, 2, 16, D).transpose(3, 1, 0, 2, 4).reshape(16, 32, D)
+    return out.transpose(2, 0, 1, 3).reshape(16, 32, D)
 
 
 def solution(mesh):

time: 132 us -> 130 us (0.985)
  no operation moved by 1% of the time
where the time goes in v6:
time: 130 us
  blocking collectives  58.3 us (45%)
  waiting for transfers between devices  33.3 us (26%)
  Pallas kernels  18.8 us (14%)
  starting transfers between devices  14.9 us (11%)
  local copies, waits for them, and re-layouts  4.24 us (3%)
    all_to_all x1, blocking collectives, per_device(): att = lax.all_to_all(attend(shares, got, v2), CHIPS, 0, 0, tiled=True)  21 us
    all_to_all x1, waiting for transfers between devices, per_device(): got = lax.all_to_all(proj, ('y_hi', 'z'), 0, 0, tiled=True)  17.8 us
    all_to_all x1, blocking collectives, per_device(): parts = lax.all_to_all(parts, SEQ, 0, 0, tiled=True)  13.7 us
    all_to_all x1, blocking collectives, per_device(): out = lax.all_to_all(out, SEQ, 0, 0, tiled=True)  12.6 us
    pallas_call x1, Pallas kernels, columns(): pl.pallas_call(columns_kernel, in_specs=[pl.BlockSpec(memory_space=pltpu....  11.4 us
    all_to_all x1, blocking collectives, per_device(): shares = lax.all_to_all(softmax(parts), SEQ, 0, 0, tiled=True)  11 us
    ppermute x3, waiting for transfers between devices, per_device(): lax.ppermute(block, 'x', [(i, i ^ k) for i in range(4)])  9.47 us
    all_to_all x1, starting transfers between devices, per_device(): got = lax.all_to_all(proj, ('y_hi', 'z'), 0, 0, tiled=True)  8.11 us
  transfers between devices with their start and end apart: 7, of which 6 were waited for; matrix products, arithmetic and copies ran while one was open for 1% of the time, Pallas kernels for 4%

profile of v6, /device:TPU:0, one launch (start us, length us, event | category | flops | bytes accessed | tf_op | source)
XLA Modules:
  0.0 129.8 jit_solution(15813872250911569784)
XLA Ops:
  0.0 1.0 constant_dynamic-slice_fusion.1
  1.0 0.1 copy.13
  1.2 1.7 %collective-permute-start = (bf16[16,16,768]{2,0,1:T(8,128)(2,1)S(1)}, bf16[16,16,768]{2,0,1:T(8,128)(2,1)S(1)}, u32[]{:S(2)}, u32[]{:S(2)}) collective-permute-start(bf16[16,16,768]{2,0,1:T(8,128)(2,1)S(1)} %bitcast.40), channel_id=1, source_target_pairs={{0,64},{64,0},{1,65},{65,1},{2,66},{66,2},{3,67},{67,3},{4,68},{68... | collective-permute-start | bytes 1179656 | tf_op jit(solution)/shard_map/ppermute | solution.py:320
  2.9 0.1 pad_add_fusion.me_ref
  3.0 5.7 %project.1 = bf16[8,1408,128]{2,1,0:T(8,128)(2,1)} custom-call(bf16[512,768]{1,0:T(8,128)(2,1)} %bitcast.36, bf16[768,2304]{1,0:T(8,128)(2,1)} %w_hbm.1), custom_call_target="tpu_custom_call" | custom-call | flops 1811939328 | bytes 6291456 | tf_op jit(solution)/shard_map/project/pallas_call | solution.py:113
  8.7 3.4 %collective-permute-done = bf16[16,16,768]{2,0,1:T(8,128)(2,1)S(1)} collective-permute-done((bf16[16,16,768]{2,0,1:T(8,128)(2,1)S(1)}, bf16[16,16,768]{2,0,1:T(8,128)(2,1)S(1)}, u32[]{:S(2)}, u32[]{:S(2)}) %collective-permute-start) | collective-permute-done | bytes 393248 | tf_op jit(solution)/shard_map/ppermute | solution.py:320
  12.0 8.1 %all-to-all-start = ((bf16[8,1408,128]{2,1,0:T(8,128)(2,1)}), bf16[8,1408,128]{2,1,0:T(8,128)(2,1)S(1)}, u32[]{:S(2)}, u32[]{:S(2)}) async-start(bf16[8,1408,128]{2,1,0:T(8,128)(2,1)} %project.1), calls=%async_computation | async-start | bytes 5767168 | tf_op jit(solution)/shard_map/all_to_all | solution.py:323
  20.1 1.0 constant_dynamic-slice_fusion
  21.1 0.1 copy.11
  21.3 0.1 fusion.1
  21.4 1.6 %collective-permute-start.1 = (bf16[2,4,16,768]{3,2,1,0:T(8,128)(2,1)S(1)}, bf16[2,4,16,768]{3,2,1,0:T(8,128)(2,1)S(1)}, u32[]{:S(2)}, u32[]{:S(2)}) collective-permute-start(bf16[2,4,16,768]{3,2,1,0:T(8,128)(2,1)S(1)} %get-tuple-element.33), channel_id=1, source_target_pairs={{0,16},{16,0},{32,48},{48,32},{1,17},{17,1},{33,49},{49,33},{2,18}... | collective-permute-start | bytes 589832 | tf_op jit(solution)/shard_map/ppermute | solution.py:329
  22.9 2.7 %collective-permute-start.2 = (bf16[2,4,16,768]{3,2,1,0:T(8,128)(2,1)S(1)}, bf16[2,4,16,768]{3,2,1,0:T(8,128)(2,1)S(1)}, u32[]{:S(2)}, u32[]{:S(2)}) collective-permute-start(bf16[2,4,16,768]{3,2,1,0:T(8,128)(2,1)S(1)} %get-tuple-element.34), channel_id=1, source_target_pairs={{0,32},{16,48},{32,0},{48,16},{1,33},{17,49},{33,1},{49,17},{2,34}... | collective-permute-start | bytes 589832 | tf_op jit(solution)/shard_map/ppermute | solution.py:329
  25.7 0.5 collective-permute-start.3
  26.1 2.9 %collective-permute-done.1.x1 = bf16[2,4,16,768]{3,2,1,0:T(8,128)(2,1)S(1)} collective-permute-done((bf16[2,4,16,768]{3,2,1,0:T(8,128)(2,1)S(1)}, bf16[2,4,16,768]{3,2,1,0:T(8,128)(2,1)S(1)}, u32[]{:S(2)}, u32[]{:S(2)}) %collective-permute-start.1) | collective-permute-done | bytes 196640 | tf_op jit(solution)/shard_map/ppermute | solution.py:329
  29.1 4.4 %collective-permute-done.2.x2 = bf16[2,4,16,768]{3,2,1,0:T(8,128)(2,1)S(1)} collective-permute-done((bf16[2,4,16,768]{3,2,1,0:T(8,128)(2,1)S(1)}, bf16[2,4,16,768]{3,2,1,0:T(8,128)(2,1)S(1)}, u32[]{:S(2)}, u32[]{:S(2)}) %collective-permute-start.2) | collective-permute-done | bytes 196640 | tf_op jit(solution)/shard_map/ppermute | solution.py:329
  33.4 2.2 %collective-permute-done.3.x3 = bf16[2,4,16,768]{3,2,1,0:T(8,128)(2,1)S(1)} collective-permute-done((bf16[2,4,16,768]{3,2,1,0:T(8,128)(2,1)S(1)}, bf16[2,4,16,768]{3,2,1,0:T(8,128)(2,1)S(1)}, u32[]{:S(2)}, u32[]{:S(2)}) %collective-permute-start.3) | collective-permute-done | bytes 196640 | tf_op jit(solution)/shard_map/ppermute | solution.py:329
  35.6 0.0 copy-start.3
  35.6 0.7 copy-done.3
  36.3 17.8 %all-to-all-done.got_ref = bf16[8,1408,128]{2,1,0:T(8,128)(2,1)S(1)} async-done(((bf16[8,1408,128]{2,1,0:T(8,128)(2,1)}), bf16[8,1408,128]{2,1,0:T(8,128)(2,1)S(1)}, u32[]{:S(2)}, u32[]{:S(2)}) %all-to-all-start) | async-done | bytes 2883616 | tf_op jit(solution)/shard_map/all_to_all | solution.py:323
  54.1 0.0 copy-start.4
  54.1 0.1 slice.6
  54.2 0.1 collective-permute-start.4
  54.3 2.6 %collective-permute-done.4.k2_ref = bf16[8,512,128]{2,1,0:T(8,128)(2,1)S(1)} collective-permute-done((bf16[8,512,128]{2,1,0:T(8,128)(2,1)S(1)}, bf16[8,512,128]{2,1,0:T(8,128)(2,1)S(1)}, u32[]{:S(2)}, u32[]{:S(2)}) %collective-permute-start.4) | collective-permute-done | bytes 1048608 | tf_op jit(solution)/shard_map/ppermute | solution.py:331
  56.9 0.0 slice-start
  56.9 0.0 slice-start.2
  56.9 0.7 scores.1
  57.7 0.1 slice.7
  57.7 0.2 collective-permute-start.5
  57.9 13.7 %all_to_all.25.parts_ref = bf16[8,48,512]{2,1,0:T(8,128)(2,1)S(1)} all-to-all(bf16[8,48,512]{2,1,0:T(8,128)(2,1)S(1)} %scores.1), channel_id=1, replica_groups=mesh['y_lo'=2,'x'=4,'y_hi'=2,'z'=4,'core'=2] {'y_lo','x'}, dimensions={0} | all-to-all | bytes 786432 | tf_op jit(solution)/shard_map/all_to_all | solution.py:333
  71.6 0.0 slice-start.1
  71.6 0.0 slice-start.3
  71.6 0.0 collective-permute-done.5.v2_ref
  71.6 0.2 softmax.1
  71.9 11.0 %all_to_all.26.w_ref = bf16[8,48,512]{2,1,0:T(8,128)(2,1)S(1)} all-to-all(bf16[8,48,512]{2,1,0:T(8,128)(2,1)S(1)} %softmax.1), channel_id=1, replica_groups=mesh['y_lo'=2,'x'=4,'y_hi'=2,'z'=4,'core'=2] {'y_lo','x'}, dimensions={0} | all-to-all | bytes 786432 | tf_op jit(solution)/shard_map/all_to_all | solution.py:336
  82.9 0.0 copy-start
  82.9 0.0 copy-start.1
  82.9 0.0 copy-start.2
  82.9 0.7 attend.1
  83.6 21.0 %all_to_all.27 = bf16[64,48,128]{2,1,0:T(8,128)(2,1)S(1)} all-to-all(bf16[64,48,128]{2,1,0:T(8,128)(2,1)S(1)} %attend.1), channel_id=1, replica_groups=mesh['y_lo'=2,'x'=4,'y_hi'=2,'z'=4,'core'=2] {'y_lo','x','y_hi','z'}, dimensions={0} | all-to-all | bytes 1572864 | tf_op jit(solution)/shard_map/all_to_all | solution.py:337
  104.6 0.0 copy-done.4
  104.6 0.0 slice-done
  104.7 0.0 slice-done.2
  104.7 0.0 slice-done.1
  104.7 0.0 slice-done.3
  104.7 0.0 copy-done
  104.7 0.0 copy-done.1
  104.7 0.0 copy-done.2
  104.7 11.4 %columns.1 = bf16[8,4,16,768]{3,2,1,0:T(8,128)(2,1)S(1)} custom-call(s32[2]{0:T(128)S(1)} %pad_add_fusion.me_ref, bf16[8,2,4,48,128]{4,3,2,1,0:T(8,128)(2,1)S(1)} %bitcast.30, bf16[2,4,16,768]{3,2,1,0:T(8,128)(2,1)S(1)} %get-tuple-element.27.x0, bf16[2,4,16,768]{3,2,1,0:T(8,128)(2,1)S(1)} %collective-permute-done.1.x1, ...), custom_call_target="tpu_custom_call" | custom-call | flops 8000000000 | bytes 18874368 | tf_op jit(solution)/shard_map/columns/pallas_call | solution.py:296
  116.2 12.6 %all_to_all.28 = bf16[8,4,16,768]{3,2,1,0:T(8,128)(2,1)S(1)} all-to-all(bf16[8,4,16,768]{3,2,1,0:T(8,128)(2,1)S(1)} %columns.1), channel_id=1, replica_groups=mesh['y_lo'=2,'x'=4,'y_hi'=2,'z'=4,'core'=2] {'y_lo','x'}, dimensions={0} | all-to-all | bytes 1572864 | tf_op jit(solution)/shard_map/all_to_all | solution.py:340
  128.7 1.1 copy.10
  (2 shorter events, 0.0 us)
Async XLA Ops:
  1.2 10.9 %collective-permute-start = (bf16[16,16,768]{2,0,1:T(8,128)(2,1)S(1)}, bf16[16,16,768]{2,0,1:T(8,128)(2,1)S(1)}, u32[]{:S(2)}, u32[]{:S(2)}) collective-permute-start(bf16[16,16,768]{2,0,1:T(8,128)(2,1)S(1)} %bitcast.40), channel_id=1, source_target_pairs={{0,64},{64,0},{1,65},{65,1},{2,66},{66,2},{3,67},{67,3},{4,68},{68... | collective-permute-start | bytes 1179656 | tf_op jit(solution)/shard_map/ppermute | solution.py:320
  12.0 42.1 %all-to-all-start = ((bf16[8,1408,128]{2,1,0:T(8,128)(2,1)}), bf16[8,1408,128]{2,1,0:T(8,128)(2,1)S(1)}, u32[]{:S(2)}, u32[]{:S(2)}) async-start(bf16[8,1408,128]{2,1,0:T(8,128)(2,1)} %project.1), calls=%async_computation | async-start | bytes 5767168 | tf_op jit(solution)/shard_map/all_to_all | solution.py:323
  21.4 7.7 %collective-permute-start.1 = (bf16[2,4,16,768]{3,2,1,0:T(8,128)(2,1)S(1)}, bf16[2,4,16,768]{3,2,1,0:T(8,128)(2,1)S(1)}, u32[]{:S(2)}, u32[]{:S(2)}) collective-permute-start(bf16[2,4,16,768]{3,2,1,0:T(8,128)(2,1)S(1)} %get-tuple-element.33), channel_id=1, source_target_pairs={{0,16},{16,0},{32,48},{48,32},{1,17},{17,1},{33,49},{49,33},{2,18}... | collective-permute-start | bytes 589832 | tf_op jit(solution)/shard_map/ppermute | solution.py:329
  22.9 10.5 %collective-permute-start.2 = (bf16[2,4,16,768]{3,2,1,0:T(8,128)(2,1)S(1)}, bf16[2,4,16,768]{3,2,1,0:T(8,128)(2,1)S(1)}, u32[]{:S(2)}, u32[]{:S(2)}) collective-permute-start(bf16[2,4,16,768]{3,2,1,0:T(8,128)(2,1)S(1)} %get-tuple-element.34), channel_id=1, source_target_pairs={{0,32},{16,48},{32,0},{48,16},{1,33},{17,49},{33,1},{49,17},{2,34}... | collective-permute-start | bytes 589832 | tf_op jit(solution)/shard_map/ppermute | solution.py:329
  25.7 9.9 %collective-permute-start.3 = (bf16[2,4,16,768]{3,2,1,0:T(8,128)(2,1)S(1)}, bf16[2,4,16,768]{3,2,1,0:T(8,128)(2,1)S(1)}, u32[]{:S(2)}, u32[]{:S(2)}) collective-permute-start(bf16[2,4,16,768]{3,2,1,0:T(8,128)(2,1)S(1)} %get-tuple-element.31), channel_id=1, source_target_pairs={{0,48},{16,32},{32,16},{48,0},{1,49},{17,33},{33,17},{49,1},{2,50}... | collective-permute-start | bytes 589832 | tf_op jit(solution)/shard_map/ppermute | solution.py:329
  35.6 0.7 copy-start.3
  54.1 50.6 %copy-start.4 = (bf16[2,4,16,768]{3,2,1,0:T(8,128)(2,1)S(1)}, bf16[2,4,16,768]{3,2,1,0:T(8,128)(2,1)}, u32[]{:S(2)}) copy-start(bf16[2,4,16,768]{3,2,1,0:T(8,128)(2,1)} %copy-done.3) | copy-start | bytes 589828
  54.2 2.7 %collective-permute-start.4 = (bf16[8,512,128]{2,1,0:T(8,128)(2,1)S(1)}, bf16[8,512,128]{2,1,0:T(8,128)(2,1)S(1)}, u32[]{:S(2)}, u32[]{:S(2)}) collective-permute-start(bf16[8,512,128]{2,1,0:T(8,128)(2,1)S(1)} %slice.6), channel_id=1, source_target_pairs={{0,1},{1,0},{2,3},{3,2},{4,5},{5,4},{6,7},{7,6},{8,9},{9,8},{10,11... | collective-permute-start | bytes 3145736 | tf_op jit(solution)/shard_map/ppermute | solution.py:331
  56.9 47.8 %slice-start = ((s8[4718592]{0:T(1024)(128)(4,1)}), s8[4194304]{0:T(1024)(128)(4,1)S(1)}, s32[]{:S(2)}) async-start(s8[4718592]{0:T(1024)(128)(4,1)} %bitcast.31), calls=%async_computation.5 | async-start | bytes 8388608
  56.9 47.8 %slice-start.2 = ((s8[4718592]{0:T(1024)(128)(4,1)}), s8[4194304]{0:T(1024)(128)(4,1)S(1)}, s32[]{:S(2)}) async-start(s8[4718592]{0:T(1024)(128)(4,1)} %bitcast.33), calls=%async_computation.7 | async-start | bytes 8388608
  57.7 13.9 %collective-permute-start.5 = (bf16[8,512,128]{2,1,0:T(8,128)(2,1)S(1)}, bf16[8,512,128]{2,1,0:T(8,128)(2,1)S(1)}, u32[]{:S(2)}, u32[]{:S(2)}) collective-permute-start(bf16[8,512,128]{2,1,0:T(8,128)(2,1)S(1)} %slice.7), channel_id=1, source_target_pairs={{0,1},{1,0},{2,3},{3,2},{4,5},{5,4},{6,7},{7,6},{8,9},{9,8},{10,11... | collective-permute-start | bytes 3145736 | tf_op jit(solution)/shard_map/ppermute | solution.py:334
  71.6 33.0 %slice-start.1 = ((s8[4718592]{0:T(1024)(128)(4,1)}), s8[524288]{0:T(1024)(128)(4,1)S(1)}, s32[]{:S(2)}) async-start(s8[4718592]{0:T(1024)(128)(4,1)} %bitcast.31), calls=%async_computation.6 | async-start | bytes 1048576
  71.6 33.0 %slice-start.3 = ((s8[4718592]{0:T(1024)(128)(4,1)}), s8[524288]{0:T(1024)(128)(4,1)S(1)}, s32[]{:S(2)}) async-start(s8[4718592]{0:T(1024)(128)(4,1)} %bitcast.33), calls=%async_computation.8 | async-start | bytes 1048576
  82.9 21.8 %copy-start = (bf16[768,2304]{1,0:T(8,128)(2,1)S(1)}, bf16[768,2304]{1,0:T(8,128)(2,1)}, u32[]{:S(2)}) copy-start(bf16[768,2304]{1,0:T(8,128)(2,1)} %wqkv.1) | copy-start | bytes 10616836
  82.9 21.8 %copy-start.1 = (bf16[768,768]{1,0:T(8,128)(2,1)S(1)}, bf16[768,768]{1,0:T(8,128)(2,1)}, u32[]{:S(2)}) copy-start(bf16[768,768]{1,0:T(8,128)(2,1)} %wo.1) | copy-start | bytes 3538948
  82.9 21.8 %copy-start.2 = (bf16[768,768]{1,0:T(8,128)(2,1)S(1)}, bf16[768,768]{1,0:T(8,128)(2,1)}, u32[]{:S(2)}) copy-start(bf16[768,768]{1,0:T(8,128)(2,1)} %wco.1) | copy-start | bytes 3538948

commit v7 on v6

--- a/solution.py
+++ b/solution.py
@@ -119,7 +119,7 @@
             pltpu.VMEM((512, D), BF),
             pltpu.VMEM((D, 3 * D), BF),
             pltpu.VMEM((8, 1408, 128), BF),
-            pltpu.VMEM((1024, 128), F32),
+            pltpu.VMEM((1032, 128), F32),
             pltpu.SemaphoreType.DMA((7,)),
         ],
         compiler_params=params(58),
@@ -219,7 +219,7 @@
         in_specs=[vmem, vmem, vmem],
         out_specs=vmem,
         out_shape=jax.ShapeDtypeStruct((64, 48, 128), BF),
-        scratch_shapes=[pltpu.VMEM((2048, 128), F32), pltpu.VMEM((1024, 128), F32)],
+        scratch_shapes=[pltpu.VMEM((2056, 128), F32), pltpu.VMEM((1032, 128), F32)],
         compiler_params=params(12),
         cost_estimate=pl.CostEstimate(
             flops=2 * 384 * 512 * 1024, bytes_accessed=3 * MIB, transcendentals=0

time: 130 us -> 130 us (level)
  no operation moved by 1% of the time
where the time goes in v7:
time: 130 us
  blocking collectives  58.3 us (45%)
  waiting for transfers between devices  33.3 us (26%)
  Pallas kernels  18.8 us (14%)
  starting transfers between devices  14.9 us (11%)
  local copies, waits for them, and re-layouts  4.24 us (3%)
    all_to_all x1, blocking collectives, per_device(): att = lax.all_to_all(attend(shares, got, v2), CHIPS, 0, 0, tiled=True)  21 us
    all_to_all x1, waiting for transfers between devices, per_device(): got = lax.all_to_all(proj, ('y_hi', 'z'), 0, 0, tiled=True)  17.8 us
    all_to_all x1, blocking collectives, per_device(): parts = lax.all_to_all(parts, SEQ, 0, 0, tiled=True)  13.7 us
    all_to_all x1, blocking collectives, per_device(): out = lax.all_to_all(out, SEQ, 0, 0, tiled=True)  12.6 us
    pallas_call x1, Pallas kernels, columns(): pl.pallas_call(columns_kernel, in_specs=[pl.BlockSpec(memory_space=pltpu....  11.4 us
    all_to_all x1, blocking collectives, per_device(): shares = lax.all_to_all(softmax(parts), SEQ, 0, 0, tiled=True)  11 us
    ppermute x3, waiting for transfers between devices, per_device(): lax.ppermute(block, 'x', [(i, i ^ k) for i in range(4)])  9.47 us
    all_to_all x1, starting transfers between devices, per_device(): got = lax.all_to_all(proj, ('y_hi', 'z'), 0, 0, tiled=True)  8.11 us
  transfers between devices with their start and end apart: 7, of which 6 were waited for; matrix products, arithmetic and copies ran while one was open for 1% of the time, Pallas kernels for 4%

profile of v7, /device:TPU:0, one launch (start us, length us, event | category | flops | bytes accessed | tf_op | source)
XLA Modules:
  0.0 129.8 jit_solution(3151965553048374584)
XLA Ops:
  0.0 1.0 constant_dynamic-slice_fusion.1
  1.0 0.1 copy.13
  1.2 1.7 %collective-permute-start = (bf16[16,16,768]{2,0,1:T(8,128)(2,1)S(1)}, bf16[16,16,768]{2,0,1:T(8,128)(2,1)S(1)}, u32[]{:S(2)}, u32[]{:S(2)}) collective-permute-start(bf16[16,16,768]{2,0,1:T(8,128)(2,1)S(1)} %bitcast.40), channel_id=1, source_target_pairs={{0,64},{64,0},{1,65},{65,1},{2,66},{66,2},{3,67},{67,3},{4,68},{68... | collective-permute-start | bytes 1179656 | tf_op jit(solution)/shard_map/ppermute | solution.py:320
  2.9 0.1 pad_add_fusion.me_ref
  3.0 5.7 %project.1 = bf16[8,1408,128]{2,1,0:T(8,128)(2,1)} custom-call(bf16[512,768]{1,0:T(8,128)(2,1)} %bitcast.36, bf16[768,2304]{1,0:T(8,128)(2,1)} %w_hbm.1), custom_call_target="tpu_custom_call" | custom-call | flops 1811939328 | bytes 6291456 | tf_op jit(solution)/shard_map/project/pallas_call | solution.py:113
  8.7 3.4 %collective-permute-done = bf16[16,16,768]{2,0,1:T(8,128)(2,1)S(1)} collective-permute-done((bf16[16,16,768]{2,0,1:T(8,128)(2,1)S(1)}, bf16[16,16,768]{2,0,1:T(8,128)(2,1)S(1)}, u32[]{:S(2)}, u32[]{:S(2)}) %collective-permute-start) | collective-permute-done | bytes 393248 | tf_op jit(solution)/shard_map/ppermute | solution.py:320
  12.0 8.1 %all-to-all-start = ((bf16[8,1408,128]{2,1,0:T(8,128)(2,1)}), bf16[8,1408,128]{2,1,0:T(8,128)(2,1)S(1)}, u32[]{:S(2)}, u32[]{:S(2)}) async-start(bf16[8,1408,128]{2,1,0:T(8,128)(2,1)} %project.1), calls=%async_computation | async-start | bytes 5767168 | tf_op jit(solution)/shard_map/all_to_all | solution.py:323
  20.1 1.0 constant_dynamic-slice_fusion
  21.1 0.1 copy.11
  21.3 0.1 fusion.1
  21.4 1.6 %collective-permute-start.1 = (bf16[2,4,16,768]{3,2,1,0:T(8,128)(2,1)S(1)}, bf16[2,4,16,768]{3,2,1,0:T(8,128)(2,1)S(1)}, u32[]{:S(2)}, u32[]{:S(2)}) collective-permute-start(bf16[2,4,16,768]{3,2,1,0:T(8,128)(2,1)S(1)} %get-tuple-element.33), channel_id=1, source_target_pairs={{0,16},{16,0},{32,48},{48,32},{1,17},{17,1},{33,49},{49,33},{2,18}... | collective-permute-start | bytes 589832 | tf_op jit(solution)/shard_map/ppermute | solution.py:329
  22.9 2.7 %collective-permute-start.2 = (bf16[2,4,16,768]{3,2,1,0:T(8,128)(2,1)S(1)}, bf16[2,4,16,768]{3,2,1,0:T(8,128)(2,1)S(1)}, u32[]{:S(2)}, u32[]{:S(2)}) collective-permute-start(bf16[2,4,16,768]{3,2,1,0:T(8,128)(2,1)S(1)} %get-tuple-element.34), channel_id=1, source_target_pairs={{0,32},{16,48},{32,0},{48,16},{1,33},{17,49},{33,1},{49,17},{2,34}... | collective-permute-start | bytes 589832 | tf_op jit(solution)/shard_map/ppermute | solution.py:329
  25.7 0.5 collective-permute-start.3
  26.1 2.9 %collective-permute-done.1.x1 = bf16[2,4,16,768]{3,2,1,0:T(8,128)(2,1)S(1)} collective-permute-done((bf16[2,4,16,768]{3,2,1,0:T(8,128)(2,1)S(1)}, bf16[2,4,16,768]{3,2,1,0:T(8,128)(2,1)S(1)}, u32[]{:S(2)}, u32[]{:S(2)}) %collective-permute-start.1) | collective-permute-done | bytes 196640 | tf_op jit(solution)/shard_map/ppermute | solution.py:329
  29.1 4.4 %collective-permute-done.2.x2 = bf16[2,4,16,768]{3,2,1,0:T(8,128)(2,1)S(1)} collective-permute-done((bf16[2,4,16,768]{3,2,1,0:T(8,128)(2,1)S(1)}, bf16[2,4,16,768]{3,2,1,0:T(8,128)(2,1)S(1)}, u32[]{:S(2)}, u32[]{:S(2)}) %collective-permute-start.2) | collective-permute-done | bytes 196640 | tf_op jit(solution)/shard_map/ppermute | solution.py:329
  33.4 2.2 %collective-permute-done.3.x3 = bf16[2,4,16,768]{3,2,1,0:T(8,128)(2,1)S(1)} collective-permute-done((bf16[2,4,16,768]{3,2,1,0:T(8,128)(2,1)S(1)}, bf16[2,4,16,768]{3,2,1,0:T(8,128)(2,1)S(1)}, u32[]{:S(2)}, u32[]{:S(2)}) %collective-permute-start.3) | collective-permute-done | bytes 196640 | tf_op jit(solution)/shard_map/ppermute | solution.py:329
  35.6 0.0 copy-start.3
  35.6 0.7 copy-done.3
  36.3 17.8 %all-to-all-done.got_ref = bf16[8,1408,128]{2,1,0:T(8,128)(2,1)S(1)} async-done(((bf16[8,1408,128]{2,1,0:T(8,128)(2,1)}), bf16[8,1408,128]{2,1,0:T(8,128)(2,1)S(1)}, u32[]{:S(2)}, u32[]{:S(2)}) %all-to-all-start) | async-done | bytes 2883616 | tf_op jit(solution)/shard_map/all_to_all | solution.py:323
  54.1 0.0 copy-start.4
  54.1 0.1 slice.6
  54.2 0.1 collective-permute-start.4
  54.3 2.6 %collective-permute-done.4.k2_ref = bf16[8,512,128]{2,1,0:T(8,128)(2,1)S(1)} collective-permute-done((bf16[8,512,128]{2,1,0:T(8,128)(2,1)S(1)}, bf16[8,512,128]{2,1,0:T(8,128)(2,1)S(1)}, u32[]{:S(2)}, u32[]{:S(2)}) %collective-permute-start.4) | collective-permute-done | bytes 1048608 | tf_op jit(solution)/shard_map/ppermute | solution.py:331
  56.9 0.0 slice-start
  56.9 0.0 slice-start.2
  56.9 0.7 scores.1
  57.7 0.1 slice.7
  57.7 0.2 collective-permute-start.5
  57.9 13.7 %all_to_all.25.parts_ref = bf16[8,48,512]{2,1,0:T(8,128)(2,1)S(1)} all-to-all(bf16[8,48,512]{2,1,0:T(8,128)(2,1)S(1)} %scores.1), channel_id=1, replica_groups=mesh['y_lo'=2,'x'=4,'y_hi'=2,'z'=4,'core'=2] {'y_lo','x'}, dimensions={0} | all-to-all | bytes 786432 | tf_op jit(solution)/shard_map/all_to_all | solution.py:333
  71.6 0.0 slice-start.1
  71.6 0.0 slice-start.3
  71.6 0.0 collective-permute-done.5.v2_ref
  71.6 0.2 softmax.1
  71.9 11.0 %all_to_all.26.w_ref = bf16[8,48,512]{2,1,0:T(8,128)(2,1)S(1)} all-to-all(bf16[8,48,512]{2,1,0:T(8,128)(2,1)S(1)} %softmax.1), channel_id=1, replica_groups=mesh['y_lo'=2,'x'=4,'y_hi'=2,'z'=4,'core'=2] {'y_lo','x'}, dimensions={0} | all-to-all | bytes 786432 | tf_op jit(solution)/shard_map/all_to_all | solution.py:336
  82.9 0.0 copy-start
  82.9 0.0 copy-start.1
  82.9 0.0 copy-start.2
  82.9 0.7 attend.1
  83.6 21.0 %all_to_all.27 = bf16[64,48,128]{2,1,0:T(8,128)(2,1)S(1)} all-to-all(bf16[64,48,128]{2,1,0:T(8,128)(2,1)S(1)} %attend.1), channel_id=1, replica_groups=mesh['y_lo'=2,'x'=4,'y_hi'=2,'z'=4,'core'=2] {'y_lo','x','y_hi','z'}, dimensions={0} | all-to-all | bytes 1572864 | tf_op jit(solution)/shard_map/all_to_all | solution.py:337
  104.6 0.0 copy-done.4
  104.6 0.0 slice-done
  104.7 0.0 slice-done.2
  104.7 0.0 slice-done.1
  104.7 0.0 slice-done.3
  104.7 0.0 copy-done
  104.7 0.0 copy-done.1
  104.7 0.0 copy-done.2
  104.7 11.4 %columns.1 = bf16[8,4,16,768]{3,2,1,0:T(8,128)(2,1)S(1)} custom-call(s32[2]{0:T(128)S(1)} %pad_add_fusion.me_ref, bf16[8,2,4,48,128]{4,3,2,1,0:T(8,128)(2,1)S(1)} %bitcast.30, bf16[2,4,16,768]{3,2,1,0:T(8,128)(2,1)S(1)} %get-tuple-element.27.x0, bf16[2,4,16,768]{3,2,1,0:T(8,128)(2,1)S(1)} %collective-permute-done.1.x1, ...), custom_call_target="tpu_custom_call" | custom-call | flops 8000000000 | bytes 18874368 | tf_op jit(solution)/shard_map/columns/pallas_call | solution.py:296
  116.2 12.6 %all_to_all.28 = bf16[8,4,16,768]{3,2,1,0:T(8,128)(2,1)S(1)} all-to-all(bf16[8,4,16,768]{3,2,1,0:T(8,128)(2,1)S(1)} %columns.1), channel_id=1, replica_groups=mesh['y_lo'=2,'x'=4,'y_hi'=2,'z'=4,'core'=2] {'y_lo','x'}, dimensions={0} | all-to-all | bytes 1572864 | tf_op jit(solution)/shard_map/all_to_all | solution.py:340
  128.7 1.1 copy.10
  (2 shorter events, 0.0 us)
Async XLA Ops:
  1.2 10.9 %collective-permute-start = (bf16[16,16,768]{2,0,1:T(8,128)(2,1)S(1)}, bf16[16,16,768]{2,0,1:T(8,128)(2,1)S(1)}, u32[]{:S(2)}, u32[]{:S(2)}) collective-permute-start(bf16[16,16,768]{2,0,1:T(8,128)(2,1)S(1)} %bitcast.40), channel_id=1, source_target_pairs={{0,64},{64,0},{1,65},{65,1},{2,66},{66,2},{3,67},{67,3},{4,68},{68... | collective-permute-start | bytes 1179656 | tf_op jit(solution)/shard_map/ppermute | solution.py:320
  12.0 42.1 %all-to-all-start = ((bf16[8,1408,128]{2,1,0:T(8,128)(2,1)}), bf16[8,1408,128]{2,1,0:T(8,128)(2,1)S(1)}, u32[]{:S(2)}, u32[]{:S(2)}) async-start(bf16[8,1408,128]{2,1,0:T(8,128)(2,1)} %project.1), calls=%async_computation | async-start | bytes 5767168 | tf_op jit(solution)/shard_map/all_to_all | solution.py:323
  21.4 7.7 %collective-permute-start.1 = (bf16[2,4,16,768]{3,2,1,0:T(8,128)(2,1)S(1)}, bf16[2,4,16,768]{3,2,1,0:T(8,128)(2,1)S(1)}, u32[]{:S(2)}, u32[]{:S(2)}) collective-permute-start(bf16[2,4,16,768]{3,2,1,0:T(8,128)(2,1)S(1)} %get-tuple-element.33), channel_id=1, source_target_pairs={{0,16},{16,0},{32,48},{48,32},{1,17},{17,1},{33,49},{49,33},{2,18}... | collective-permute-start | bytes 589832 | tf_op jit(solution)/shard_map/ppermute | solution.py:329
  22.9 10.5 %collective-permute-start.2 = (bf16[2,4,16,768]{3,2,1,0:T(8,128)(2,1)S(1)}, bf16[2,4,16,768]{3,2,1,0:T(8,128)(2,1)S(1)}, u32[]{:S(2)}, u32[]{:S(2)}) collective-permute-start(bf16[2,4,16,768]{3,2,1,0:T(8,128)(2,1)S(1)} %get-tuple-element.34), channel_id=1, source_target_pairs={{0,32},{16,48},{32,0},{48,16},{1,33},{17,49},{33,1},{49,17},{2,34}... | collective-permute-start | bytes 589832 | tf_op jit(solution)/shard_map/ppermute | solution.py:329
  25.7 9.9 %collective-permute-start.3 = (bf16[2,4,16,768]{3,2,1,0:T(8,128)(2,1)S(1)}, bf16[2,4,16,768]{3,2,1,0:T(8,128)(2,1)S(1)}, u32[]{:S(2)}, u32[]{:S(2)}) collective-permute-start(bf16[2,4,16,768]{3,2,1,0:T(8,128)(2,1)S(1)} %get-tuple-element.31), channel_id=1, source_target_pairs={{0,48},{16,32},{32,16},{48,0},{1,49},{17,33},{33,17},{49,1},{2,50}... | collective-permute-start | bytes 589832 | tf_op jit(solution)/shard_map/ppermute | solution.py:329
  35.6 0.7 copy-start.3
  54.1 50.6 %copy-start.4 = (bf16[2,4,16,768]{3,2,1,0:T(8,128)(2,1)S(1)}, bf16[2,4,16,768]{3,2,1,0:T(8,128)(2,1)}, u32[]{:S(2)}) copy-start(bf16[2,4,16,768]{3,2,1,0:T(8,128)(2,1)} %copy-done.3) | copy-start | bytes 589828
  54.2 2.7 %collective-permute-start.4 = (bf16[8,512,128]{2,1,0:T(8,128)(2,1)S(1)}, bf16[8,512,128]{2,1,0:T(8,128)(2,1)S(1)}, u32[]{:S(2)}, u32[]{:S(2)}) collective-permute-start(bf16[8,512,128]{2,1,0:T(8,128)(2,1)S(1)} %slice.6), channel_id=1, source_target_pairs={{0,1},{1,0},{2,3},{3,2},{4,5},{5,4},{6,7},{7,6},{8,9},{9,8},{10,11... | collective-permute-start | bytes 3145736 | tf_op jit(solution)/shard_map/ppermute | solution.py:331
  56.9 47.8 %slice-start = ((s8[4718592]{0:T(1024)(128)(4,1)}), s8[4194304]{0:T(1024)(128)(4,1)S(1)}, s32[]{:S(2)}) async-start(s8[4718592]{0:T(1024)(128)(4,1)} %bitcast.31), calls=%async_computation.5 | async-start | bytes 8388608
  56.9 47.8 %slice-start.2 = ((s8[4718592]{0:T(1024)(128)(4,1)}), s8[4194304]{0:T(1024)(128)(4,1)S(1)}, s32[]{:S(2)}) async-start(s8[4718592]{0:T(1024)(128)(4,1)} %bitcast.33), calls=%async_computation.7 | async-start | bytes 8388608
  57.7 13.9 %collective-permute-start.5 = (bf16[8,512,128]{2,1,0:T(8,128)(2,1)S(1)}, bf16[8,512,128]{2,1,0:T(8,128)(2,1)S(1)}, u32[]{:S(2)}, u32[]{:S(2)}) collective-permute-start(bf16[8,512,128]{2,1,0:T(8,128)(2,1)S(1)} %slice.7), channel_id=1, source_target_pairs={{0,1},{1,0},{2,3},{3,2},{4,5},{5,4},{6,7},{7,6},{8,9},{9,8},{10,11... | collective-permute-start | bytes 3145736 | tf_op jit(solution)/shard_map/ppermute | solution.py:334
  71.6 33.0 %slice-start.1 = ((s8[4718592]{0:T(1024)(128)(4,1)}), s8[524288]{0:T(1024)(128)(4,1)S(1)}, s32[]{:S(2)}) async-start(s8[4718592]{0:T(1024)(128)(4,1)} %bitcast.31), calls=%async_computation.6 | async-start | bytes 1048576
  71.6 33.0 %slice-start.3 = ((s8[4718592]{0:T(1024)(128)(4,1)}), s8[524288]{0:T(1024)(128)(4,1)S(1)}, s32[]{:S(2)}) async-start(s8[4718592]{0:T(1024)(128)(4,1)} %bitcast.33), calls=%async_computation.8 | async-start | bytes 1048576
  82.9 21.8 %copy-start = (bf16[768,2304]{1,0:T(8,128)(2,1)S(1)}, bf16[768,2304]{1,0:T(8,128)(2,1)}, u32[]{:S(2)}) copy-start(bf16[768,2304]{1,0:T(8,128)(2,1)} %wqkv.1) | copy-start | bytes 10616836
  82.9 21.8 %copy-start.1 = (bf16[768,768]{1,0:T(8,128)(2,1)S(1)}, bf16[768,768]{1,0:T(8,128)(2,1)}, u32[]{:S(2)}) copy-start(bf16[768,768]{1,0:T(8,128)(2,1)} %wo.1) | copy-start | bytes 3538948
  82.9 21.8 %copy-start.2 = (bf16[768,768]{1,0:T(8,128)(2,1)S(1)}, bf16[768,768]{1,0:T(8,128)(2,1)}, u32[]{:S(2)}) copy-start(bf16[768,768]{1,0:T(8,128)(2,1)} %wco.1) | copy-start | bytes 3538948

commit v8 on v7

--- a/solution.py
+++ b/solution.py
@@ -54,6 +54,27 @@
 
 def params(mib, **kw):
     return pltpu.CompilerParams(vmem_limit_bytes=mib * MIB, **kw)
+
+
+def take_far_kernel(x_hbm, out_ref, sem):
+    at = pl.multiple_of((1 - lax.axis_index("y_lo")) * 16, 16)
+    copy = pltpu.make_async_copy(x_hbm.at[:, pl.ds(at, 16), :], out_ref, sem)
+    copy.start()
+    copy.wait()
+
+
+def take_far(x):
+    anywhere = pl.BlockSpec(memory_space=pl.ANY)
+    return pl.pallas_call(
+        take_far_kernel,
+        in_specs=[anywhere],
+        out_specs=pl.BlockSpec(memory_space=pltpu.VMEM),
+        out_shape=jax.ShapeDtypeStruct((16, 16, D), BF),
+        scratch_shapes=[pltpu.SemaphoreType.DMA],
+        compiler_params=params(8),
+        cost_estimate=pl.CostEstimate(flops=0, bytes_accessed=MIB, transcendentals=0),
+        name="take_far",
+    )(x)
 
 
 def project_kernel(x_hbm, w_hbm, out_hbm, x_ref, w_ref, out_ref, third, sems):
@@ -316,8 +337,7 @@
     barrier = lax.optimization_barrier
     swap = [(0, 1), (1, 0)]
     y_me, x_me = lax.axis_index("y_lo"), lax.axis_index("x")
-    halves = x.reshape(16, 2, 16, D)
-    far = lax.ppermute(lax.dynamic_index_in_dim(halves, 1 - y_me, 1, False), "y_lo", swap)
+    far = lax.ppermute(take_far(x), "y_lo", swap)
     me = jnp.stack([y_me, x_me]).astype(jnp.int32)
     proj, x, far, me = barrier((project(x.reshape(512, D), row_qkv), x, far, me))
     got = lax.all_to_all(proj, ("y_hi", "z"), 0, 0, tiled=True)

time: 130 us -> 130 us (level)
  no operation moved by 1% of the time
where the time goes in v8:
time: 130 us
  blocking collectives  58.3 us (45%)
  waiting for transfers between devices  33.2 us (26%)
  Pallas kernels  18.8 us (14%)
  starting transfers between devices  14.9 us (11%)
  local copies, waits for them, and re-layouts  4.35 us (3%)
    all_to_all x1, blocking collectives, per_device(): att = lax.all_to_all(attend(shares, got, v2), CHIPS, 0, 0, tiled=True)  21 us
    all_to_all x1, waiting for transfers between devices, per_device(): got = lax.all_to_all(proj, ('y_hi', 'z'), 0, 0, tiled=True)  17.7 us
    all_to_all x1, blocking collectives, per_device(): parts = lax.all_to_all(parts, SEQ, 0, 0, tiled=True)  13.7 us
    all_to_all x1, blocking collectives, per_device(): out = lax.all_to_all(out, SEQ, 0, 0, tiled=True)  12.6 us
    pallas_call x1, Pallas kernels, columns(): pl.pallas_call(columns_kernel, in_specs=[pl.BlockSpec(memory_space=pltpu....  11.4 us
    all_to_all x1, blocking collectives, per_device(): shares = lax.all_to_all(softmax(parts), SEQ, 0, 0, tiled=True)  11 us
    ppermute x3, waiting for transfers between devices, per_device(): lax.ppermute(block, 'x', [(i, i ^ k) for i in range(4)])  9.47 us
    all_to_all x1, starting transfers between devices, per_device(): got = lax.all_to_all(proj, ('y_hi', 'z'), 0, 0, tiled=True)  8.11 us
  transfers between devices with their start and end apart: 7, of which 6 were waited for; matrix products, arithmetic and copies ran while one was open for 1% of the time, Pallas kernels for 4%

profile of v8, /device:TPU:0, one launch (start us, length us, event | category | flops | bytes accessed | tf_op | source)
XLA Modules:
  0.0 129.9 jit_solution(2851091460861598977)
XLA Ops:
  0.0 0.0 copy-start
  0.0 1.1 copy-done
  1.2 1.7 %collective-permute-start = (bf16[16,16,768]{2,1,0:T(8,128)(2,1)S(1)}, bf16[16,16,768]{2,1,0:T(8,128)(2,1)S(1)}, u32[]{:S(2)}, u32[]{:S(2)}) collective-permute-start(bf16[16,16,768]{2,1,0:T(8,128)(2,1)S(1)} %take_far.1), channel_id=1, source_target_pairs={{0,64},{64,0},{1,65},{65,1},{2,66},{66,2},{3,67},{67,3},{4,68},{68... | collective-permute-start | bytes 1179656 | tf_op jit(solution)/shard_map/ppermute | solution.py:340
  2.9 0.1 pad_add_fusion.me_ref
  3.0 5.7 %project.1 = bf16[8,1408,128]{2,1,0:T(8,128)(2,1)} custom-call(bf16[512,768]{1,0:T(8,128)(2,1)} %bitcast.26, bf16[768,2304]{1,0:T(8,128)(2,1)} %w_hbm.1), custom_call_target="tpu_custom_call" | custom-call | flops 1811939328 | bytes 6291456 | tf_op jit(solution)/shard_map/project/pallas_call | solution.py:134
  8.7 3.4 %collective-permute-done = bf16[16,16,768]{2,1,0:T(8,128)(2,1)S(1)} collective-permute-done((bf16[16,16,768]{2,1,0:T(8,128)(2,1)S(1)}, bf16[16,16,768]{2,1,0:T(8,128)(2,1)S(1)}, u32[]{:S(2)}, u32[]{:S(2)}) %collective-permute-start) | collective-permute-done | bytes 393248 | tf_op jit(solution)/shard_map/ppermute | solution.py:340
  12.0 8.1 %all-to-all-start = ((bf16[8,1408,128]{2,1,0:T(8,128)(2,1)}), bf16[8,1408,128]{2,1,0:T(8,128)(2,1)S(1)}, u32[]{:S(2)}, u32[]{:S(2)}) async-start(bf16[8,1408,128]{2,1,0:T(8,128)(2,1)} %project.1), calls=%async_computation | async-start | bytes 5767168 | tf_op jit(solution)/shard_map/all_to_all | solution.py:343
  20.2 1.0 constant_dynamic-slice_fusion
  21.2 0.1 copy.11
  21.3 0.1 copy.9
  21.4 0.1 fusion.1
  21.5 1.6 %collective-permute-start.1 = (bf16[2,4,16,768]{3,2,1,0:T(8,128)(2,1)S(1)}, bf16[2,4,16,768]{3,2,1,0:T(8,128)(2,1)S(1)}, u32[]{:S(2)}, u32[]{:S(2)}) collective-permute-start(bf16[2,4,16,768]{3,2,1,0:T(8,128)(2,1)S(1)} %get-tuple-element.33), channel_id=1, source_target_pairs={{0,16},{16,0},{32,48},{48,32},{1,17},{17,1},{33,49},{49,33},{2,18}... | collective-permute-start | bytes 589832 | tf_op jit(solution)/shard_map/ppermute | solution.py:349
  23.1 2.7 %collective-permute-start.2 = (bf16[2,4,16,768]{3,2,1,0:T(8,128)(2,1)S(1)}, bf16[2,4,16,768]{3,2,1,0:T(8,128)(2,1)S(1)}, u32[]{:S(2)}, u32[]{:S(2)}) collective-permute-start(bf16[2,4,16,768]{3,2,1,0:T(8,128)(2,1)S(1)} %get-tuple-element.34), channel_id=1, source_target_pairs={{0,32},{16,48},{32,0},{48,16},{1,33},{17,49},{33,1},{49,17},{2,34}... | collective-permute-start | bytes 589832 | tf_op jit(solution)/shard_map/ppermute | solution.py:349
  25.8 0.5 collective-permute-start.3
  26.3 2.9 %collective-permute-done.1.x1 = bf16[2,4,16,768]{3,2,1,0:T(8,128)(2,1)S(1)} collective-permute-done((bf16[2,4,16,768]{3,2,1,0:T(8,128)(2,1)S(1)}, bf16[2,4,16,768]{3,2,1,0:T(8,128)(2,1)S(1)}, u32[]{:S(2)}, u32[]{:S(2)}) %collective-permute-start.1) | collective-permute-done | bytes 196640 | tf_op jit(solution)/shard_map/ppermute | solution.py:349
  29.2 4.4 %collective-permute-done.2.x2 = bf16[2,4,16,768]{3,2,1,0:T(8,128)(2,1)S(1)} collective-permute-done((bf16[2,4,16,768]{3,2,1,0:T(8,128)(2,1)S(1)}, bf16[2,4,16,768]{3,2,1,0:T(8,128)(2,1)S(1)}, u32[]{:S(2)}, u32[]{:S(2)}) %collective-permute-start.2) | collective-permute-done | bytes 196640 | tf_op jit(solution)/shard_map/ppermute | solution.py:349
  33.6 2.2 %collective-permute-done.3.x3 = bf16[2,4,16,768]{3,2,1,0:T(8,128)(2,1)S(1)} collective-permute-done((bf16[2,4,16,768]{3,2,1,0:T(8,128)(2,1)S(1)}, bf16[2,4,16,768]{3,2,1,0:T(8,128)(2,1)S(1)}, u32[]{:S(2)}, u32[]{:S(2)}) %collective-permute-start.3) | collective-permute-done | bytes 196640 | tf_op jit(solution)/shard_map/ppermute | solution.py:349
  35.8 0.0 copy-start.4
  35.8 0.7 copy-done.4
  36.4 17.7 %all-to-all-done.got_ref = bf16[8,1408,128]{2,1,0:T(8,128)(2,1)S(1)} async-done(((bf16[8,1408,128]{2,1,0:T(8,128)(2,1)}), bf16[8,1408,128]{2,1,0:T(8,128)(2,1)S(1)}, u32[]{:S(2)}, u32[]{:S(2)}) %all-to-all-start) | async-done | bytes 2883616 | tf_op jit(solution)/shard_map/all_to_all | solution.py:343
  54.1 0.0 copy-start.5
  54.1 0.1 slice.6
  54.2 0.1 collective-permute-start.4
  54.3 2.6 %collective-permute-done.4.k2_ref = bf16[8,512,128]{2,1,0:T(8,128)(2,1)S(1)} collective-permute-done((bf16[8,512,128]{2,1,0:T(8,128)(2,1)S(1)}, bf16[8,512,128]{2,1,0:T(8,128)(2,1)S(1)}, u32[]{:S(2)}, u32[]{:S(2)}) %collective-permute-start.4) | collective-permute-done | bytes 1048608 | tf_op jit(solution)/shard_map/ppermute | solution.py:351
  56.9 0.0 slice-start
  56.9 0.0 slice-start.2
  56.9 0.7 scores.1
  57.7 0.1 slice.7
  57.8 0.2 collective-permute-start.5
  58.0 13.7 %all_to_all.25.parts_ref = bf16[8,48,512]{2,1,0:T(8,128)(2,1)S(1)} all-to-all(bf16[8,48,512]{2,1,0:T(8,128)(2,1)S(1)} %scores.1), channel_id=1, replica_groups=mesh['y_lo'=2,'x'=4,'y_hi'=2,'z'=4,'core'=2] {'y_lo','x'}, dimensions={0} | all-to-all | bytes 786432 | tf_op jit(solution)/shard_map/all_to_all | solution.py:353
  71.7 0.0 slice-start.1
  71.7 0.0 slice-start.3
  71.7 0.0 collective-permute-done.5.v2_ref
  71.7 0.2 softmax.1
  71.9 11.0 %all_to_all.26.w_ref = bf16[8,48,512]{2,1,0:T(8,128)(2,1)S(1)} all-to-all(bf16[8,48,512]{2,1,0:T(8,128)(2,1)S(1)} %softmax.1), channel_id=1, replica_groups=mesh['y_lo'=2,'x'=4,'y_hi'=2,'z'=4,'core'=2] {'y_lo','x'}, dimensions={0} | all-to-all | bytes 786432 | tf_op jit(solution)/shard_map/all_to_all | solution.py:356
  82.9 0.0 copy-start.1
  82.9 0.0 copy-start.2
  83.0 0.0 copy-start.3
  83.0 0.7 attend.1
  83.6 21.0 %all_to_all.27 = bf16[64,48,128]{2,1,0:T(8,128)(2,1)S(1)} all-to-all(bf16[64,48,128]{2,1,0:T(8,128)(2,1)S(1)} %attend.1), channel_id=1, replica_groups=mesh['y_lo'=2,'x'=4,'y_hi'=2,'z'=4,'core'=2] {'y_lo','x','y_hi','z'}, dimensions={0} | all-to-all | bytes 1572864 | tf_op jit(solution)/shard_map/all_to_all | solution.py:357
  104.7 0.0 copy-done.5
  104.7 0.0 slice-done
  104.7 0.0 slice-done.2
  104.7 0.0 slice-done.1
  104.7 0.0 slice-done.3
  104.7 0.0 copy-done.1
  104.7 0.0 copy-done.2
  104.7 0.0 copy-done.3
  104.8 11.4 %columns.1 = bf16[8,4,16,768]{3,2,1,0:T(8,128)(2,1)S(1)} custom-call(s32[2]{0:T(128)S(1)} %pad_add_fusion.me_ref, bf16[8,2,4,48,128]{4,3,2,1,0:T(8,128)(2,1)S(1)} %bitcast.28, bf16[2,4,16,768]{3,2,1,0:T(8,128)(2,1)S(1)} %get-tuple-element.27.x0, bf16[2,4,16,768]{3,2,1,0:T(8,128)(2,1)S(1)} %collective-permute-done.1.x1, ...), custom_call_target="tpu_custom_call" | custom-call | flops 8000000000 | bytes 18874368 | tf_op jit(solution)/shard_map/columns/pallas_call | solution.py:317
  116.2 12.6 %all_to_all.28 = bf16[8,4,16,768]{3,2,1,0:T(8,128)(2,1)S(1)} all-to-all(bf16[8,4,16,768]{3,2,1,0:T(8,128)(2,1)S(1)} %columns.1), channel_id=1, replica_groups=mesh['y_lo'=2,'x'=4,'y_hi'=2,'z'=4,'core'=2] {'y_lo','x'}, dimensions={0} | all-to-all | bytes 1572864 | tf_op jit(solution)/shard_map/all_to_all | solution.py:360
  128.8 1.1 copy.10
  (3 shorter events, 0.0 us)
Async XLA Ops:
  0.0 1.1 copy-start
  1.2 10.9 %collective-permute-start = (bf16[16,16,768]{2,1,0:T(8,128)(2,1)S(1)}, bf16[16,16,768]{2,1,0:T(8,128)(2,1)S(1)}, u32[]{:S(2)}, u32[]{:S(2)}) collective-permute-start(bf16[16,16,768]{2,1,0:T(8,128)(2,1)S(1)} %take_far.1), channel_id=1, source_target_pairs={{0,64},{64,0},{1,65},{65,1},{2,66},{66,2},{3,67},{67,3},{4,68},{68... | collective-permute-start | bytes 1179656 | tf_op jit(solution)/shard_map/ppermute | solution.py:340
  12.0 42.1 %all-to-all-start = ((bf16[8,1408,128]{2,1,0:T(8,128)(2,1)}), bf16[8,1408,128]{2,1,0:T(8,128)(2,1)S(1)}, u32[]{:S(2)}, u32[]{:S(2)}) async-start(bf16[8,1408,128]{2,1,0:T(8,128)(2,1)} %project.1), calls=%async_computation | async-start | bytes 5767168 | tf_op jit(solution)/shard_map/all_to_all | solution.py:343
  21.5 7.7 %collective-permute-start.1 = (bf16[2,4,16,768]{3,2,1,0:T(8,128)(2,1)S(1)}, bf16[2,4,16,768]{3,2,1,0:T(8,128)(2,1)S(1)}, u32[]{:S(2)}, u32[]{:S(2)}) collective-permute-start(bf16[2,4,16,768]{3,2,1,0:T(8,128)(2,1)S(1)} %get-tuple-element.33), channel_id=1, source_target_pairs={{0,16},{16,0},{32,48},{48,32},{1,17},{17,1},{33,49},{49,33},{2,18}... | collective-permute-start | bytes 589832 | tf_op jit(solution)/shard_map/ppermute | solution.py:349
  23.1 10.5 %collective-permute-start.2 = (bf16[2,4,16,768]{3,2,1,0:T(8,128)(2,1)S(1)}, bf16[2,4,16,768]{3,2,1,0:T(8,128)(2,1)S(1)}, u32[]{:S(2)}, u32[]{:S(2)}) collective-permute-start(bf16[2,4,16,768]{3,2,1,0:T(8,128)(2,1)S(1)} %get-tuple-element.34), channel_id=1, source_target_pairs={{0,32},{16,48},{32,0},{48,16},{1,33},{17,49},{33,1},{49,17},{2,34}... | collective-permute-start | bytes 589832 | tf_op jit(solution)/shard_map/ppermute | solution.py:349
  25.8 9.9 %collective-permute-start.3 = (bf16[2,4,16,768]{3,2,1,0:T(8,128)(2,1)S(1)}, bf16[2,4,16,768]{3,2,1,0:T(8,128)(2,1)S(1)}, u32[]{:S(2)}, u32[]{:S(2)}) collective-permute-start(bf16[2,4,16,768]{3,2,1,0:T(8,128)(2,1)S(1)} %get-tuple-element.31), channel_id=1, source_target_pairs={{0,48},{16,32},{32,16},{48,0},{1,49},{17,33},{33,17},{49,1},{2,50}... | collective-permute-start | bytes 589832 | tf_op jit(solution)/shard_map/ppermute | solution.py:349
  35.8 0.7 copy-start.4
  54.1 50.6 %copy-start.5 = (bf16[2,4,16,768]{3,2,1,0:T(8,128)(2,1)S(1)}, bf16[2,4,16,768]{3,2,1,0:T(8,128)(2,1)}, u32[]{:S(2)}) copy-start(bf16[2,4,16,768]{3,2,1,0:T(8,128)(2,1)} %copy-done.4) | copy-start | bytes 589828
  54.2 2.7 %collective-permute-start.4 = (bf16[8,512,128]{2,1,0:T(8,128)(2,1)S(1)}, bf16[8,512,128]{2,1,0:T(8,128)(2,1)S(1)}, u32[]{:S(2)}, u32[]{:S(2)}) collective-permute-start(bf16[8,512,128]{2,1,0:T(8,128)(2,1)S(1)} %slice.6), channel_id=1, source_target_pairs={{0,1},{1,0},{2,3},{3,2},{4,5},{5,4},{6,7},{7,6},{8,9},{9,8},{10,11... | collective-permute-start | bytes 3145736 | tf_op jit(solution)/shard_map/ppermute | solution.py:351
  56.9 47.8 %slice-start = ((s8[4718592]{0:T(1024)(128)(4,1)}), s8[4194304]{0:T(1024)(128)(4,1)S(1)}, s32[]{:S(2)}) async-start(s8[4718592]{0:T(1024)(128)(4,1)} %bitcast.29), calls=%async_computation.5 | async-start | bytes 8388608
  56.9 47.8 %slice-start.2 = ((s8[4718592]{0:T(1024)(128)(4,1)}), s8[4194304]{0:T(1024)(128)(4,1)S(1)}, s32[]{:S(2)}) async-start(s8[4718592]{0:T(1024)(128)(4,1)} %bitcast.31), calls=%async_computation.7 | async-start | bytes 8388608
  57.8 13.9 %collective-permute-start.5 = (bf16[8,512,128]{2,1,0:T(8,128)(2,1)S(1)}, bf16[8,512,128]{2,1,0:T(8,128)(2,1)S(1)}, u32[]{:S(2)}, u32[]{:S(2)}) collective-permute-start(bf16[8,512,128]{2,1,0:T(8,128)(2,1)S(1)} %slice.7), channel_id=1, source_target_pairs={{0,1},{1,0},{2,3},{3,2},{4,5},{5,4},{6,7},{7,6},{8,9},{9,8},{10,11... | collective-permute-start | bytes 3145736 | tf_op jit(solution)/shard_map/ppermute | solution.py:354
  71.7 33.0 %slice-start.1 = ((s8[4718592]{0:T(1024)(128)(4,1)}), s8[524288]{0:T(1024)(128)(4,1)S(1)}, s32[]{:S(2)}) async-start(s8[4718592]{0:T(1024)(128)(4,1)} %bitcast.29), calls=%async_computation.6 | async-start | bytes 1048576
  71.7 33.0 %slice-start.3 = ((s8[4718592]{0:T(1024)(128)(4,1)}), s8[524288]{0:T(1024)(128)(4,1)S(1)}, s32[]{:S(2)}) async-start(s8[4718592]{0:T(1024)(128)(4,1)} %bitcast.31), calls=%async_computation.8 | async-start | bytes 1048576
  82.9 21.8 %copy-start.1 = (bf16[768,2304]{1,0:T(8,128)(2,1)S(1)}, bf16[768,2304]{1,0:T(8,128)(2,1)}, u32[]{:S(2)}) copy-start(bf16[768,2304]{1,0:T(8,128)(2,1)} %wqkv.1) | copy-start | bytes 10616836
  82.9 21.8 %copy-start.2 = (bf16[768,768]{1,0:T(8,128)(2,1)S(1)}, bf16[768,768]{1,0:T(8,128)(2,1)}, u32[]{:S(2)}) copy-start(bf16[768,768]{1,0:T(8,128)(2,1)} %wo.1) | copy-start | bytes 3538948
  83.0 21.8 %copy-start.3 = (bf16[768,768]{1,0:T(8,128)(2,1)S(1)}, bf16[768,768]{1,0:T(8,128)(2,1)}, u32[]{:S(2)}) copy-start(bf16[768,768]{1,0:T(8,128)(2,1)} %wco.1) | copy-start | bytes 3538948
